TPU v7x, 512 devices: a whole 4x8x8 slice. The times are simulated.
512 devices in a mesh: seq: 64 (over y, z_lo, core), head: 8 (over z_hi, x).
Axes of the slice: x: 4, y: 8, z: 8 (z_hi: 2, z_lo: 4; z = z_hi * 4 + z_lo), core: 2. Of those that a mesh axis runs over, the one named last changes fastest.
Arguments:
- queries: bfloat16 [4096, 64, 576], P('seq', 'head'), may hold values from -17.5 to 17.5
- latents: bfloat16 [4096, 576], P('seq'), may hold values from -6 to 6
- positions: int32 [4096], P('seq'), may hold values from 0 to 4095, as said below
- lengths: int32 [8], replicated, may hold values from 1 to 1024, 4096 in all
- value_up: bfloat16 [64, 512, 128], P('head'), may hold values from -1 to 1
- out_weight: bfloat16 [8192, 4096], P('head', 'seq'), may hold values from -0.0625 to 0.0625
Outputs:
- mixed: bfloat16 [4096, 4096], P('seq', 'head')
Inputs may be any that keep to these rules, and one draw needn't show every extreme that they name: A permutation: stored token r sits at sequence position positions[r]. `lengths`: segment 0 is the problem statement, the others are solutions; they sum to 4096.
All inputs are finite; a program needn't handle non-finite values.
Results may differ from a plain program's by a relative error of at most 0.022.
Values may be sent and summed in bfloat16 or wider, within the bound.
No kernel may reach another device: no remote copies, remote signals or barrier semaphores. Data moves between devices by JAX's collectives and lax.ppermute only.
A program may use at most 64 MiB of HBM per device.

v0:
```python
import math

import jax
import jax.numpy as jnp
from jax import lax
from jax.sharding import PartitionSpec as P

LATENT = 512


SCALE = 192.0 ** (-0.5)


def segment_of(where, lengths):
    segment_ends = jnp.cumsum(lengths)
    return jnp.sum((where[:, None] >= segment_ends[None, :]).astype(jnp.int32), axis=1)


def apply_rope(rotary, where):
    full_width = rotary.shape[-1]
    half_width = full_width // 2
    frequency = jnp.exp(
        jnp.arange(half_width, dtype=jnp.float32) * (-2.0 * math.log(10000.0) / full_width)
    )
    angles = where.astype(jnp.float32)[:, None] * frequency[None, :]
    target_shape = (angles.shape[0],) + (1,) * (rotary.ndim - 2) + (half_width,)
    cosines = jnp.cos(angles).reshape(target_shape)
    sines = jnp.sin(angles).reshape(target_shape)
    first_half = rotary[..., :half_width].astype(jnp.float32)
    second_half = rotary[..., half_width:].astype(jnp.float32)
    return jnp.concatenate(
        [first_half * cosines - second_half * sines, first_half * sines + second_half * cosines],
        axis=-1,
    )


def prepare(source, where):
    turned = apply_rope(source[..., LATENT:], where)
    return jnp.concatenate([source[..., :LATENT].astype(jnp.float32), turned], axis=-1).astype(
        jnp.bfloat16
    )


def on_device(queries, latents, positions, lengths, value_up, out_weight):
    tok_rows = queries.shape[0]
    head_count = queries.shape[1]
    full_width = queries.shape[2]
    query_rows = tok_rows * head_count
    q_rot = prepare(queries, positions).reshape(query_rows, full_width)
    k_rot = prepare(latents, positions)
    query_pos = jnp.repeat(positions, head_count)
    query_seg = jnp.repeat(segment_of(positions, lengths), head_count)
    key_block = lax.all_gather(k_rot, "seq", axis=0, tiled=True)
    key_pos = lax.all_gather(positions, "seq", axis=0, tiled=True)
    key_seg = segment_of(key_pos, lengths)
    top_old = jnp.full((query_rows,), -1e30, jnp.float32)
    scores = (
        lax.dot_general(
            q_rot, key_block, (((1,), (1,)), ((), ())), preferred_element_type=jnp.float32
        )
        * SCALE
    )
    visible = (key_pos[None, :] <= query_pos[:, None]) & (
        (key_seg[None, :] == query_seg[:, None]) | (key_seg[None, :] == 0)
    )
    top_new = jnp.maximum(top_old, jnp.max(jnp.where(visible, scores, -1e30), axis=1))
    weights = jnp.where(visible, jnp.exp(scores - top_new[:, None]), 0.0)
    totals = jnp.sum(weights, axis=1)
    accum = jnp.dot(
        weights.astype(jnp.bfloat16), key_block[:, :LATENT], preferred_element_type=jnp.float32
    )
    context = (accum / totals[:, None]).astype(jnp.bfloat16).reshape(tok_rows, head_count, LATENT)
    values = jnp.einsum(
        "thl,hlv->thv", context, value_up, preferred_element_type=jnp.float32
    ).astype(jnp.bfloat16)
    values = values.reshape(tok_rows, head_count * value_up.shape[2])
    partial_value = jnp.dot(
        values,
        lax.all_gather(out_weight, "seq", axis=1, tiled=True),
        preferred_element_type=jnp.float32,
    )
    summed = lax.psum(partial_value.astype(jnp.bfloat16), "head").astype(jnp.float32)
    own_cols = partial_value.shape[1] // lax.axis_size("head")
    mixed = lax.dynamic_slice_in_dim(summed, lax.axis_index("head") * own_cols, own_cols, 1)
    return mixed.astype(jnp.bfloat16)


def solution(mesh):
    placed = (
        P("seq", "head", None),
        P("seq", None),
        P("seq"),
        P(),
        P("head", None, None),
        P("head", "seq"),
    )
    return jax.shard_map(
        on_device, mesh=mesh, in_specs=placed, out_specs=P("seq", "head"), check_vma=False
    )
```

profile of v0, /device:TPU:8, one launch (start us, length us, event | category | flops | bytes accessed | tf_op | source)
XLA Modules:
  0.0 436.1 jit_solution(10961398188512418060)
XLA Ops:
  6.5 0.7 convert_element_type.51
  7.3 0.8 slice.30
  8.1 1.0 multiply_cosine_fusion
  9.1 0.7 pad_maximum_fusion
  9.9 0.7 all-gather.5.cloned.1.call-update
  10.7 0.8 reduce-window.8
  11.5 0.8 convert_reduce_fusion.1
  12.3 0.1 broadcast_in_dim.13
  12.4 0.1 eq.27
  12.5 0.7 broadcast_in_dim.12
  13.2 0.1 le.16
  13.3 1.3 dynamic-slice
  15.3 0.9 dynamic-update-slice
  16.1 256.5 %all-reduce = s32[4096]{0:T(1024)S(1)} all-reduce(s32[4096]{0:T(1024)S(1)} %dynamic-update-slice), channel_id=1, replica_groups=mesh['seq'=64,'head'=8] {'seq'}, use_global_device_ids=true, to_apply=%add | all-reduce | flops 4096 | bytes 32768
  272.6 0.1 convert_reduce_fusion
  272.8 1.1 fusion.30
  273.9 1.1 slice_bitcast_fusion
  275.0 7.3 %select_reduce_fusion = (f32[512]{0:T(512)S(1)}, f32[512,4096]{1,0:T(8,128)S(1)}) fusion(pred[4096]{0:T(1024)(128)(4,1)S(1)} %broadcast_compare_fusion, s32[512]{0:T(512)S(1)} %eq.27, s32[4096]{0:T(1024)S(1)} %convert_reduce_fusion, s32[512]{0:T(512)S(1)} %le.16, s32[4096]{0:T(1024)S(1)} %all-reduce, bf16[4096,576]{1,0:T(8,128)(2,1)} %all-gather.3.cloned.1.call-done, ...), kind=kOutput, calls=%fused_computation.1 | convolution fusion | flops 2432368128 | bytes 13740032 | tf_op jit(solution)/shard_map/dot_general | solution.py:58
  282.3 4.3 fusion
  286.7 3.6 fusion.13
  290.3 0.4 fusion.8
  290.7 6.9 %convolution_convert_fusion = bf16[64,4096]{1,0:T(8,128)(2,1)} fusion(bf16[1024,4096]{0,1:T(8,128)(2,1)} %all-gather.5.cloned.1.call-done, bf16[8,8,8,128]{3,2,1,0:T(8,128)(2,1)S(1)} %fusion.8), kind=kOutput, calls=%fused_computation.5 | convolution fusion | flops 537133056 | bytes 9043968 | tf_op jit(solution)/shard_map/dot_general | solution.py:77
  297.6 130.5 %all-reduce.3.cloned.1.call-done = bf16[64,4096]{1,0:T(8,128)(2,1)} async-done(((bf16[64,4096]{1,0:T(8,128)(2,1)}), bf16[64,4096]{1,0:T(8,128)(2,1)}) %all-reduce.3.cloned.1.call-update) | async-done | bytes 524304 | tf_op jit(solution)/shard_map/psum | solution.py:82
  428.1 1.5 convert_convert_fusion
  (18 shorter events, 0.2 us)
Async XLA Ops:
  6.5 283.7 %copy-start = (bf16[8,512,128]{2,1,0:T(8,128)(2,1)S(1)}, bf16[8,512,128]{2,1,0:T(8,128)(2,1)}, u32[]{:S(2)}) copy-start(bf16[8,512,128]{2,1,0:T(8,128)(2,1)} %param.10) | copy-start | bytes 3145732
  6.5 268.5 %all-gather.3.cloned.1.call-start = ((), (), s32[]{:S(2)}) async-start(), calls=%async_computation | async-start | bytes 5324800 | tf_op jit(solution)/shard_map/all_gather | solution.py:53
  9.9 280.8 %all-gather.5.cloned.1.call-start = ((), (), s32[]{:S(2)}) async-start(), calls=%async_computation.1 | async-start | bytes 8519680 | tf_op jit(solution)/shard_map/all_gather | solution.py:79
  10.6 417.5 %all-reduce.3.cloned.1.call-start = ((), (), s32[]{:S(2)}) async-start(), calls=%async_computation.2 | async-start | bytes 1048576 | tf_op jit(solution)/shard_map/psum | solution.py:82
  275.0 11.7 %slice-start = ((s8[5242880]{0:T(1024)(128)(4,1)}), s8[4194304]{0:T(1024)(128)(4,1)S(1)}, s32[]{:S(2)}) async-start(s8[5242880]{0:T(1024)(128)(4,1)} %bitcast.22), calls=%async_computation.3 | async-start | bytes 8388608
  275.0 11.7 %slice-start.1 = ((s8[5242880]{0:T(1024)(128)(4,1)}), s8[1048576]{0:T(1024)(128)(4,1)S(1)}, s32[]{:S(2)}) async-start(s8[5242880]{0:T(1024)(128)(4,1)} %bitcast.22), calls=%async_computation.4 | async-start | bytes 2097152
Sparse Core Ops, SparseCore 0:
  10.0 125.7 all-gather.2
  137.9 122.7 all-gather.4
  297.8 130.3 all-reduce.2
where the time goes:
time: 437 us; the launch traced here: 436 us
  blocking collectives  256 us (59%)
  waiting for transfers between devices  131 us (30%)
  matrix products  18.2 us (4%)
  between operations  13.9 us (3%)
  other arithmetic  11.1 us (3%)
  local copies, waits for them, and re-layouts  5.07 us (1%)
    unnamed x1, blocking collectives  256 us
    psum x1, waiting for transfers between devices, on_device(): lax.psum(partial_value.astype(jnp.bfloat16), 'head').astype(jnp.float32)  130 us
  transfers between devices with their start and end apart: 3, of which 1 were waited for; matrix products, arithmetic and copies ran while one was open for 5% of the time, Pallas kernels for 0%

commit v1 on v0

v1 whole, which is shorter than its diff:
```python
import functools
import math

import jax
import jax.numpy as jnp
import numpy as np
from jax import lax
from jax.experimental import pallas as pl
from jax.experimental.pallas import tpu as pltpu
from jax.sharding import Mesh, PartitionSpec as P

LATENT = 512
ROPE = 64
WIDTH = 640
SCALE = 192.0 ** (-0.5)
LOG2_SCALE = SCALE * math.log2(math.e)
HIDDEN = -1e30
VMEM = 48 * 1024 * 1024
NT = (((1,), (1,)), ((), ()))


def rotate(rotary, where):
    half = ROPE // 2
    frequency = jnp.exp(jnp.arange(half, dtype=jnp.float32) * (-2.0 * math.log(10000.0) / ROPE))
    angles = where.astype(jnp.float32)[:, None] * frequency[None, :]
    shape = (angles.shape[0],) + (1,) * (rotary.ndim - 2) + (half,)
    cosines = jnp.cos(angles).reshape(shape)
    sines = jnp.sin(angles).reshape(shape)
    first = rotary[..., :half].astype(jnp.float32)
    second = rotary[..., half:].astype(jnp.float32)
    return jnp.concatenate(
        [first * cosines - second * sines, first * sines + second * cosines], axis=-1
    ).astype(jnp.bfloat16)


def position_parts(where):
    return jnp.stack([where >> 6, where & 63], axis=-1).astype(jnp.bfloat16)


def shift_z(x, by):
    perm = []
    for z in range(8):
        to = (z + by) % 8
        source = ((z % 4) // 2 * 2 + z % 2) * 2 + z // 4
        target = ((to % 4) // 2 * 2 + to % 2) * 2 + to // 4
        perm.append((source, target))
    return lax.ppermute(x, ("zh_lat", "zl_lat", "z_hi"), perm)


def swap(x, axis):
    return lax.ppermute(x, axis, [(0, 1), (1, 0)])


def attend_kernel(blocks, first, last, *refs):
    ends_ref, q_ref = refs[0], refs[1]
    key_refs = refs[2 : 2 + blocks]
    rest = refs[2 + blocks :]
    if not first:
        m_in, l_in, acc_in = rest[:3]
        rest = rest[3:]
    if last:
        up_ref, out_ref = rest
    else:
        m_out, l_out, acc_out = rest
    heads, toks, _ = q_ref.shape
    rows = heads * toks
    meta = q_ref[0, :, LATENT:].astype(jnp.float32)
    query_pos = meta[:, 66:67] * 64.0 + meta[:, 67:68]
    query_start = jnp.zeros_like(query_pos)
    for k in range(8):
        end = ends_ref[k].astype(jnp.float32)
        query_start = jnp.where(query_pos >= end, end, query_start)
    first_end = ends_ref[0].astype(jnp.float32)
    q = q_ref[...].reshape(rows, WIDTH)
    lane = lax.broadcasted_iota(jnp.int32, (toks, 128), 1)
    pick = jnp.where(lane == 64, 64.0, jnp.where(lane == 65, 1.0, 0.0)).astype(jnp.bfloat16)
    scores = []
    for key_ref in key_refs:
        keys = key_ref[...]
        key_pos = lax.dot_general(
            pick, keys[:, LATENT:], NT, preferred_element_type=jnp.float32
        )
        visible = (key_pos <= query_pos) & ((key_pos >= query_start) | (key_pos < first_end))
        raw = lax.dot_general(q, keys, NT, preferred_element_type=jnp.float32)
        raw = raw.reshape(heads, toks, keys.shape[0])
        scores.append(jnp.where(visible[None], raw, HIDDEN).reshape(rows, keys.shape[0]))
    top = functools.reduce(jnp.maximum, [jnp.max(s, axis=1, keepdims=True) for s in scores])
    if not first:
        old = m_in[...].reshape(rows, 128)[:, :1]
        top = jnp.maximum(top, old)
        fade = jnp.exp2((old - top) * LOG2_SCALE)
    total = 0.0
    mixed = 0.0
    for key_ref, s in zip(key_refs, scores):
        weights = jnp.exp2((s - top) * LOG2_SCALE)
        total = total + jnp.sum(weights, axis=1, keepdims=True)
        mixed = mixed + jnp.dot(
            weights.astype(jnp.bfloat16), key_ref[:, :LATENT], preferred_element_type=jnp.float32
        )
    if not first:
        total = total + fade * l_in[...].reshape(rows, 128)[:, :1]
        mixed = mixed + fade * acc_in[...].reshape(rows, LATENT)
    if not last:
        m_out[...] = jnp.broadcast_to(top, (rows, 128)).reshape(heads, toks, 128)
        l_out[...] = jnp.broadcast_to(total, (rows, 128)).reshape(heads, toks, 128)
        acc_out[...] = mixed.reshape(heads, toks, LATENT)
        return
    context = (mixed / total).astype(jnp.bfloat16).reshape(heads, toks, LATENT)
    level = (top * LOG2_SCALE + jnp.log2(total)).reshape(heads, toks, 1)
    half = toks // 2
    for h in range(heads):
        part = jnp.dot(context[h], up_ref[h], preferred_element_type=jnp.float32)
        at = slice(h * 128, h * 128 + 128)
        spread = jnp.broadcast_to(level[h], (toks, 128))
        for side in range(2):
            out_ref[side, 0, :, at] = part[side * half : (side + 1) * half]
            out_ref[side, 1, :, at] = spread[side * half : (side + 1) * half]


def attend(ends, q, keys, carry=None, up=None, group=2):
    heads, toks, _ = q.shape
    first, last = carry is None, up is not None
    per_head = lambda width: pl.BlockSpec((group, toks, width), lambda i: (i, 0, 0))
    in_specs = [pl.BlockSpec(memory_space=pltpu.SMEM), per_head(WIDTH)]
    in_specs += [pl.BlockSpec(k.shape, lambda i: (0, 0)) for k in keys]
    args = [ends, q, *keys]
    state_specs = [per_head(128), per_head(128), per_head(LATENT)]
    if not first:
        in_specs += state_specs
        args += list(carry)
    if last:
        in_specs.append(pl.BlockSpec((group, LATENT, 128), lambda i: (i, 0, 0)))
        args.append(up)
        out_shape = jax.ShapeDtypeStruct((2, 2, toks // 2, heads * 128), jnp.float32)
        out_specs = pl.BlockSpec((2, 2, toks // 2, group * 128), lambda i: (0, 0, 0, i))
    else:
        out_shape = [
            jax.ShapeDtypeStruct((heads, toks, w), jnp.float32) for w in (128, 128, LATENT)
        ]
        out_specs = state_specs
    count = sum(k.shape[0] for k in keys)
    rows = heads * toks
    return pl.pallas_call(
        functools.partial(attend_kernel, len(keys), first, last),
        grid=(heads // group,),
        in_specs=in_specs,
        out_specs=out_specs,
        out_shape=out_shape,
        compiler_params=pltpu.CompilerParams(vmem_limit_bytes=VMEM),
        cost_estimate=pl.CostEstimate(
            flops=2 * rows * count * (WIDTH + LATENT),
            bytes_accessed=2 * count * WIDTH + rows * 4096,
            transcendentals=rows * count,
        ),
    )(*args)


def project_kernel(here_ref, v_ref, own_ref, other_ref, out_ref):
    core, near = here_ref[0], here_ref[1]
    half = v_ref.shape[1] // 2
    v_own = v_ref[:, pl.ds(pl.multiple_of(core * half, half), half)]
    v_other = v_ref[:, pl.ds(pl.multiple_of((1 - core) * half, half), half)]
    part = lax.dot_general(v_own, own_ref[0], NT, preferred_element_type=jnp.float32)
    part += lax.dot_general(v_other, other_ref[0], NT, preferred_element_type=jnp.float32)
    toks = part.shape[0] // 2
    part = part.astype(jnp.bfloat16)
    out_ref[0, near] = part[:toks]
    out_ref[0, 1 - near] = part[toks:]


def project(here, v, w_own, w_other):
    blocks, cols, depth = w_own.shape
    toks = v.shape[0] // 2
    return pl.pallas_call(
        project_kernel,
        grid=(blocks,),
        in_specs=[
            pl.BlockSpec(memory_space=pltpu.SMEM),
            pl.BlockSpec(v.shape, lambda i: (0, 0)),
            pl.BlockSpec((1, cols, depth), lambda i: (i, 0, 0)),
            pl.BlockSpec((1, cols, depth), lambda i: (i, 0, 0)),
        ],
        out_specs=pl.BlockSpec((1, 2, toks, cols), lambda i: (i, 0, 0, 0)),
        out_shape=jax.ShapeDtypeStruct((blocks, 2, toks, cols), jnp.bfloat16),
        compiler_params=pltpu.CompilerParams(vmem_limit_bytes=VMEM),
        cost_estimate=pl.CostEstimate(
            flops=8 * toks * blocks * cols * depth,
            bytes_accessed=4 * blocks * cols * depth,
            transcendentals=0,
        ),
    )(here, v, w_own, w_other)


def total_kernel(parts_ref, out_ref):
    heads = parts_ref.shape[0]
    for near in range(2):
        total = parts_ref[0, near].astype(jnp.float32)
        for h in range(1, heads):
            total += parts_ref[h, near].astype(jnp.float32)
        for far in range(2):
            at = far * 256 + near * 128
            out_ref[:, at : at + 128] = total[:, far * 128 : far * 128 + 128].astype(out_ref.dtype)


def add_heads(parts):
    _, _, toks, cols = parts.shape
    return pl.pallas_call(
        total_kernel,
        out_shape=jax.ShapeDtypeStruct((toks, 2 * cols), jnp.bfloat16),
        compiler_params=pltpu.CompilerParams(vmem_limit_bytes=VMEM),
    )(parts)


def on_device(queries, latents, positions, lengths, value_up, out_weight):
    toks, heads, width = queries.shape
    ends = jnp.cumsum(lengths).astype(jnp.int32)
    core = lax.axis_index("core").astype(jnp.int32)
    far = lax.axis_index("zh_lat")
    near = lax.axis_index("zl_lat").astype(jnp.int32)

    parts = position_parts(positions)
    zeros = lambda n: jnp.zeros((toks, n), jnp.bfloat16)
    key_rows = jnp.concatenate(
        [latents[:, :LATENT], rotate(latents[:, LATENT:], positions), parts, zeros(62)], axis=1
    )
    along_y = lax.all_to_all(
        jnp.broadcast_to(key_rows[None], (8, toks, WIDTH)), "y", 0, 0
    ).reshape(8 * toks, WIDTH)

    tail = jnp.concatenate([zeros(2), parts, zeros(60)], axis=1)
    q_own = jnp.concatenate(
        [
            queries[..., :LATENT],
            rotate(queries[..., LATENT:], positions),
            jnp.broadcast_to(tail[:, None, :], (toks, heads, 64)),
        ],
        axis=2,
    ).transpose(1, 0, 2)
    q = jnp.concatenate([q_own, swap(q_own, "core")], axis=1)

    from_left = shift_z(along_y, 1)
    from_right = shift_z(along_y, -1)
    carry = attend(ends, q, [along_y])
    middle = along_y.shape[0] // 2
    across_left = shift_z(from_left[:middle], 1)
    across_right = shift_z(from_right[middle:], -1)
    carry = attend(ends, q, [from_left, from_right], carry)

    w, _ = lax.optimization_barrier((out_weight.T, along_y))
    w = lax.all_to_all(w, "core", 1, 0, tiled=True)
    w_far = swap(w, "zh_lat")
    w = jnp.where(far == 0, jnp.stack([w, w_far]), jnp.stack([w_far, w]))
    w_own = lax.all_gather(w.reshape(1, -1, w.shape[2]), "y", axis=0, tiled=True)
    w_other = swap(w_own, "core")

    both = attend(ends, q, [across_left, across_right], carry, value_up)
    mine, theirs = both[0], swap(both[1], "core")
    level = jnp.maximum(mine[1], theirs[1])
    share_mine = jnp.exp2(mine[1] - level)
    share_theirs = jnp.exp2(theirs[1] - level)
    values = (
        (mine[0] * share_mine + theirs[0] * share_theirs) / (share_mine + share_theirs)
    ).astype(jnp.bfloat16)
    v = jnp.concatenate([values, swap(values, "zl_lat")], axis=0)

    partial = project(jnp.stack([core, near]), v, w_own, w_other)
    rows = partial.shape[2]
    cols = partial.shape[3]
    arrived = lax.all_to_all(
        partial.reshape(16, rows, cols), ("z_hi", "x", "zl_lat"), 0, 0
    ).reshape(8, 2, rows, cols)
    return add_heads(arrived)


def solution(mesh):
    grid = Mesh(
        mesh.devices.reshape(8, 2, 2, 2, 2, 4), ("y", "zh_lat", "zl_lat", "core", "z_hi", "x")
    )
    seq, head = ("y", "zh_lat", "zl_lat", "core"), ("z_hi", "x")
    placed = (
        P(seq, head, None),
        P(seq, None),
        P(seq),
        P(),
        P(head, None, None),
        P(head, seq),
    )
    return jax.shard_map(
        on_device, mesh=grid, in_specs=placed, out_specs=P(seq, head), check_vma=False
    )
```

time: 437 us -> 175 us (0.40)
  the two profiles are of different devices: /device:TPU:8 before, /device:TPU:65 now
where the time goes in v1:
time: 175 us; the launch traced here: 174 us
  blocking collectives  59.1 us (34%)
  waiting for transfers between devices  39.7 us (23%)
  starting transfers between devices  31.7 us (18%)
  Pallas kernels  23.1 us (13%)
  between operations  13.7 us (8%)
  local copies, waits for them, and re-layouts  3.78 us (2%)
  other arithmetic  3.32 us (2%)
    all_gather x1, waiting for transfers between devices, on_device(): lax.all_gather(w.reshape(1, -1, w.shape[2]), 'y', axis=0, tiled=True)  29.5 us
    all_to_all x1, blocking collectives, on_device(): lax.all_to_all(partial.reshape(16, rows, cols), ('z_hi', 'x', 'zl_lat'),...  27.6 us
    all_to_all x1, blocking collectives, on_device(): lax.all_to_all(jnp.broadcast_to(key_rows[None], (8, toks, WIDTH)), 'y', 0...  25.8 us
    ppermute x5, starting transfers between devices, swap(): return lax.ppermute(x, axis, [(0, 1), (1, 0)])  21.2 us
    pallas_call x3, Pallas kernels, attend(): pl.pallas_call(functools.partial(attend_kernel, len(keys), first, last),...  16.9 us
    ppermute x4, starting transfers between devices, shift_z(): return lax.ppermute(x, ('zh_lat', 'zl_lat', 'z_hi'), perm)  10.6 us
    ppermute x5, waiting for transfers between devices, swap(): return lax.ppermute(x, axis, [(0, 1), (1, 0)])  10.2 us
    all_to_all x1, blocking collectives, on_device(): w = lax.all_to_all(w, 'core', 1, 0, tiled=True)  5.72 us
  transfers between devices with their start and end apart: 10, of which 4 were waited for; matrix products, arithmetic and copies ran while one was open for 1% of the time, Pallas kernels for 10%

profile of v1, /device:TPU:65, one launch (start us, length us, event | category | flops | bytes accessed | tf_op | source)
XLA Modules:
  0.0 174.4 jit_solution(12631967034474989862)
XLA Ops:
  6.5 0.7 fusion.18
  7.5 0.8 slice.55
  8.4 1.0 fusion.16
  9.5 25.8 %all_to_all.29 = bf16[8,64,640]{2,1,0:T(8,128)(2,1)S(1)} all-to-all(bf16[8,64,640]{2,1,0:T(8,128)(2,1)S(1)} %broadcast_in_dim.14), channel_id=1, replica_groups=mesh['y'=8,'zh_lat'=2,'zl_lat'=2,'core'=2,'z_hi'=2,'x'=4] {'y'}, dimensions={0} | all-to-all | bytes 1310720 | tf_op jit(solution)/shard_map/all_to_all | solution.py:226
  35.3 5.7 %all_to_all.30 = bf16[64,2,512]{2,0,1:T(8,128)(2,1)S(1)} all-to-all(bf16[64,2,512]{2,0,1:T(8,128)(2,1)S(1)} %bitcast.68), channel_id=1, replica_groups=mesh['y'=8,'zh_lat'=2,'zl_lat'=2,'core'=2,'z_hi'=2,'x'=4] {'core'}, dimensions={1} | all-to-all | bytes 262144 | tf_op jit(solution)/shard_map/all_to_all | solution.py:250
  41.1 5.8 %collective-permute-start.7 = (bf16[128,512]{1,0:T(8,128)(2,1)S(1)}, bf16[128,512]{1,0:T(8,128)(2,1)S(1)}, u32[]{:S(2)}, u32[]{:S(2)}) collective-permute-start(bf16[128,512]{1,0:T(8,128)(2,1)S(1)} %bitcast.66), channel_id=1, source_target_pairs={{0,32},{32,0},{1,33},{33,1},{2,34},{34,2},{3,35},{35,3},{4,36},{36... | collective-permute-start | bytes 393224 | tf_op jit(solution)/shard_map/ppermute | solution.py:51
  46.9 5.1 %collective-permute-done.7 = bf16[128,512]{1,0:T(8,128)(2,1)S(1)} collective-permute-done((bf16[128,512]{1,0:T(8,128)(2,1)S(1)}, bf16[128,512]{1,0:T(8,128)(2,1)S(1)}, u32[]{:S(2)}, u32[]{:S(2)}) %collective-permute-start.7) | collective-permute-done | bytes 131104 | tf_op jit(solution)/shard_map/ppermute | solution.py:51
  54.2 2.4 %collective-permute-start = (bf16[8,64,640]{2,1,0:T(8,128)(2,1)S(1)}, bf16[8,64,640]{2,1,0:T(8,128)(2,1)S(1)}, u32[]{:S(2)}, u32[]{:S(2)}) collective-permute-start(bf16[8,64,640]{2,1,0:T(8,128)(2,1)S(1)} %maximum_bitcast_fusion), channel_id=1, source_target_pairs={{0,8},{8,0},{1,9},{9,1},{2,10},{10,2},{3,11},{11,3},{4,12},{12,4},... | collective-permute-start | bytes 1966088 | tf_op jit(solution)/shard_map/ppermute | solution.py:51
  56.6 1.9 %collective-permute-start.1 = (bf16[512,640]{1,0:T(8,128)(2,1)S(1)}, bf16[512,640]{1,0:T(8,128)(2,1)S(1)}, u32[]{:S(2)}, u32[]{:S(2)}) collective-permute-start(bf16[512,640]{1,0:T(8,128)(2,1)S(1)} %bitcast.59), channel_id=1, source_target_pairs={{0,16},{16,32},{32,48},{48,4},{4,20},{20,36},{36,52},{52,0},{1,17}... | collective-permute-start | bytes 1966088 | tf_op jit(solution)/shard_map/ppermute | solution.py:47
  58.5 3.4 %collective-permute-start.3 = (bf16[512,640]{1,0:T(8,128)(2,1)S(1)}, bf16[512,640]{1,0:T(8,128)(2,1)S(1)}, u32[]{:S(2)}, u32[]{:S(2)}) collective-permute-start(bf16[512,640]{1,0:T(8,128)(2,1)S(1)} %bitcast.60), channel_id=1, source_target_pairs={{0,52},{16,0},{32,16},{48,32},{4,48},{20,4},{36,20},{52,36},{1,53}... | collective-permute-start | bytes 1966088 | tf_op jit(solution)/shard_map/ppermute | solution.py:47
  61.9 29.5 %all-gather.2.cloned.1.call-done.own_ref = bf16[8,256,512]{2,1,0:T(8,128)(2,1)} async-done(((bf16[1,256,512]{2,1,0:T(8,128)(2,1)}), bf16[8,256,512]{2,1,0:T(8,128)(2,1)}) %all-gather.2.cloned.1.call-update) | async-done | bytes 2097168 | tf_op jit(solution)/shard_map/all_gather | solution.py:253
  91.4 6.5 %collective-permute-start.8 = (bf16[8,256,512]{2,1,0:T(8,128)(2,1)}, bf16[8,256,512]{2,1,0:T(8,128)(2,1)}, u32[]{:S(2)}, u32[]{:S(2)}) collective-permute-start(bf16[8,256,512]{2,1,0:T(8,128)(2,1)} %all-gather.2.cloned.1.call-done.own_ref), channel_id=1, source_target_pairs={{0,8},{8,0},{1,9},{9,1},{2,10},{10,2},{3,11},{11,3},{4,12},{12,4},... | collective-permute-start | bytes 6291464 | tf_op jit(solution)/shard_map/ppermute | solution.py:51
  98.2 3.3 %collective-permute-start.2 = (bf16[256,640]{1,0:T(8,128)(2,1)S(1)}, bf16[256,640]{1,0:T(8,128)(2,1)S(1)}, u32[]{:S(2)}, u32[]{:S(2)}) collective-permute-start(bf16[256,640]{1,0:T(8,128)(2,1)S(1)} %slice.65), channel_id=1, source_target_pairs={{0,16},{16,32},{32,48},{48,4},{4,20},{20,36},{36,52},{52,0},{1,17}... | collective-permute-start | bytes 983048 | tf_op jit(solution)/shard_map/ppermute | solution.py:47
  101.5 2.0 %collective-permute-start.4 = (bf16[256,640]{1,0:T(8,128)(2,1)S(1)}, bf16[256,640]{1,0:T(8,128)(2,1)S(1)}, u32[]{:S(2)}, u32[]{:S(2)}) collective-permute-start(bf16[256,640]{1,0:T(8,128)(2,1)S(1)} %slice.66), channel_id=1, source_target_pairs={{0,52},{16,0},{32,16},{48,32},{4,48},{20,4},{36,20},{52,36},{1,53}... | collective-permute-start | bytes 983048 | tf_op jit(solution)/shard_map/ppermute | solution.py:47
  103.5 3.7 %shard_map.64 = (f32[8,128,128]{2,1,0:T(8,128)S(1)}, f32[8,128,128]{2,1,0:T(8,128)S(1)}, f32[8,128,512]{2,1,0:T(8,128)S(1)}) custom-call(s32[8]{0:T(128)S(1)} %bitcast.62, bf16[8,128,640]{2,1,0:T(8,128)(2,1)S(1)} %pad_maximum_fusion.refs_1_, bf16[512,640]{1,0:T(8,128)(2,1)S(1)} %bitcast.61), custom_call_target="tpu_custom_call" | custom-call | flops 1207959552 | bytes 4849664 | tf_op jit(solution)/shard_map/pallas_call | solution.py:143
  107.2 1.3 copy-done.2
  108.6 7.6 %shard_map.65 = (f32[8,128,128]{2,1,0:T(8,128)S(1)}, f32[8,128,128]{2,1,0:T(8,128)S(1)}, f32[8,128,512]{2,1,0:T(8,128)}) custom-call(s32[8]{0:T(128)S(1)} %bitcast.63, bf16[8,128,640]{2,1,0:T(8,128)(2,1)S(1)} %pad_maximum_fusion.refs_1_, bf16[512,640]{1,0:T(8,128)(2,1)S(1)} %collective-permute-done.1.refs_2_, ...), custom_call_target="tpu_custom_call" | custom-call | flops 2415919104 | bytes 5505024 | tf_op jit(solution)/shard_map/pallas_call | solution.py:143
  116.2 5.6 %shard_map.66 = f32[2,2,64,1024]{3,2,1,0:T(8,128)S(1)} custom-call(s32[8]{0:T(128)S(1)} %bitcast.64, bf16[8,128,640]{2,1,0:T(8,128)(2,1)S(1)} %pad_maximum_fusion.refs_1_, bf16[256,640]{1,0:T(8,128)(2,1)S(1)} %collective-permute-done.2.refs_2_, bf16[256,640]{1,0:T(8,128)(2,1)S(1)} %collective-permute-done.4.refs_3_, ...), custom_call_target="tpu_custom_call" | custom-call | flops 1207959552 | bytes 4849664 | tf_op jit(solution)/shard_map/pallas_call | solution.py:143
  121.9 2.6 %collective-permute-start.5 = (f32[2,64,1024]{2,1,0:T(8,128)S(1)}, f32[2,64,1024]{2,1,0:T(8,128)S(1)}, u32[]{:S(2)}, u32[]{:S(2)}) collective-permute-start(f32[2,64,1024]{2,1,0:T(8,128)S(1)} %slice_bitcast_fusion), channel_id=1, source_target_pairs={{0,8},{8,0},{1,9},{9,1},{2,10},{10,2},{3,11},{11,3},{4,12},{12,4},... | collective-permute-start | bytes 1572872 | tf_op jit(solution)/shard_map/ppermute | solution.py:51
  124.5 1.5 collective-permute-done.5
  126.1 3.9 %collective-permute-start.6 = (bf16[64,1024]{1,0:T(8,128)(2,1)S(1)}, bf16[64,1024]{1,0:T(8,128)(2,1)S(1)}, u32[]{:S(2)}, u32[]{:S(2)}) collective-permute-start(bf16[64,1024]{1,0:T(8,128)(2,1)S(1)} %fusion.12), channel_id=1, source_target_pairs={{0,16},{16,0},{1,17},{17,1},{2,18},{18,2},{3,19},{19,3},{4,20},{20... | collective-permute-start | bytes 393224 | tf_op jit(solution)/shard_map/ppermute | solution.py:51
  130.1 3.6 %collective-permute-done.6 = bf16[64,1024]{1,0:T(8,128)(2,1)S(1)} collective-permute-done((bf16[64,1024]{1,0:T(8,128)(2,1)S(1)}, bf16[64,1024]{1,0:T(8,128)(2,1)S(1)}, u32[]{:S(2)}, u32[]{:S(2)}) %collective-permute-start.6) | collective-permute-done | bytes 131104 | tf_op jit(solution)/shard_map/ppermute | solution.py:51
  133.7 5.5 %shard_map.67 = bf16[8,2,64,256]{3,2,1,0:T(8,128)(2,1)S(1)} custom-call(s32[2]{0:T(128)S(1)} %pad_add_fusion.here_ref, bf16[128,1024]{1,0:T(8,128)(2,1)S(1)} %pad_maximum_fusion.1.v_ref, bf16[8,256,512]{2,1,0:T(8,128)(2,1)S(1)} %copy-done, bf16[8,256,512]{2,1,0:T(8,128)(2,1)} %collective-permute-done.8.other_ref), custom_call_target="tpu_custom_call" | custom-call | flops 536870912 | bytes 4194304 | tf_op jit(solution)/shard_map/pallas_call | solution.py:174
  139.2 27.6 %all_to_all.31 = bf16[16,64,256]{2,1,0:T(8,128)(2,1)S(1)} all-to-all(bf16[16,64,256]{2,1,0:T(8,128)(2,1)S(1)} %bitcast.57), channel_id=1, replica_groups=mesh['y'=8,'zh_lat'=2,'zl_lat'=2,'core'=2,'z_hi'=2,'x'=4] {'z_hi','x','z..., dimensions={0} | all-to-all | bytes 1048576 | tf_op jit(solution)/shard_map/all_to_all | solution.py:269
  (48 shorter events, 3.9 us)
Async XLA Ops:
  6.5 28.8 %copy-start.4 = (bf16[1024,64]{0,1:T(8,128)(2,1)S(1)}, bf16[1024,64]{0,1:T(8,128)(2,1)}, u32[]{:S(2)}) copy-start(bf16[1024,64]{0,1:T(8,128)(2,1)} %param.11) | copy-start | bytes 393220
  6.5 84.8 %all-gather.2.cloned.1.call-start = ((), (), s32[]{:S(2)}) async-start(), calls=%async_computation.3 | async-start | bytes 2359296 | tf_op jit(solution)/shard_map/all_gather | solution.py:253
  35.3 17.5 %slice-start = ((bf16[64,8,576]{2,1,0:T(8,128)(2,1)}), bf16[64,8,512]{2,1,0:T(8,128)(2,1)S(1)}, s32[]{:S(2)}) async-start(bf16[64,8,576]{2,1,0:T(8,128)(2,1)} %param.6), calls=%async_computation.4 | async-start | bytes 1048576 | tf_op jit(solution)/shard_map/slice | solution.py:233
  41.1 10.9 %collective-permute-start.7 = (bf16[128,512]{1,0:T(8,128)(2,1)S(1)}, bf16[128,512]{1,0:T(8,128)(2,1)S(1)}, u32[]{:S(2)}, u32[]{:S(2)}) collective-permute-start(bf16[128,512]{1,0:T(8,128)(2,1)S(1)} %bitcast.66), channel_id=1, source_target_pairs={{0,32},{32,0},{1,33},{33,1},{2,34},{34,2},{3,35},{35,3},{4,36},{36... | collective-permute-start | bytes 393224 | tf_op jit(solution)/shard_map/ppermute | solution.py:51
  52.7 1.1 copy-start.3
  53.8 44.0 %copy-start.5 = (s32[8]{0:T(128)S(1)}, s32[8]{0:T(128)}, u32[]{:S(2)}) copy-start(s32[8]{0:T(128)} %param.9) | copy-start | bytes 100
  54.2 43.8 %collective-permute-start = (bf16[8,64,640]{2,1,0:T(8,128)(2,1)S(1)}, bf16[8,64,640]{2,1,0:T(8,128)(2,1)S(1)}, u32[]{:S(2)}, u32[]{:S(2)}) collective-permute-start(bf16[8,64,640]{2,1,0:T(8,128)(2,1)S(1)} %maximum_bitcast_fusion), channel_id=1, source_target_pairs={{0,8},{8,0},{1,9},{9,1},{2,10},{10,2},{3,11},{11,3},{4,12},{12,4},... | collective-permute-start | bytes 1966088 | tf_op jit(solution)/shard_map/ppermute | solution.py:51
  56.6 41.6 %collective-permute-start.1 = (bf16[512,640]{1,0:T(8,128)(2,1)S(1)}, bf16[512,640]{1,0:T(8,128)(2,1)S(1)}, u32[]{:S(2)}, u32[]{:S(2)}) collective-permute-start(bf16[512,640]{1,0:T(8,128)(2,1)S(1)} %bitcast.59), channel_id=1, source_target_pairs={{0,16},{16,32},{32,48},{48,4},{4,20},{20,36},{36,52},{52,0},{1,17}... | collective-permute-start | bytes 1966088 | tf_op jit(solution)/shard_map/ppermute | solution.py:47
  58.5 43.0 %collective-permute-start.3 = (bf16[512,640]{1,0:T(8,128)(2,1)S(1)}, bf16[512,640]{1,0:T(8,128)(2,1)S(1)}, u32[]{:S(2)}, u32[]{:S(2)}) collective-permute-start(bf16[512,640]{1,0:T(8,128)(2,1)S(1)} %bitcast.60), channel_id=1, source_target_pairs={{0,52},{16,0},{32,16},{48,32},{4,48},{20,4},{36,20},{52,36},{1,53}... | collective-permute-start | bytes 1966088 | tf_op jit(solution)/shard_map/ppermute | solution.py:47
  91.4 42.3 %collective-permute-start.8 = (bf16[8,256,512]{2,1,0:T(8,128)(2,1)}, bf16[8,256,512]{2,1,0:T(8,128)(2,1)}, u32[]{:S(2)}, u32[]{:S(2)}) collective-permute-start(bf16[8,256,512]{2,1,0:T(8,128)(2,1)} %all-gather.2.cloned.1.call-done.own_ref), channel_id=1, source_target_pairs={{0,8},{8,0},{1,9},{9,1},{2,10},{10,2},{3,11},{11,3},{4,12},{12,4},... | collective-permute-start | bytes 6291464 | tf_op jit(solution)/shard_map/ppermute | solution.py:51
  98.2 18.0 %collective-permute-start.2 = (bf16[256,640]{1,0:T(8,128)(2,1)S(1)}, bf16[256,640]{1,0:T(8,128)(2,1)S(1)}, u32[]{:S(2)}, u32[]{:S(2)}) collective-permute-start(bf16[256,640]{1,0:T(8,128)(2,1)S(1)} %slice.65), channel_id=1, source_target_pairs={{0,16},{16,32},{32,48},{48,4},{4,20},{20,36},{36,52},{52,0},{1,17}... | collective-permute-start | bytes 983048 | tf_op jit(solution)/shard_map/ppermute | solution.py:47
  101.5 14.7 %collective-permute-start.4 = (bf16[256,640]{1,0:T(8,128)(2,1)S(1)}, bf16[256,640]{1,0:T(8,128)(2,1)S(1)}, u32[]{:S(2)}, u32[]{:S(2)}) collective-permute-start(bf16[256,640]{1,0:T(8,128)(2,1)S(1)} %slice.66), channel_id=1, source_target_pairs={{0,52},{16,0},{32,16},{48,32},{4,48},{20,4},{36,20},{52,36},{1,53}... | collective-permute-start | bytes 983048 | tf_op jit(solution)/shard_map/ppermute | solution.py:47
  107.2 1.3 copy-start.2
  108.6 7.6 %copy-start.1 = (bf16[8,512,128]{2,1,0:T(8,128)(2,1)S(1)}, bf16[8,512,128]{2,1,0:T(8,128)(2,1)}, u32[]{:S(2)}) copy-start(bf16[8,512,128]{2,1,0:T(8,128)(2,1)} %refs_7_.1) | copy-start | bytes 3145732
  121.8 11.9 %copy-start = (bf16[8,256,512]{2,1,0:T(8,128)(2,1)S(1)}, bf16[8,256,512]{2,1,0:T(8,128)(2,1)}, u32[]{:S(2)}) copy-start(bf16[8,256,512]{2,1,0:T(8,128)(2,1)} %all-gather.2.cloned.1.call-done.own_ref) | copy-start | bytes 6291460
  121.9 4.1 %collective-permute-start.5 = (f32[2,64,1024]{2,1,0:T(8,128)S(1)}, f32[2,64,1024]{2,1,0:T(8,128)S(1)}, u32[]{:S(2)}, u32[]{:S(2)}) collective-permute-start(f32[2,64,1024]{2,1,0:T(8,128)S(1)} %slice_bitcast_fusion), channel_id=1, source_target_pairs={{0,8},{8,0},{1,9},{9,1},{2,10},{10,2},{3,11},{11,3},{4,12},{12,4},... | collective-permute-start | bytes 1572872 | tf_op jit(solution)/shard_map/ppermute | solution.py:51
  126.1 7.5 %collective-permute-start.6 = (bf16[64,1024]{1,0:T(8,128)(2,1)S(1)}, bf16[64,1024]{1,0:T(8,128)(2,1)S(1)}, u32[]{:S(2)}, u32[]{:S(2)}) collective-permute-start(bf16[64,1024]{1,0:T(8,128)(2,1)S(1)} %fusion.12), channel_id=1, source_target_pairs={{0,16},{16,0},{1,17},{17,1},{2,18},{18,2},{3,19},{19,3},{4,20},{20... | collective-permute-start | bytes 393224 | tf_op jit(solution)/shard_map/ppermute | solution.py:51
Sparse Core Ops, SparseCore 0:
  52.9 38.4 all-gather.1

commit v2 on v1

--- a/solution.py
+++ b/solution.py
@@ -155,21 +155,17 @@
     )(*args)
 
 
-def project_kernel(here_ref, v_ref, own_ref, other_ref, out_ref):
-    core, near = here_ref[0], here_ref[1]
-    half = v_ref.shape[1] // 2
-    v_own = v_ref[:, pl.ds(pl.multiple_of(core * half, half), half)]
-    v_other = v_ref[:, pl.ds(pl.multiple_of((1 - core) * half, half), half)]
-    part = lax.dot_general(v_own, own_ref[0], NT, preferred_element_type=jnp.float32)
-    part += lax.dot_general(v_other, other_ref[0], NT, preferred_element_type=jnp.float32)
+def project_kernel(near_ref, v_ref, w_ref, out_ref):
+    near = near_ref[0]
+    part = lax.dot_general(v_ref[...], w_ref[0], NT, preferred_element_type=jnp.float32)
     toks = part.shape[0] // 2
     part = part.astype(jnp.bfloat16)
     out_ref[0, near] = part[:toks]
     out_ref[0, 1 - near] = part[toks:]
 
 
-def project(here, v, w_own, w_other):
-    blocks, cols, depth = w_own.shape
+def project(near, v, w):
+    blocks, cols, depth = w.shape
     toks = v.shape[0] // 2
     return pl.pallas_call(
         project_kernel,
@@ -178,17 +174,16 @@
             pl.BlockSpec(memory_space=pltpu.SMEM),
             pl.BlockSpec(v.shape, lambda i: (0, 0)),
             pl.BlockSpec((1, cols, depth), lambda i: (i, 0, 0)),
-            pl.BlockSpec((1, cols, depth), lambda i: (i, 0, 0)),
         ],
         out_specs=pl.BlockSpec((1, 2, toks, cols), lambda i: (i, 0, 0, 0)),
         out_shape=jax.ShapeDtypeStruct((blocks, 2, toks, cols), jnp.bfloat16),
         compiler_params=pltpu.CompilerParams(vmem_limit_bytes=VMEM),
         cost_estimate=pl.CostEstimate(
-            flops=8 * toks * blocks * cols * depth,
-            bytes_accessed=4 * blocks * cols * depth,
+            flops=4 * toks * blocks * cols * depth,
+            bytes_accessed=2 * blocks * cols * depth,
             transcendentals=0,
         ),
-    )(here, v, w_own, w_other)
+    )(near, v, w)
 
 
 def total_kernel(parts_ref, out_ref):
@@ -214,9 +209,10 @@
 def on_device(queries, latents, positions, lengths, value_up, out_weight):
     toks, heads, width = queries.shape
     ends = jnp.cumsum(lengths).astype(jnp.int32)
-    core = lax.axis_index("core").astype(jnp.int32)
-    far = lax.axis_index("zh_lat")
     near = lax.axis_index("zl_lat").astype(jnp.int32)
+
+    w = lax.all_gather(out_weight.T, ("y", "zh_lat", "core"), axis=0, tiled=True)
+    w = w.reshape(8, w.shape[0] // 8, w.shape[1])
 
     parts = position_parts(positions)
     zeros = lambda n: jnp.zeros((toks, n), jnp.bfloat16)
@@ -240,18 +236,11 @@
 
     from_left = shift_z(along_y, 1)
     from_right = shift_z(along_y, -1)
-    carry = attend(ends, q, [along_y])
+    carry = attend(ends, q, [along_y], group=8)
     middle = along_y.shape[0] // 2
     across_left = shift_z(from_left[:middle], 1)
     across_right = shift_z(from_right[middle:], -1)
-    carry = attend(ends, q, [from_left, from_right], carry)
-
-    w, _ = lax.optimization_barrier((out_weight.T, along_y))
-    w = lax.all_to_all(w, "core", 1, 0, tiled=True)
-    w_far = swap(w, "zh_lat")
-    w = jnp.where(far == 0, jnp.stack([w, w_far]), jnp.stack([w_far, w]))
-    w_own = lax.all_gather(w.reshape(1, -1, w.shape[2]), "y", axis=0, tiled=True)
-    w_other = swap(w_own, "core")
+    carry = attend(ends, q, [from_left, from_right], carry, group=8)
 
     both = attend(ends, q, [across_left, across_right], carry, value_up)
     mine, theirs = both[0], swap(both[1], "core")
@@ -263,7 +252,7 @@
     ).astype(jnp.bfloat16)
     v = jnp.concatenate([values, swap(values, "zl_lat")], axis=0)
 
-    partial = project(jnp.stack([core, near]), v, w_own, w_other)
+    partial = project(near.reshape(1), v, w)
     rows = partial.shape[2]
     cols = partial.shape[3]
     arrived = lax.all_to_all(

time: 175 us -> 164 us (0.937)
  the two profiles are of different devices: /device:TPU:65 before, /device:TPU:64 now
where the time goes in v2:
time: 164 us
  waiting for transfers between devices  67 us (41%)
  blocking collectives  29.2 us (18%)
  starting transfers between devices  26.3 us (16%)
  Pallas kernels  18.2 us (11%)
  between operations  13.6 us (8%)
  local copies, waits for them, and re-layouts  6.83 us (4%)
  other arithmetic  2.52 us (2%)
    ppermute x4, waiting for transfers between devices, shift_z(): return lax.ppermute(x, ('zh_lat', 'zl_lat', 'z_hi'), perm)  39.4 us
    all_to_all x1, blocking collectives, on_device(): lax.all_to_all(partial.reshape(16, rows, cols), ('z_hi', 'x', 'zl_lat'),...  29.2 us
    all_to_all x1, waiting for transfers between devices, on_device(): lax.all_to_all(jnp.broadcast_to(key_rows[None], (8, toks, WIDTH)), 'y', 0...  19.5 us
    pallas_call x3, Pallas kernels, attend(): pl.pallas_call(functools.partial(attend_kernel, len(keys), first, last),...  15 us
    ppermute x4, starting transfers between devices, shift_z(): return lax.ppermute(x, ('zh_lat', 'zl_lat', 'z_hi'), perm)  13.3 us
    ppermute x3, waiting for transfers between devices, swap(): return lax.ppermute(x, axis, [(0, 1), (1, 0)])  7.38 us
    all_to_all x1, starting transfers between devices, on_device(): lax.all_to_all(jnp.broadcast_to(key_rows[None], (8, toks, WIDTH)), 'y', 0...  7.23 us
    ppermute x3, starting transfers between devices, swap(): return lax.ppermute(x, axis, [(0, 1), (1, 0)])  5.76 us
  transfers between devices with their start and end apart: 9, of which 5 were waited for; matrix products, arithmetic and copies ran while one was open for 3% of the time, Pallas kernels for 9%

profile of v2, /device:TPU:64, one launch (start us, length us, event | category | flops | bytes accessed | tf_op | source)
XLA Modules:
  0.0 163.7 jit_solution(10593549839182805965)
XLA Ops:
  7.3 0.7 fusion.18
  8.2 0.8 slice.55
  9.1 1.0 fusion.16
  10.2 0.9 broadcast_in_dim.14
  11.1 7.2 %all-to-all-start = ((bf16[8,64,640]{2,1,0:T(8,128)(2,1)}), bf16[8,64,640]{2,1,0:T(8,128)(2,1)S(1)}, u32[]{:S(2)}, u32[]{:S(2)}) async-start(bf16[8,64,640]{2,1,0:T(8,128)(2,1)} %broadcast_in_dim.14), calls=%async_computation | async-start | bytes 1310720 | tf_op jit(solution)/shard_map/all_to_all | solution.py:222
  18.7 0.7 copy-done.3
  19.8 1.9 %collective-permute-start = (bf16[8,64,640]{2,1,0:T(8,128)(2,1)S(1)}, bf16[8,64,640]{2,1,0:T(8,128)(2,1)S(1)}, u32[]{:S(2)}, u32[]{:S(2)}) collective-permute-start(bf16[8,64,640]{2,1,0:T(8,128)(2,1)S(1)} %maximum_bitcast_fusion), channel_id=1, source_target_pairs={{0,8},{8,0},{1,9},{9,1},{2,10},{10,2},{3,11},{11,3},{4,12},{12,4},... | collective-permute-start | bytes 1966088 | tf_op jit(solution)/shard_map/ppermute | solution.py:51
  21.8 19.5 %all-to-all-done = bf16[8,64,640]{2,1,0:T(8,128)(2,1)S(1)} async-done(((bf16[8,64,640]{2,1,0:T(8,128)(2,1)}), bf16[8,64,640]{2,1,0:T(8,128)(2,1)S(1)}, u32[]{:S(2)}, u32[]{:S(2)}) %all-to-all-start) | async-done | bytes 655392 | tf_op jit(solution)/shard_map/all_to_all | solution.py:222
  41.3 4.4 %collective-permute-start.1 = (bf16[512,640]{1,0:T(8,128)(2,1)S(1)}, bf16[512,640]{1,0:T(8,128)(2,1)S(1)}, u32[]{:S(2)}, u32[]{:S(2)}) collective-permute-start(bf16[512,640]{1,0:T(8,128)(2,1)S(1)} %bitcast.49), channel_id=1, source_target_pairs={{0,16},{16,32},{32,48},{48,4},{4,20},{20,36},{36,52},{52,0},{1,17}... | collective-permute-start | bytes 1966088 | tf_op jit(solution)/shard_map/ppermute | solution.py:47
  45.7 1.9 %collective-permute-start.3 = (bf16[512,640]{1,0:T(8,128)(2,1)S(1)}, bf16[512,640]{1,0:T(8,128)(2,1)S(1)}, u32[]{:S(2)}, u32[]{:S(2)}) collective-permute-start(bf16[512,640]{1,0:T(8,128)(2,1)S(1)} %bitcast.50), channel_id=1, source_target_pairs={{0,52},{16,0},{32,16},{48,32},{4,48},{20,4},{36,20},{52,36},{1,53}... | collective-permute-start | bytes 1966088 | tf_op jit(solution)/shard_map/ppermute | solution.py:47
  48.0 39.0 %collective-permute-done.1.refs_2_ = bf16[512,640]{1,0:T(8,128)(2,1)S(1)} collective-permute-done((bf16[512,640]{1,0:T(8,128)(2,1)S(1)}, bf16[512,640]{1,0:T(8,128)(2,1)S(1)}, u32[]{:S(2)}, u32[]{:S(2)}) %collective-permute-start.1) | collective-permute-done | bytes 655392 | tf_op jit(solution)/shard_map/ppermute | solution.py:47
  87.1 5.1 %collective-permute-start.2 = (bf16[256,640]{1,0:T(8,128)(2,1)S(1)}, bf16[256,640]{1,0:T(8,128)(2,1)S(1)}, u32[]{:S(2)}, u32[]{:S(2)}) collective-permute-start(bf16[256,640]{1,0:T(8,128)(2,1)S(1)} %slice.65), channel_id=1, source_target_pairs={{0,16},{16,32},{32,48},{48,4},{4,20},{20,36},{36,52},{52,0},{1,17}... | collective-permute-start | bytes 983048 | tf_op jit(solution)/shard_map/ppermute | solution.py:47
  92.5 1.9 %collective-permute-start.4 = (bf16[256,640]{1,0:T(8,128)(2,1)S(1)}, bf16[256,640]{1,0:T(8,128)(2,1)S(1)}, u32[]{:S(2)}, u32[]{:S(2)}) collective-permute-start(bf16[256,640]{1,0:T(8,128)(2,1)S(1)} %slice.66), channel_id=1, source_target_pairs={{0,52},{16,0},{32,16},{48,32},{4,48},{20,4},{36,20},{52,36},{1,53}... | collective-permute-start | bytes 983048 | tf_op jit(solution)/shard_map/ppermute | solution.py:47
  94.4 2.4 %shard_map.64 = (f32[8,128,128]{2,1,0:T(8,128)S(1)}, f32[8,128,128]{2,1,0:T(8,128)S(1)}, f32[8,128,512]{2,1,0:T(8,128)S(1)}) custom-call(s32[8]{0:T(128)S(1)} %bitcast.52, bf16[8,128,640]{2,1,0:T(8,128)(2,1)S(1)} %pad_maximum_fusion.refs_1_, bf16[512,640]{1,0:T(8,128)(2,1)S(1)} %bitcast.51), custom_call_target="tpu_custom_call" | custom-call | flops 1207959552 | bytes 4849664 | tf_op jit(solution)/shard_map/pallas_call | solution.py:143
  96.8 1.3 copy-done.2
  98.1 7.1 %shard_map.65 = (f32[8,128,128]{2,1,0:T(8,128)S(1)}, f32[8,128,128]{2,1,0:T(8,128)S(1)}, f32[8,128,512]{2,1,0:T(8,128)}) custom-call(s32[8]{0:T(128)S(1)} %bitcast.53, bf16[8,128,640]{2,1,0:T(8,128)(2,1)S(1)} %pad_maximum_fusion.refs_1_, bf16[512,640]{1,0:T(8,128)(2,1)S(1)} %collective-permute-done.1.refs_2_, ...), custom_call_target="tpu_custom_call" | custom-call | flops 2415919104 | bytes 5505024 | tf_op jit(solution)/shard_map/pallas_call | solution.py:143
  105.2 5.6 %shard_map.66 = f32[2,2,64,1024]{3,2,1,0:T(8,128)S(1)} custom-call(s32[8]{0:T(128)S(1)} %bitcast.54, bf16[8,128,640]{2,1,0:T(8,128)(2,1)S(1)} %pad_maximum_fusion.refs_1_, bf16[256,640]{1,0:T(8,128)(2,1)S(1)} %collective-permute-done.2.refs_2_, bf16[256,640]{1,0:T(8,128)(2,1)S(1)} %collective-permute-done.4.refs_3_, ...), custom_call_target="tpu_custom_call" | custom-call | flops 1207959552 | bytes 4849664 | tf_op jit(solution)/shard_map/pallas_call | solution.py:143
  110.8 1.9 %collective-permute-start.5 = (f32[2,64,1024]{2,1,0:T(8,128)S(1)}, f32[2,64,1024]{2,1,0:T(8,128)S(1)}, u32[]{:S(2)}, u32[]{:S(2)}) collective-permute-start(f32[2,64,1024]{2,1,0:T(8,128)S(1)} %slice_bitcast_fusion), channel_id=1, source_target_pairs={{0,8},{8,0},{1,9},{9,1},{2,10},{10,2},{3,11},{11,3},{4,12},{12,4},... | collective-permute-start | bytes 1572872 | tf_op jit(solution)/shard_map/ppermute | solution.py:51
  112.8 1.9 %collective-permute-done.5 = f32[2,64,1024]{2,1,0:T(8,128)S(1)} collective-permute-done((f32[2,64,1024]{2,1,0:T(8,128)S(1)}, f32[2,64,1024]{2,1,0:T(8,128)S(1)}, u32[]{:S(2)}, u32[]{:S(2)}) %collective-permute-start.5) | collective-permute-done | bytes 524320 | tf_op jit(solution)/shard_map/ppermute | solution.py:51
  114.8 1.9 %collective-permute-start.6 = (bf16[64,1024]{1,0:T(8,128)(2,1)S(1)}, bf16[64,1024]{1,0:T(8,128)(2,1)S(1)}, u32[]{:S(2)}, u32[]{:S(2)}) collective-permute-start(bf16[64,1024]{1,0:T(8,128)(2,1)S(1)} %fusion.12), channel_id=1, source_target_pairs={{0,16},{16,0},{1,17},{17,1},{2,18},{18,2},{3,19},{19,3},{4,20},{20... | collective-permute-start | bytes 393224 | tf_op jit(solution)/shard_map/ppermute | solution.py:51
  116.7 5.5 %collective-permute-done.6 = bf16[64,1024]{1,0:T(8,128)(2,1)S(1)} collective-permute-done((bf16[64,1024]{1,0:T(8,128)(2,1)S(1)}, bf16[64,1024]{1,0:T(8,128)(2,1)S(1)}, u32[]{:S(2)}, u32[]{:S(2)}) %collective-permute-start.6) | collective-permute-done | bytes 131104 | tf_op jit(solution)/shard_map/ppermute | solution.py:51
  122.3 2.2 %copy-done = bf16[2048,1024]{1,0:T(8,128)(2,1)S(1)} copy-done((bf16[2048,1024]{1,0:T(8,128)(2,1)S(1)}, bf16[2048,1024]{1,0:T(8,128)(2,1)}, u32[]{:S(2)}) %copy-start) | copy-done | bytes 4194328
  124.5 2.5 %shard_map.67 = bf16[8,2,64,256]{3,2,1,0:T(8,128)(2,1)S(1)} custom-call(s32[1]{0:T(128)} %bitcast.near_ref, bf16[128,1024]{1,0:T(8,128)(2,1)S(1)} %pad_maximum_fusion.1.v_ref, bf16[8,256,1024]{2,1,0:T(8,128)(2,1)S(1)} %bitcast.46), custom_call_target="tpu_custom_call" | custom-call | flops 536870912 | bytes 4194304 | tf_op jit(solution)/shard_map/pallas_call | solution.py:170
  127.0 29.2 %all_to_all.10 = bf16[16,64,256]{2,1,0:T(8,128)(2,1)S(1)} all-to-all(bf16[16,64,256]{2,1,0:T(8,128)(2,1)S(1)} %bitcast.47), channel_id=1, replica_groups=mesh['y'=8,'zh_lat'=2,'zl_lat'=2,'core'=2,'z_hi'=2,'x'=4] {'z_hi','x','z..., dimensions={0} | all-to-all | bytes 1048576 | tf_op jit(solution)/shard_map/all_to_all | solution.py:258
  (39 shorter events, 3.4 us)
Async XLA Ops:
  6.5 115.7 %all-gather.2.cloned.1.call-start = ((), (), s32[]{:S(2)}) async-start(), calls=%async_computation.2 | async-start | bytes 4325376 | tf_op jit(solution)/shard_map/all_gather | solution.py:214
  11.1 7.3 %slice-start = ((bf16[64,8,576]{2,1,0:T(8,128)(2,1)}), bf16[64,8,512]{2,1,0:T(8,128)(2,1)S(1)}, s32[]{:S(2)}) async-start(bf16[64,8,576]{2,1,0:T(8,128)(2,1)} %param.6), calls=%async_computation.3 | async-start | bytes 1048576 | tf_op jit(solution)/shard_map/slice | solution.py:229
  11.1 30.2 %all-to-all-start = ((bf16[8,64,640]{2,1,0:T(8,128)(2,1)}), bf16[8,64,640]{2,1,0:T(8,128)(2,1)S(1)}, u32[]{:S(2)}, u32[]{:S(2)}) async-start(bf16[8,64,640]{2,1,0:T(8,128)(2,1)} %broadcast_in_dim.14), calls=%async_computation | async-start | bytes 1310720 | tf_op jit(solution)/shard_map/all_to_all | solution.py:222
  18.4 1.1 copy-start.3
  19.4 28.2 %copy-start.4 = (s32[8]{0:T(128)S(1)}, s32[8]{0:T(128)}, u32[]{:S(2)}) copy-start(s32[8]{0:T(128)} %param.9) | copy-start | bytes 100
  19.8 28.0 %collective-permute-start = (bf16[8,64,640]{2,1,0:T(8,128)(2,1)S(1)}, bf16[8,64,640]{2,1,0:T(8,128)(2,1)S(1)}, u32[]{:S(2)}, u32[]{:S(2)}) collective-permute-start(bf16[8,64,640]{2,1,0:T(8,128)(2,1)S(1)} %maximum_bitcast_fusion), channel_id=1, source_target_pairs={{0,8},{8,0},{1,9},{9,1},{2,10},{10,2},{3,11},{11,3},{4,12},{12,4},... | collective-permute-start | bytes 1966088 | tf_op jit(solution)/shard_map/ppermute | solution.py:51
  41.3 45.7 %collective-permute-start.1 = (bf16[512,640]{1,0:T(8,128)(2,1)S(1)}, bf16[512,640]{1,0:T(8,128)(2,1)S(1)}, u32[]{:S(2)}, u32[]{:S(2)}) collective-permute-start(bf16[512,640]{1,0:T(8,128)(2,1)S(1)} %bitcast.49), channel_id=1, source_target_pairs={{0,16},{16,32},{32,48},{48,4},{4,20},{20,36},{36,52},{52,0},{1,17}... | collective-permute-start | bytes 1966088 | tf_op jit(solution)/shard_map/ppermute | solution.py:47
  45.7 46.7 %collective-permute-start.3 = (bf16[512,640]{1,0:T(8,128)(2,1)S(1)}, bf16[512,640]{1,0:T(8,128)(2,1)S(1)}, u32[]{:S(2)}, u32[]{:S(2)}) collective-permute-start(bf16[512,640]{1,0:T(8,128)(2,1)S(1)} %bitcast.50), channel_id=1, source_target_pairs={{0,52},{16,0},{32,16},{48,32},{4,48},{20,4},{36,20},{52,36},{1,53}... | collective-permute-start | bytes 1966088 | tf_op jit(solution)/shard_map/ppermute | solution.py:47
  87.1 18.2 %collective-permute-start.2 = (bf16[256,640]{1,0:T(8,128)(2,1)S(1)}, bf16[256,640]{1,0:T(8,128)(2,1)S(1)}, u32[]{:S(2)}, u32[]{:S(2)}) collective-permute-start(bf16[256,640]{1,0:T(8,128)(2,1)S(1)} %slice.65), channel_id=1, source_target_pairs={{0,16},{16,32},{32,48},{48,4},{4,20},{20,36},{36,52},{52,0},{1,17}... | collective-permute-start | bytes 983048 | tf_op jit(solution)/shard_map/ppermute | solution.py:47
  92.5 12.8 %collective-permute-start.4 = (bf16[256,640]{1,0:T(8,128)(2,1)S(1)}, bf16[256,640]{1,0:T(8,128)(2,1)S(1)}, u32[]{:S(2)}, u32[]{:S(2)}) collective-permute-start(bf16[256,640]{1,0:T(8,128)(2,1)S(1)} %slice.66), channel_id=1, source_target_pairs={{0,52},{16,0},{32,16},{48,32},{4,48},{20,4},{36,20},{52,36},{1,53}... | collective-permute-start | bytes 983048 | tf_op jit(solution)/shard_map/ppermute | solution.py:47
  96.8 1.3 copy-start.2
  98.1 7.1 %copy-start.1 = (bf16[8,512,128]{2,1,0:T(8,128)(2,1)S(1)}, bf16[8,512,128]{2,1,0:T(8,128)(2,1)}, u32[]{:S(2)}) copy-start(bf16[8,512,128]{2,1,0:T(8,128)(2,1)} %refs_7_.1) | copy-start | bytes 3145732
  110.8 3.8 %collective-permute-start.5 = (f32[2,64,1024]{2,1,0:T(8,128)S(1)}, f32[2,64,1024]{2,1,0:T(8,128)S(1)}, u32[]{:S(2)}, u32[]{:S(2)}) collective-permute-start(f32[2,64,1024]{2,1,0:T(8,128)S(1)} %slice_bitcast_fusion), channel_id=1, source_target_pairs={{0,8},{8,0},{1,9},{9,1},{2,10},{10,2},{3,11},{11,3},{4,12},{12,4},... | collective-permute-start | bytes 1572872 | tf_op jit(solution)/shard_map/ppermute | solution.py:51
  114.8 7.4 %collective-permute-start.6 = (bf16[64,1024]{1,0:T(8,128)(2,1)S(1)}, bf16[64,1024]{1,0:T(8,128)(2,1)S(1)}, u32[]{:S(2)}, u32[]{:S(2)}) collective-permute-start(bf16[64,1024]{1,0:T(8,128)(2,1)S(1)} %fusion.12), channel_id=1, source_target_pairs={{0,16},{16,0},{1,17},{17,1},{2,18},{18,2},{3,19},{19,3},{4,20},{20... | collective-permute-start | bytes 393224 | tf_op jit(solution)/shard_map/ppermute | solution.py:51
  122.3 2.2 %copy-start = (bf16[2048,1024]{1,0:T(8,128)(2,1)S(1)}, bf16[2048,1024]{1,0:T(8,128)(2,1)}, u32[]{:S(2)}) copy-start(bf16[2048,1024]{1,0:T(8,128)(2,1)} %all-gather.2.cloned.1.call-done) | copy-start | bytes 12582916
Sparse Core Ops, SparseCore 0:
  9.5 84.3 all-gather.1

commit v3 on v2

--- a/solution.py
+++ b/solution.py
@@ -19,22 +19,60 @@
 NT = (((1,), (1,)), ((), ()))
 
 
-def rotate(rotary, where):
+def turns(where_ref, frequency_ref):
+    toks = where_ref.shape[1]
+    row = lax.broadcasted_iota(jnp.int32, (toks, toks), 0)
+    column = lax.broadcasted_iota(jnp.int32, (toks, toks), 1)
+    spread = jnp.broadcast_to(where_ref[...], (toks, toks))
+    where = jnp.sum(jnp.where(row == column, spread, 0).astype(jnp.float32), axis=1, keepdims=True)
+    angles = where * frequency_ref[...]
+    sines = jnp.sin(angles)
+    lane = lax.broadcasted_iota(jnp.int32, sines.shape, 1)
+    return where, jnp.cos(angles), jnp.where(lane < ROPE // 2, -sines, sines)
+
+
+def turned(rotary, cosines, sines):
     half = ROPE // 2
-    frequency = jnp.exp(jnp.arange(half, dtype=jnp.float32) * (-2.0 * math.log(10000.0) / ROPE))
-    angles = where.astype(jnp.float32)[:, None] * frequency[None, :]
-    shape = (angles.shape[0],) + (1,) * (rotary.ndim - 2) + (half,)
-    cosines = jnp.cos(angles).reshape(shape)
-    sines = jnp.sin(angles).reshape(shape)
-    first = rotary[..., :half].astype(jnp.float32)
-    second = rotary[..., half:].astype(jnp.float32)
-    return jnp.concatenate(
-        [first * cosines - second * sines, first * sines + second * cosines], axis=-1
-    ).astype(jnp.bfloat16)
+    other = jnp.concatenate([rotary[:, half:], rotary[:, :half]], axis=1)
+    return rotary * cosines + other * sines
 
 
 def position_parts(where):
-    return jnp.stack([where >> 6, where & 63], axis=-1).astype(jnp.bfloat16)
+    high = jnp.floor(where * (1.0 / 64.0))
+    return high, where - 64.0 * high
+
+
+def key_kernel(where_ref, frequency_ref, latents_ref, out_ref):
+    where, cosines, sines = turns(where_ref, frequency_ref)
+    rotary = turned(latents_ref[:, LATENT:].astype(jnp.float32), cosines, sines)
+    lane = lax.broadcasted_iota(jnp.int32, rotary.shape, 1)
+    high, low = position_parts(where)
+    tail = jnp.where(lane == 0, high, jnp.where(lane == 1, low, 0.0))
+    last = jnp.concatenate([rotary, tail], axis=1).astype(jnp.bfloat16)
+    for copy in range(out_ref.shape[0]):
+        out_ref[copy, :, :LATENT] = latents_ref[:, :LATENT]
+        out_ref[copy, :, LATENT:] = last
+
+
+def query_kernel(where_ref, frequency_ref, queries_ref, out_ref):
+    where, cosines, sines = turns(where_ref, frequency_ref)
+    lane = lax.broadcasted_iota(jnp.int32, sines.shape, 1)
+    high, low = position_parts(where)
+    tail = jnp.where(lane == 2, high, jnp.where(lane == 3, low, 0.0))
+    for h in range(queries_ref.shape[0]):
+        rotary = turned(queries_ref[h, :, LATENT:].astype(jnp.float32), cosines, sines)
+        out_ref[h, :, :LATENT] = queries_ref[h, :, :LATENT]
+        out_ref[h, :, LATENT:] = jnp.concatenate([rotary, tail], axis=1).astype(jnp.bfloat16)
+
+
+def prepare(kernel, positions, rows, copies):
+    half = np.exp(np.arange(ROPE // 2) * (-2.0 * math.log(10000.0) / ROPE))
+    frequency = jnp.asarray(np.concatenate([half, half])[None], jnp.float32)
+    return pl.pallas_call(
+        kernel,
+        out_shape=jax.ShapeDtypeStruct((copies, rows.shape[-2], WIDTH), jnp.bfloat16),
+        compiler_params=pltpu.CompilerParams(vmem_limit_bytes=VMEM),
+    )(positions.reshape(1, -1), frequency, rows)
 
 
 def shift_z(x, by):
@@ -117,7 +155,7 @@
             out_ref[side, 1, :, at] = spread[side * half : (side + 1) * half]
 
 
-def attend(ends, q, keys, carry=None, up=None, group=2):
+def attend(ends, q, keys, carry=None, up=None, group=2, weight=1):
     heads, toks, _ = q.shape
     first, last = carry is None, up is not None
     per_head = lambda width: pl.BlockSpec((group, toks, width), lambda i: (i, 0, 0))
@@ -148,117 +186,143 @@
         out_shape=out_shape,
         compiler_params=pltpu.CompilerParams(vmem_limit_bytes=VMEM),
         cost_estimate=pl.CostEstimate(
-            flops=2 * rows * count * (WIDTH + LATENT),
-            bytes_accessed=2 * count * WIDTH + rows * 4096,
-            transcendentals=rows * count,
+            flops=2 * weight * rows * count * (WIDTH + LATENT),
+            bytes_accessed=weight * (2 * count * WIDTH + rows * 4096),
+            transcendentals=weight * rows * count,
         ),
     )(*args)
 
 
-def project_kernel(near_ref, v_ref, w_ref, out_ref):
-    near = near_ref[0]
+def project_kernel(slots_ref, v_ref, w_ref, *refs):
+    out_ref = refs[-1]
+    core = slots_ref[1]
     part = lax.dot_general(v_ref[...], w_ref[0], NT, preferred_element_type=jnp.float32)
     toks = part.shape[0] // 2
     part = part.astype(jnp.bfloat16)
-    out_ref[0, near] = part[:toks]
-    out_ref[0, 1 - near] = part[toks:]
-
-
-def project(near, v, w):
+    out_ref[0, 0, core] = part[:toks]
+    out_ref[0, 0, 1 - core] = part[toks:]
+
+
+def project(near, core, v, w, into=None):
     blocks, cols, depth = w.shape
     toks = v.shape[0] // 2
+    in_specs = [
+        pl.BlockSpec(v.shape, lambda i, slots: (0, 0)),
+        pl.BlockSpec((1, cols, depth), lambda i, slots: (i, 0, 0)),
+    ]
+    args = [jnp.stack([near, core]), v, w]
+    if into is not None:
+        in_specs.append(pl.BlockSpec(memory_space=pl.ANY))
+        args.append(into)
     return pl.pallas_call(
         project_kernel,
-        grid=(blocks,),
-        in_specs=[
-            pl.BlockSpec(memory_space=pltpu.SMEM),
-            pl.BlockSpec(v.shape, lambda i: (0, 0)),
-            pl.BlockSpec((1, cols, depth), lambda i: (i, 0, 0)),
-        ],
-        out_specs=pl.BlockSpec((1, 2, toks, cols), lambda i: (i, 0, 0, 0)),
-        out_shape=jax.ShapeDtypeStruct((blocks, 2, toks, cols), jnp.bfloat16),
+        grid_spec=pltpu.PrefetchScalarGridSpec(
+            num_scalar_prefetch=1,
+            grid=(blocks,),
+            in_specs=in_specs,
+            out_specs=pl.BlockSpec(
+                (1, 1, 2, toks, cols), lambda i, slots: (i, slots[0], 0, 0, 0)
+            ),
+        ),
+        out_shape=jax.ShapeDtypeStruct((blocks, 2, 2, toks, cols), jnp.bfloat16),
+        input_output_aliases={} if into is None else {3: 0},
         compiler_params=pltpu.CompilerParams(vmem_limit_bytes=VMEM),
         cost_estimate=pl.CostEstimate(
             flops=4 * toks * blocks * cols * depth,
             bytes_accessed=2 * blocks * cols * depth,
             transcendentals=0,
         ),
-    )(near, v, w)
-
-
-def total_kernel(parts_ref, out_ref):
+    )(*args)
+
+
+def add_heads_kernel(parts_ref, out_ref):
     heads = parts_ref.shape[0]
     for near in range(2):
-        total = parts_ref[0, near].astype(jnp.float32)
-        for h in range(1, heads):
-            total += parts_ref[h, near].astype(jnp.float32)
+        total = []
+        for core in range(2):
+            t = parts_ref[0, near, core].astype(jnp.float32)
+            for h in range(1, heads):
+                t += parts_ref[h, near, core].astype(jnp.float32)
+            total.append(t.astype(out_ref.dtype))
         for far in range(2):
             at = far * 256 + near * 128
-            out_ref[:, at : at + 128] = total[:, far * 128 : far * 128 + 128].astype(out_ref.dtype)
+            lanes = slice(far * 64, far * 64 + 64)
+            out_ref[:, at : at + 128] = jnp.concatenate([t[:, lanes] for t in total], axis=1)
 
 
 def add_heads(parts):
-    _, _, toks, cols = parts.shape
-    return pl.pallas_call(
-        total_kernel,
-        out_shape=jax.ShapeDtypeStruct((toks, 2 * cols), jnp.bfloat16),
+    toks, cols = parts.shape[3:]
+    return pl.pallas_call(
+        add_heads_kernel,
+        out_shape=jax.ShapeDtypeStruct((toks, 4 * cols), parts.dtype),
         compiler_params=pltpu.CompilerParams(vmem_limit_bytes=VMEM),
     )(parts)
+
+
+def pair_kernel(far_ref, own_ref, other_ref, _, out_ref):
+    far = far_ref[0]
+    out_ref[0, far] = own_ref[...]
+    out_ref[0, 1 - far] = other_ref[...]
+
+
+def pair(far, own, other, earlier, copies):
+    corner = earlier.reshape(-1, earlier.shape[-1])
+    whole = pl.BlockSpec(own.shape, lambda i: (0, 0))
+    return pl.pallas_call(
+        pair_kernel,
+        grid=(copies,),
+        in_specs=[
+            pl.BlockSpec(memory_space=pltpu.SMEM),
+            whole,
+            whole,
+            pl.BlockSpec((16, 128), lambda i: (0, 0)),
+        ],
+        out_specs=pl.BlockSpec((1, 2) + own.shape, lambda i: (i, 0, 0, 0)),
+        out_shape=jax.ShapeDtypeStruct((copies, 2) + own.shape, own.dtype),
+    )(far, own, other, corner)
 
 
 def on_device(queries, latents, positions, lengths, value_up, out_weight):
     toks, heads, width = queries.shape
     ends = jnp.cumsum(lengths).astype(jnp.int32)
+    core = lax.axis_index("core").astype(jnp.int32)
+    far = lax.axis_index("zh_lat").astype(jnp.int32)
     near = lax.axis_index("zl_lat").astype(jnp.int32)
 
-    w = lax.all_gather(out_weight.T, ("y", "zh_lat", "core"), axis=0, tiled=True)
-    w = w.reshape(8, w.shape[0] // 8, w.shape[1])
-
-    parts = position_parts(positions)
-    zeros = lambda n: jnp.zeros((toks, n), jnp.bfloat16)
-    key_rows = jnp.concatenate(
-        [latents[:, :LATENT], rotate(latents[:, LATENT:], positions), parts, zeros(62)], axis=1
-    )
-    along_y = lax.all_to_all(
-        jnp.broadcast_to(key_rows[None], (8, toks, WIDTH)), "y", 0, 0
-    ).reshape(8 * toks, WIDTH)
-
-    tail = jnp.concatenate([zeros(2), parts, zeros(60)], axis=1)
-    q_own = jnp.concatenate(
-        [
-            queries[..., :LATENT],
-            rotate(queries[..., LATENT:], positions),
-            jnp.broadcast_to(tail[:, None, :], (toks, heads, 64)),
-        ],
-        axis=2,
-    ).transpose(1, 0, 2)
+    key_rows = prepare(key_kernel, positions, latents, 8)
+    along_y = lax.all_to_all(key_rows, "y", 0, 0).reshape(8 * toks, WIDTH)
+
+    q_own = prepare(query_kernel, positions, queries.transpose(1, 0, 2), heads)
     q = jnp.concatenate([q_own, swap(q_own, "core")], axis=1)
+
+    w = out_weight.T
+    w = pair(far.reshape(1), w, swap(w, "zh_lat"), q, 8)
+    w = lax.all_to_all(w, "y", 0, 0)
+    w = w.reshape(8, -1, w.shape[3])
 
     from_left = shift_z(along_y, 1)
     from_right = shift_z(along_y, -1)
-    carry = attend(ends, q, [along_y], group=8)
+    carry = attend(ends, q, [along_y], group=8, weight=8)
     middle = along_y.shape[0] // 2
     across_left = shift_z(from_left[:middle], 1)
     across_right = shift_z(from_right[middle:], -1)
-    carry = attend(ends, q, [from_left, from_right], carry, group=8)
+    carry = attend(ends, q, [from_left, from_right], carry, group=8, weight=8)
 
     both = attend(ends, q, [across_left, across_right], carry, value_up)
-    mine, theirs = both[0], swap(both[1], "core")
-    level = jnp.maximum(mine[1], theirs[1])
-    share_mine = jnp.exp2(mine[1] - level)
-    share_theirs = jnp.exp2(theirs[1] - level)
-    values = (
-        (mine[0] * share_mine + theirs[0] * share_theirs) / (share_mine + share_theirs)
-    ).astype(jnp.bfloat16)
-    v = jnp.concatenate([values, swap(values, "zl_lat")], axis=0)
-
-    partial = project(near.reshape(1), v, w)
-    rows = partial.shape[2]
-    cols = partial.shape[3]
+    theirs = swap(both, "core")
+    values = []
+    for side in range(2):
+        (part_a, level_a), (part_b, level_b) = both[side], theirs[1 - side]
+        level = jnp.maximum(level_a, level_b)
+        share_a, share_b = jnp.exp2(level_a - level), jnp.exp2(level_b - level)
+        values.append((part_a * share_a + part_b * share_b) / (share_a + share_b))
+    values = jnp.concatenate(values, axis=0).astype(jnp.bfloat16)
+    partial = project(near, core, values, w)
+    partial = project(1 - near, core, swap(values, "zl_lat"), w, partial)
     arrived = lax.all_to_all(
-        partial.reshape(16, rows, cols), ("z_hi", "x", "zl_lat"), 0, 0
-    ).reshape(8, 2, rows, cols)
-    return add_heads(arrived)
+        partial.reshape((32,) + partial.shape[3:]), ("z_hi", "x", "zl_lat", "core"), 0, 0
+    )
+    return add_heads(arrived.reshape(partial.shape))
 
 
 def solution(mesh):

time: 164 us -> 126 us (0.77)
  the two profiles are of different devices: /device:TPU:64 before, /device:TPU:72 now
where the time goes in v3:
time: 126 us
  starting transfers between devices  45.9 us (36%)
  blocking collectives  26.7 us (21%)
  Pallas kernels  25.9 us (21%)
  waiting for transfers between devices  18.9 us (15%)
  local copies, waits for them, and re-layouts  6.27 us (5%)
  other arithmetic  1.84 us (1%)
    all_to_all x1, blocking collectives, on_device(): lax.all_to_all(partial.reshape((32,) + partial.shape[3:]), ('z_hi', 'x',...  26.7 us
    ppermute x4, starting transfers between devices, shift_z(): return lax.ppermute(x, ('zh_lat', 'zl_lat', 'z_hi'), perm)  16.4 us
    ppermute x4, starting transfers between devices, swap(): return lax.ppermute(x, axis, [(0, 1), (1, 0)])  15.1 us
    pallas_call x3, Pallas kernels, attend(): pl.pallas_call(functools.partial(attend_kernel, len(keys), first, last),...  14.9 us
    ppermute x4, waiting for transfers between devices, swap(): return lax.ppermute(x, axis, [(0, 1), (1, 0)])  10.5 us
    ppermute x4, waiting for transfers between devices, shift_z(): return lax.ppermute(x, ('zh_lat', 'zl_lat', 'z_hi'), perm)  7.97 us
    all_to_all x1, starting transfers between devices, on_device(): along_y = lax.all_to_all(key_rows, 'y', 0, 0).reshape(8 * toks, WIDTH)  7.68 us
    all_to_all x1, starting transfers between devices, on_device(): w = lax.all_to_all(w, 'y', 0, 0)  6.76 us
  transfers between devices with their start and end apart: 10, of which 6 were waited for; matrix products, arithmetic and copies ran while one was open for 2% of the time, Pallas kernels for 17%

profile of v3, /device:TPU:72, one launch (start us, length us, event | category | flops | bytes accessed | tf_op | source)
XLA Modules:
  0.0 125.8 jit_solution(373834041690085648)
XLA Ops:
  2.2 1.1 shard_map.83
  3.3 7.7 %all-to-all-start = ((bf16[8,64,640]{2,1,0:T(8,128)(2,1)}), bf16[8,64,640]{2,1,0:T(8,128)(2,1)S(1)}, u32[]{:S(2)}, u32[]{:S(2)}) async-start(bf16[8,64,640]{2,1,0:T(8,128)(2,1)} %shard_map.83), calls=%async_computation | async-start | bytes 1310720 | tf_op jit(solution)/shard_map/all_to_all | solution.py:293
  11.4 1.9 %collective-permute-start = (bf16[8,64,640]{2,1,0:T(8,128)(2,1)S(1)}, bf16[8,64,640]{2,1,0:T(8,128)(2,1)S(1)}, u32[]{:S(2)}, u32[]{:S(2)}) collective-permute-start(bf16[8,64,640]{2,1,0:T(8,128)(2,1)S(1)} %shard_map.82), channel_id=1, source_target_pairs={{0,8},{8,0},{1,9},{9,1},{2,10},{10,2},{3,11},{11,3},{4,12},{12,4},... | collective-permute-start | bytes 1966088 | tf_op jit(solution)/shard_map/ppermute | solution.py:89
  13.4 6.1 %collective-permute-start.7 = (bf16[64,1024]{1,0:T(8,128)(2,1)S(1)}, bf16[64,1024]{1,0:T(8,128)(2,1)S(1)}, u32[]{:S(2)}, u32[]{:S(2)}) collective-permute-start(bf16[64,1024]{1,0:T(8,128)(2,1)S(1)} %bitcast.91), channel_id=1, source_target_pairs={{0,32},{32,0},{1,33},{33,1},{2,34},{34,2},{3,35},{35,3},{4,36},{36... | collective-permute-start | bytes 393224 | tf_op jit(solution)/shard_map/ppermute | solution.py:89
  19.6 1.2 pad_maximum_fusion.refs_1_
  20.9 3.9 %collective-permute-done.7.other_ref = bf16[64,1024]{1,0:T(8,128)(2,1)S(1)} collective-permute-done((bf16[64,1024]{1,0:T(8,128)(2,1)S(1)}, bf16[64,1024]{1,0:T(8,128)(2,1)S(1)}, u32[]{:S(2)}, u32[]{:S(2)}) %collective-permute-start.7) | collective-permute-done | bytes 131104 | tf_op jit(solution)/shard_map/ppermute | solution.py:89
  25.4 4.0 %shard_map.87 = bf16[8,2,64,1024]{3,2,1,0:T(8,128)(2,1)} custom-call(s32[1]{0:T(128)} %bitcast.15.far_ref, bf16[64,1024]{1,0:T(8,128)(2,1)} %bitcast.90, bf16[64,1024]{1,0:T(8,128)(2,1)} %copy-done.12, bf16[1024,640]{1,0:T(8,128)(2,1)} %bitcast.78), custom_call_target="tpu_custom_call" | custom-call | tf_op jit(solution)/shard_map/pallas_call | solution.py:271
  30.7 6.8 %all-to-all-start.1 = ((bf16[8,2,64,1024]{3,2,1,0:T(8,128)(2,1)}), bf16[8,2,64,1024]{3,2,1,0:T(8,128)(2,1)S(1)}, u32[]{:S(2)}, u32[]{:S(2)}) async-start(bf16[8,2,64,1024]{3,2,1,0:T(8,128)(2,1)} %shard_map.87), calls=%async_computation.1 | async-start | bytes 4194304 | tf_op jit(solution)/shard_map/all_to_all | solution.py:300
  37.5 2.5 %collective-permute-start.1 = (bf16[512,640]{1,0:T(8,128)(2,1)}, bf16[512,640]{1,0:T(8,128)(2,1)S(1)}, u32[]{:S(2)}, u32[]{:S(2)}) collective-permute-start(bf16[512,640]{1,0:T(8,128)(2,1)} %bitcast.82), channel_id=1, source_target_pairs={{0,16},{16,32},{32,48},{48,4},{4,20},{20,36},{36,52},{52,0},{1,17}... | collective-permute-start | bytes 1966088 | tf_op jit(solution)/shard_map/ppermute | solution.py:85
  39.9 3.4 %collective-permute-start.3 = (bf16[512,640]{1,0:T(8,128)(2,1)}, bf16[512,640]{1,0:T(8,128)(2,1)S(1)}, u32[]{:S(2)}, u32[]{:S(2)}) collective-permute-start(bf16[512,640]{1,0:T(8,128)(2,1)} %bitcast.83), channel_id=1, source_target_pairs={{0,52},{16,0},{32,16},{48,32},{4,48},{20,4},{36,20},{52,36},{1,53}... | collective-permute-start | bytes 1966088 | tf_op jit(solution)/shard_map/ppermute | solution.py:85
  44.4 2.3 %shard_map.84 = (f32[8,128,128]{2,1,0:T(8,128)S(1)}, f32[8,128,128]{2,1,0:T(8,128)S(1)}, f32[8,128,512]{2,1,0:T(8,128)S(1)}) custom-call(s32[8]{0:T(128)S(1)} %bitcast.87, bf16[8,128,640]{2,1,0:T(8,128)(2,1)S(1)} %copy-done, bf16[512,640]{1,0:T(8,128)(2,1)S(1)} %bitcast.84), custom_call_target="tpu_custom_call" | custom-call | flops 9663676416 | bytes 38797312 | tf_op jit(solution)/shard_map/pallas_call | solution.py:181
  46.8 1.3 %copy-done.9 = f32[8,128,512]{2,1,0:T(8,128)} copy-done((f32[8,128,512]{2,1,0:T(8,128)}, f32[8,128,512]{2,1,0:T(8,128)S(1)}, u32[]{:S(2)}) %copy-start.9) | copy-done | bytes 2097176
  48.1 7.6 %collective-permute-done.1.refs_2_ = bf16[512,640]{1,0:T(8,128)(2,1)S(1)} collective-permute-done((bf16[512,640]{1,0:T(8,128)(2,1)}, bf16[512,640]{1,0:T(8,128)(2,1)S(1)}, u32[]{:S(2)}, u32[]{:S(2)}) %collective-permute-start.1) | collective-permute-done | bytes 655392 | tf_op jit(solution)/shard_map/ppermute | solution.py:85
  55.7 3.5 %collective-permute-start.2 = (bf16[256,640]{1,0:T(8,128)(2,1)S(1)}, bf16[256,640]{1,0:T(8,128)(2,1)S(1)}, u32[]{:S(2)}, u32[]{:S(2)}) collective-permute-start(bf16[256,640]{1,0:T(8,128)(2,1)S(1)} %slice.28), channel_id=1, source_target_pairs={{0,16},{16,32},{32,48},{48,4},{4,20},{20,36},{36,52},{52,0},{1,17}... | collective-permute-start | bytes 983048 | tf_op jit(solution)/shard_map/ppermute | solution.py:85
  59.6 7.1 %collective-permute-start.4 = (bf16[256,640]{1,0:T(8,128)(2,1)S(1)}, bf16[256,640]{1,0:T(8,128)(2,1)S(1)}, u32[]{:S(2)}, u32[]{:S(2)}) collective-permute-start(bf16[256,640]{1,0:T(8,128)(2,1)S(1)} %slice.29), channel_id=1, source_target_pairs={{0,52},{16,0},{32,16},{48,32},{4,48},{20,4},{36,20},{52,36},{1,53}... | collective-permute-start | bytes 983048 | tf_op jit(solution)/shard_map/ppermute | solution.py:85
  66.7 7.0 %shard_map.85 = (f32[8,128,128]{2,1,0:T(8,128)S(1)}, f32[8,128,128]{2,1,0:T(8,128)S(1)}, f32[8,128,512]{2,1,0:T(8,128)}) custom-call(s32[8]{0:T(128)S(1)} %bitcast.88, bf16[8,128,640]{2,1,0:T(8,128)(2,1)S(1)} %copy-done, bf16[512,640]{1,0:T(8,128)(2,1)S(1)} %collective-permute-done.1.refs_2_, bf16[512,640]{1,0:T(8,128)(2,1)S(1)} %collective-permute-done.3.refs_3_, ...), custom_call_target="tpu_custom_call" | custom-call | flops 19327352832 | bytes 44040192 | tf_op jit(solution)/shard_map/pallas_call | solution.py:181
  73.7 5.5 %shard_map.86 = f32[2,2,64,1024]{3,2,1,0:T(8,128)S(1)} custom-call(s32[8]{0:T(128)S(1)} %bitcast.89, bf16[8,128,640]{2,1,0:T(8,128)(2,1)S(1)} %copy-done, bf16[256,640]{1,0:T(8,128)(2,1)S(1)} %collective-permute-done.2.refs_2_, bf16[256,640]{1,0:T(8,128)(2,1)S(1)} %collective-permute-done.4.refs_3_, f32[8,128,128]{2,1,0:T(8,128)S(1)} %get-tuple-element.14.refs_4_, ...), custom_call_target="tpu_custom_call" | custom-call | flops 1207959552 | bytes 4849664 | tf_op jit(solution)/shard_map/pallas_call | solution.py:181
  79.3 1.9 %collective-permute-start.5 = (f32[2,2,64,1024]{3,2,1,0:T(8,128)S(1)}, f32[2,2,64,1024]{3,2,1,0:T(8,128)S(1)}, u32[]{:S(2)}, u32[]{:S(2)}) collective-permute-start(f32[2,2,64,1024]{3,2,1,0:T(8,128)S(1)} %shard_map.86), channel_id=1, source_target_pairs={{0,8},{8,0},{1,9},{9,1},{2,10},{10,2},{3,11},{11,3},{4,12},{12,4},... | collective-permute-start | bytes 3145736 | tf_op jit(solution)/shard_map/ppermute | solution.py:89
  81.2 2.6 %collective-permute-done.5 = f32[2,2,64,1024]{3,2,1,0:T(8,128)S(1)} collective-permute-done((f32[2,2,64,1024]{3,2,1,0:T(8,128)S(1)}, f32[2,2,64,1024]{3,2,1,0:T(8,128)S(1)}, u32[]{:S(2)}, u32[]{:S(2)}) %collective-permute-start.5) | collective-permute-done | bytes 1048608 | tf_op jit(solution)/shard_map/ppermute | solution.py:89
  84.1 5.1 %collective-permute-start.6 = (bf16[128,1024]{1,0:T(8,128)(2,1)S(1)}, bf16[128,1024]{1,0:T(8,128)(2,1)S(1)}, u32[]{:S(2)}, u32[]{:S(2)}) collective-permute-start(bf16[128,1024]{1,0:T(8,128)(2,1)S(1)} %pad_maximum_fusion.1.v_ref), channel_id=1, source_target_pairs={{0,16},{16,0},{1,17},{17,1},{2,18},{18,2},{3,19},{19,3},{4,20},{20... | collective-permute-start | bytes 786440 | tf_op jit(solution)/shard_map/ppermute | solution.py:89
  89.4 2.5 %shard_map.88.refs_0_ = bf16[8,2,2,64,128]{4,3,2,1,0:T(8,128)(2,1)S(1)} custom-call(s32[2]{0:T(128)S(1)} %pad_add_fusion.1.slots_ref, bf16[128,1024]{1,0:T(8,128)(2,1)S(1)} %pad_maximum_fusion.1.v_ref, bf16[8,128,1024]{2,1,0:T(8,128)(2,1)S(1)} %bitcast.76), custom_call_target="tpu_custom_call" | custom-call | flops 268435456 | bytes 2097152 | tf_op jit(solution)/shard_map/pallas_call | solution.py:217
  91.9 4.0 %collective-permute-done.6.v_ref = bf16[128,1024]{1,0:T(8,128)(2,1)S(1)} collective-permute-done((bf16[128,1024]{1,0:T(8,128)(2,1)S(1)}, bf16[128,1024]{1,0:T(8,128)(2,1)S(1)}, u32[]{:S(2)}, u32[]{:S(2)}) %collective-permute-start.6) | collective-permute-done | bytes 262176 | tf_op jit(solution)/shard_map/ppermute | solution.py:89
  95.9 2.5 %shard_map.89 = bf16[8,2,2,64,128]{4,3,2,1,0:T(8,128)(2,1)S(1)} custom-call(s32[2]{0:T(128)S(1)} %pad_add_fusion.slots_ref, bf16[128,1024]{1,0:T(8,128)(2,1)S(1)} %collective-permute-done.6.v_ref, bf16[8,128,1024]{2,1,0:T(8,128)(2,1)S(1)} %bitcast.77, bf16[8,2,2,64,128]{4,3,2,1,0:T(8,128)(2,1)S(1)} %shard_map.88.refs_0_), custom_call_target="tpu_custom_call", output_to_operand_aliasing={{}: (3, {})} | custom-call | flops 268435456 | bytes 2097152 | tf_op jit(solution)/shard_map/pallas_call | solution.py:217
  98.3 26.7 %all_to_all.15 = bf16[32,64,128]{2,1,0:T(8,128)(2,1)S(1)} all-to-all(bf16[32,64,128]{2,1,0:T(8,128)(2,1)S(1)} %bitcast.79), channel_id=1, replica_groups=mesh['y'=8,'zh_lat'=2,'zl_lat'=2,'core'=2,'z_hi'=2,'x'=4] {'z_hi','x','z..., dimensions={0} | all-to-all | bytes 1048576 | tf_op jit(solution)/shard_map/all_to_all | solution.py:322
  (43 shorter events, 7.5 us)
Async XLA Ops:
  0.0 11.1 %copy-start.8 = (f32[1,64]{1,0:T(1,128)S(1)}, f32[1,64]{1,0:T(1,128)}, u32[]{:S(2)}) copy-start(f32[1,64]{1,0:T(1,128)} %constant.24.clone.frequency_ref) | copy-start | bytes 772
  0.0 11.1 %copy-start.6 = (s32[64]{0:T(128)S(1)}, s32[64]{0:T(128)}, u32[]{:S(2)}) copy-start(s32[64]{0:T(128)} %param.10) | copy-start | bytes 772
  0.0 0.9 copy-start.4
  0.9 0.7 copy-start.5
  1.6 0.7 copy-start.7
  2.2 8.8 %copy-start.10 = (bf16[64,8,576]{2,1,0:T(8,128)(2,1)S(1)}, bf16[64,8,576]{2,1,0:T(8,128)(2,1)}, u32[]{:S(2)}) copy-start(bf16[64,8,576]{2,1,0:T(8,128)(2,1)} %param.8) | copy-start | bytes 1769476
  3.3 10.0 %copy-start.11 = (bf16[1024,64]{0,1:T(8,128)(2,1)S(1)}, bf16[1024,64]{0,1:T(8,128)(2,1)}, u32[]{:S(2)}) copy-start(bf16[1024,64]{0,1:T(8,128)(2,1)} %param.13) | copy-start | bytes 393220
  3.3 16.1 %copy-start.13 = (s32[8]{0:T(128)S(1)}, s32[8]{0:T(128)}, u32[]{:S(2)}) copy-start(s32[8]{0:T(128)} %param.11) | copy-start | bytes 100
  3.3 26.5 %all-to-all-start = ((bf16[8,64,640]{2,1,0:T(8,128)(2,1)}), bf16[8,64,640]{2,1,0:T(8,128)(2,1)S(1)}, u32[]{:S(2)}, u32[]{:S(2)}) async-start(bf16[8,64,640]{2,1,0:T(8,128)(2,1)} %shard_map.83), calls=%async_computation | async-start | bytes 1310720 | tf_op jit(solution)/shard_map/all_to_all | solution.py:293
  11.4 8.2 %collective-permute-start = (bf16[8,64,640]{2,1,0:T(8,128)(2,1)S(1)}, bf16[8,64,640]{2,1,0:T(8,128)(2,1)S(1)}, u32[]{:S(2)}, u32[]{:S(2)}) collective-permute-start(bf16[8,64,640]{2,1,0:T(8,128)(2,1)S(1)} %shard_map.82), channel_id=1, source_target_pairs={{0,8},{8,0},{1,9},{9,1},{2,10},{10,2},{3,11},{11,3},{4,12},{12,4},... | collective-permute-start | bytes 1966088 | tf_op jit(solution)/shard_map/ppermute | solution.py:89
  13.4 11.4 %collective-permute-start.7 = (bf16[64,1024]{1,0:T(8,128)(2,1)S(1)}, bf16[64,1024]{1,0:T(8,128)(2,1)S(1)}, u32[]{:S(2)}, u32[]{:S(2)}) collective-permute-start(bf16[64,1024]{1,0:T(8,128)(2,1)S(1)} %bitcast.91), channel_id=1, source_target_pairs={{0,32},{32,0},{1,33},{33,1},{2,34},{34,2},{3,35},{35,3},{4,36},{36... | collective-permute-start | bytes 393224 | tf_op jit(solution)/shard_map/ppermute | solution.py:89
  24.8 0.7 copy-start.12
  29.4 13.9 %copy-start = (bf16[8,128,640]{2,1,0:T(8,128)(2,1)S(1)}, bf16[8,128,640]{2,1,0:T(8,128)(2,1)}, u32[]{:S(2)}) copy-start(bf16[8,128,640]{2,1,0:T(8,128)(2,1)} %pad_maximum_fusion.refs_1_) | copy-start | bytes 3932164
  29.8 0.9 copy-start.2
  30.7 58.7 %all-to-all-start.1 = ((bf16[8,2,64,1024]{3,2,1,0:T(8,128)(2,1)}), bf16[8,2,64,1024]{3,2,1,0:T(8,128)(2,1)S(1)}, u32[]{:S(2)}, u32[]{:S(2)}) async-start(bf16[8,2,64,1024]{3,2,1,0:T(8,128)(2,1)} %shard_map.87), calls=%async_computation.1 | async-start | bytes 4194304 | tf_op jit(solution)/shard_map/all_to_all | solution.py:300
  37.5 18.2 %collective-permute-start.1 = (bf16[512,640]{1,0:T(8,128)(2,1)}, bf16[512,640]{1,0:T(8,128)(2,1)S(1)}, u32[]{:S(2)}, u32[]{:S(2)}) collective-permute-start(bf16[512,640]{1,0:T(8,128)(2,1)} %bitcast.82), channel_id=1, source_target_pairs={{0,16},{16,32},{32,48},{48,4},{4,20},{20,36},{36,52},{52,0},{1,17}... | collective-permute-start | bytes 1966088 | tf_op jit(solution)/shard_map/ppermute | solution.py:85
  39.9 19.6 %collective-permute-start.3 = (bf16[512,640]{1,0:T(8,128)(2,1)}, bf16[512,640]{1,0:T(8,128)(2,1)S(1)}, u32[]{:S(2)}, u32[]{:S(2)}) collective-permute-start(bf16[512,640]{1,0:T(8,128)(2,1)} %bitcast.83), channel_id=1, source_target_pairs={{0,52},{16,0},{32,16},{48,32},{4,48},{20,4},{36,20},{52,36},{1,53}... | collective-permute-start | bytes 1966088 | tf_op jit(solution)/shard_map/ppermute | solution.py:85
  43.3 1.1 copy-start.3
  46.8 1.3 %copy-start.9 = (f32[8,128,512]{2,1,0:T(8,128)}, f32[8,128,512]{2,1,0:T(8,128)S(1)}, u32[]{:S(2)}) copy-start(f32[8,128,512]{2,1,0:T(8,128)S(1)} %get-tuple-element.13.refs_6_) | copy-start | bytes 6291460
  55.7 18.0 %collective-permute-start.2 = (bf16[256,640]{1,0:T(8,128)(2,1)S(1)}, bf16[256,640]{1,0:T(8,128)(2,1)S(1)}, u32[]{:S(2)}, u32[]{:S(2)}) collective-permute-start(bf16[256,640]{1,0:T(8,128)(2,1)S(1)} %slice.28), channel_id=1, source_target_pairs={{0,16},{16,32},{32,48},{48,4},{4,20},{20,36},{36,52},{52,0},{1,17}... | collective-permute-start | bytes 983048 | tf_op jit(solution)/shard_map/ppermute | solution.py:85
  59.6 14.2 %collective-permute-start.4 = (bf16[256,640]{1,0:T(8,128)(2,1)S(1)}, bf16[256,640]{1,0:T(8,128)(2,1)S(1)}, u32[]{:S(2)}, u32[]{:S(2)}) collective-permute-start(bf16[256,640]{1,0:T(8,128)(2,1)S(1)} %slice.29), channel_id=1, source_target_pairs={{0,52},{16,0},{32,16},{48,32},{4,48},{20,4},{36,20},{52,36},{1,53}... | collective-permute-start | bytes 983048 | tf_op jit(solution)/shard_map/ppermute | solution.py:85
  66.7 7.1 %copy-start.1 = (bf16[8,512,128]{2,1,0:T(8,128)(2,1)S(1)}, bf16[8,512,128]{2,1,0:T(8,128)(2,1)}, u32[]{:S(2)}) copy-start(bf16[8,512,128]{2,1,0:T(8,128)(2,1)} %refs_7_.1) | copy-start | bytes 3145732
  79.3 4.6 %collective-permute-start.5 = (f32[2,2,64,1024]{3,2,1,0:T(8,128)S(1)}, f32[2,2,64,1024]{3,2,1,0:T(8,128)S(1)}, u32[]{:S(2)}, u32[]{:S(2)}) collective-permute-start(f32[2,2,64,1024]{3,2,1,0:T(8,128)S(1)} %shard_map.86), channel_id=1, source_target_pairs={{0,8},{8,0},{1,9},{9,1},{2,10},{10,2},{3,11},{11,3},{4,12},{12,4},... | collective-permute-start | bytes 3145736 | tf_op jit(solution)/shard_map/ppermute | solution.py:89
  84.1 11.7 %collective-permute-start.6 = (bf16[128,1024]{1,0:T(8,128)(2,1)S(1)}, bf16[128,1024]{1,0:T(8,128)(2,1)S(1)}, u32[]{:S(2)}, u32[]{:S(2)}) collective-permute-start(bf16[128,1024]{1,0:T(8,128)(2,1)S(1)} %pad_maximum_fusion.1.v_ref), channel_id=1, source_target_pairs={{0,16},{16,0},{1,17},{17,1},{2,18},{18,2},{3,19},{19,3},{4,20},{20... | collective-permute-start | bytes 786440 | tf_op jit(solution)/shard_map/ppermute | solution.py:89

commit v4 on v3

v4 whole, which is shorter than its diff:
```python
import functools
import math

import jax
import jax.numpy as jnp
from jax import lax
from jax.experimental import pallas as pl
from jax.experimental.pallas import tpu as pltpu
from jax.sharding import Mesh, PartitionSpec as P

LATENT = 512
ROPE = 64
WIDTH = 640
SCALE = 192.0 ** (-0.5)
LOG2_SCALE = SCALE * math.log2(math.e)
HIDDEN = -1e30
VMEM = 48 * 1024 * 1024
NT = (((1,), (1,)), ((), ()))
WHOLE = pl.BlockSpec(memory_space=pltpu.VMEM)


def turns(where_ref):
    toks = where_ref.shape[1]
    row = lax.broadcasted_iota(jnp.int32, (toks, toks), 0)
    column = lax.broadcasted_iota(jnp.int32, (toks, toks), 1)
    spread = jnp.broadcast_to(where_ref[...], (toks, toks))
    where = jnp.sum(jnp.where(row == column, spread, 0).astype(jnp.float32), axis=1, keepdims=True)
    lane = lax.broadcasted_iota(jnp.int32, (toks, ROPE), 1)
    pair = (lane % (ROPE // 2)).astype(jnp.float32)
    angles = where * jnp.exp(pair * (-2.0 * math.log(10000.0) / ROPE))
    sines = jnp.sin(angles)
    return where, jnp.cos(angles), jnp.where(lane < ROPE // 2, -sines, sines)


def turned(rotary, cosines, sines):
    half = ROPE // 2
    other = jnp.concatenate([rotary[:, half:], rotary[:, :half]], axis=1)
    return rotary * cosines + other * sines


def position_parts(where):
    high = jnp.floor(where * (1.0 / 64.0))
    return high, where - 64.0 * high


def key_kernel(where_ref, latents_ref, out_ref):
    where, cosines, sines = turns(where_ref)
    rotary = turned(latents_ref[:, LATENT:].astype(jnp.float32), cosines, sines)
    lane = lax.broadcasted_iota(jnp.int32, rotary.shape, 1)
    high, low = position_parts(where)
    tail = jnp.where(lane == 0, high, jnp.where(lane == 1, low, 0.0))
    last = jnp.concatenate([rotary, tail], axis=1).astype(jnp.bfloat16)
    for copy in range(out_ref.shape[0]):
        out_ref[copy, :, :LATENT] = latents_ref[:, :LATENT]
        out_ref[copy, :, LATENT:] = last


def query_kernel(where_ref, queries_ref, out_ref):
    where, cosines, sines = turns(where_ref)
    lane = lax.broadcasted_iota(jnp.int32, sines.shape, 1)
    high, low = position_parts(where)
    tail = jnp.where(lane == 2, high, jnp.where(lane == 3, low, 0.0))
    for h in range(queries_ref.shape[0]):
        rotary = turned(queries_ref[h, :, LATENT:].astype(jnp.float32), cosines, sines)
        out_ref[h, :, :LATENT] = queries_ref[h, :, :LATENT]
        out_ref[h, :, LATENT:] = jnp.concatenate([rotary, tail], axis=1).astype(jnp.bfloat16)


def prepare(kernel, positions, rows, copies):
    return pl.pallas_call(
        kernel,
        in_specs=[WHOLE] * 2,
        out_specs=WHOLE,
        out_shape=jax.ShapeDtypeStruct((copies, rows.shape[-2], WIDTH), jnp.bfloat16),
        compiler_params=pltpu.CompilerParams(vmem_limit_bytes=VMEM),
    )(positions.reshape(1, -1), rows)


def shift_z(x):
    perm = []
    for z in range(8):
        for core in range(2):
            to = (z + 1 - 2 * core) % 8
            source = ((z % 4) * 2 + core) * 2 + z // 4
            target = ((to % 4) * 2 + core) * 2 + to // 4
            perm.append((source, target))
    return lax.ppermute(x, ("zh_lat", "zl_lat", "core", "z_hi"), perm)


def swap(x, axis):
    return lax.ppermute(x, axis, [(0, 1), (1, 0)])


def attend_kernel(group, first, last, ends_ref, q_ref, key_ref, up_ref, *refs):
    if not first:
        top_in, total_in, part_in = refs[:3]
        refs = refs[3:]
    if last:
        (out_ref,) = refs
    else:
        top_out, total_out, part_out = refs
    heads, toks, _ = q_ref.shape
    half = toks // 2
    meta = q_ref[0, :, LATENT:].astype(jnp.float32)
    query_pos = meta[:, 66:67] * 64.0 + meta[:, 67:68]
    query_start = jnp.zeros_like(query_pos)
    for k in range(8):
        end = ends_ref[k].astype(jnp.float32)
        query_start = jnp.where(query_pos >= end, end, query_start)
    first_end = ends_ref[0].astype(jnp.float32)
    lane = lax.broadcasted_iota(jnp.int32, (toks, 128), 1)
    pick = jnp.where(lane == 64, 64.0, jnp.where(lane == 65, 1.0, 0.0)).astype(jnp.bfloat16)
    key_pos = lax.dot_general(
        pick, key_ref[:, LATENT:], NT, preferred_element_type=jnp.float32
    )
    visible = (key_pos <= query_pos) & ((key_pos >= query_start) | (key_pos < first_end))
    count = key_ref.shape[0]
    rows = group * toks
    levels = jnp.zeros((toks, 128), jnp.float32)
    for at in range(0, heads, group):
        some = slice(at, at + group)
        raw = lax.dot_general(
            q_ref[some].reshape(rows, WIDTH), key_ref[...], NT, preferred_element_type=jnp.float32
        )
        raw = raw.reshape(group, toks, count)
        scores = jnp.where(visible[None], raw, HIDDEN).reshape(rows, count)
        wide = lambda column: jnp.broadcast_to(column, (rows, 128))
        top = wide(jnp.max(scores, axis=1, keepdims=True))
        if not first:
            old = top_in[some].reshape(rows, 128)
            top = jnp.maximum(top, old)
            fade = jnp.exp2((old - top) * LOG2_SCALE)
        weights = jnp.exp2((scores - jnp.concatenate([top] * (count // 128), axis=1)) * LOG2_SCALE)
        total = wide(jnp.sum(weights, axis=1, keepdims=True))
        if not first:
            total = total + fade * total_in[some].reshape(rows, 128)
        context = jnp.dot(
            weights.astype(jnp.bfloat16), key_ref[:, :LATENT], preferred_element_type=jnp.float32
        ).astype(jnp.bfloat16)
        if last:
            inverse = 1.0 / total
            level = top * LOG2_SCALE + jnp.log2(total)
            high = level.astype(jnp.bfloat16).astype(jnp.float32)
            middle = (level - high).astype(jnp.bfloat16).astype(jnp.float32)
            low = level - high - middle
        else:
            top_out[some] = top.reshape(group, toks, 128)
            total_out[some] = total.reshape(group, toks, 128)
        for h in range(group):
            mine = slice(h * toks, h * toks + toks)
            part = jnp.dot(context[mine], up_ref[at + h], preferred_element_type=jnp.float32)
            if not first:
                part = part + fade[mine] * part_in[at + h]
            if not last:
                part_out[at + h] = part
                continue
            part = (part * inverse[mine]).astype(jnp.bfloat16)
            lanes = slice((at + h) * 128, (at + h) * 128 + 128)
            for side in range(2):
                out_ref[side, :, lanes] = part[side * half : (side + 1) * half]
            for piece, value in enumerate((high, middle, low)):
                levels = jnp.where(lane == 3 * (at + h) + piece, value[mine], levels)
    if last:
        levels = levels.astype(jnp.bfloat16)
        for side in range(2):
            out_ref[side, :, heads * 128 :] = levels[side * half : (side + 1) * half]


def attend(ends, q, keys, up, carry=None, last=False, group=8, weight=1):
    heads, toks, _ = q.shape
    first = carry is None
    args = [ends, q, keys, up] + list(carry or ())
    if last:
        out_shape = jax.ShapeDtypeStruct((2, toks // 2, heads * 128 + 128), jnp.bfloat16)
    else:
        out_shape = [jax.ShapeDtypeStruct((heads, toks, 128), jnp.float32)] * 3
    rows, count = heads * toks, keys.shape[0]
    return pl.pallas_call(
        functools.partial(attend_kernel, group, first, last),
        in_specs=[pl.BlockSpec(memory_space=pltpu.SMEM)] + [WHOLE] * (len(args) - 1),
        out_specs=WHOLE if last else [WHOLE] * 3,
        out_shape=out_shape,
        compiler_params=pltpu.CompilerParams(vmem_limit_bytes=VMEM),
        cost_estimate=pl.CostEstimate(
            flops=2 * weight * rows * count * (WIDTH + LATENT),
            bytes_accessed=weight * (2 * count * WIDTH + rows * 4096),
            transcendentals=weight * rows * count,
        ),
    )(*args)


def merge_kernel(own_ref, other_ref, out_ref):
    _, toks, width = own_ref.shape
    wide = width - 128
    lane = lax.broadcasted_iota(jnp.int32, (128, wide), 0)
    head = lax.broadcasted_iota(jnp.int32, (128, wide), 1) // 128
    spread = ((lane >= 3 * head) & (lane < 3 * head + 3)).astype(jnp.float32).astype(jnp.bfloat16)
    for side in range(2):
        refs = (own_ref, side), (other_ref, 1 - side)
        own, other = [
            jnp.dot(r[s, :, wide:], spread, preferred_element_type=jnp.float32) for r, s in refs
        ]
        top = jnp.maximum(own, other)
        own, other = jnp.exp2(own - top), jnp.exp2(other - top)
        own_part, other_part = [r[s, :, :wide].astype(jnp.float32) for r, s in refs]
        out_ref[side * toks : (side + 1) * toks, :] = (
            (own_part * own + other_part * other) * (1.0 / (own + other))
        ).astype(out_ref.dtype)


def merge(own, other):
    _, toks, width = own.shape
    return pl.pallas_call(
        merge_kernel,
        in_specs=[WHOLE] * 2,
        out_specs=WHOLE,
        out_shape=jax.ShapeDtypeStruct((2 * toks, width - 128), own.dtype),
        compiler_params=pltpu.CompilerParams(vmem_limit_bytes=VMEM),
    )(own, other)


def project_kernel(slots_ref, v_ref, w_ref, *refs):
    out_ref = refs[-1]
    near, core = slots_ref[0], slots_ref[1]
    toks = v_ref.shape[0] // 2
    for y in range(w_ref.shape[0]):
        part = lax.dot_general(v_ref[...], w_ref[y], NT, preferred_element_type=jnp.float32)
        part = part.astype(jnp.bfloat16)
        out_ref[y, near, core] = part[:toks]
        out_ref[y, near, 1 - core] = part[toks:]


def project(near, core, v, w, into=None):
    blocks, cols, depth = w.shape
    toks = v.shape[0] // 2
    args = [jnp.stack([near, core]), v, w] + ([] if into is None else [into])
    return pl.pallas_call(
        project_kernel,
        in_specs=[pl.BlockSpec(memory_space=pltpu.SMEM)] + [WHOLE] * (len(args) - 1),
        out_specs=WHOLE,
        out_shape=jax.ShapeDtypeStruct((blocks, 2, 2, toks, cols), jnp.bfloat16),
        input_output_aliases={} if into is None else {3: 0},
        compiler_params=pltpu.CompilerParams(vmem_limit_bytes=VMEM),
        cost_estimate=pl.CostEstimate(
            flops=4 * toks * blocks * cols * depth,
            bytes_accessed=2 * blocks * cols * depth,
            transcendentals=0,
        ),
    )(*args)


def add_heads_kernel(parts_ref, out_ref):
    heads = parts_ref.shape[0]
    for near in range(2):
        total = []
        for core in range(2):
            t = parts_ref[0, near, core].astype(jnp.float32)
            for h in range(1, heads):
                t += parts_ref[h, near, core].astype(jnp.float32)
            total.append(t.astype(out_ref.dtype))
        for far in range(2):
            at = far * 256 + near * 128
            lanes = slice(far * 64, far * 64 + 64)
            out_ref[:, at : at + 128] = jnp.concatenate([t[:, lanes] for t in total], axis=1)


def add_heads(parts):
    toks, cols = parts.shape[3:]
    return pl.pallas_call(
        add_heads_kernel,
        in_specs=[WHOLE],
        out_specs=WHOLE,
        out_shape=jax.ShapeDtypeStruct((toks, 4 * cols), parts.dtype),
        compiler_params=pltpu.CompilerParams(vmem_limit_bytes=VMEM),
    )(parts)


def pair_kernel(far_ref, own_ref, other_ref, _, out_ref):
    far = far_ref[0]
    out_ref[0, far] = own_ref[...]
    out_ref[0, 1 - far] = other_ref[...]


def pair(far, own, other, earlier, copies):
    corner = earlier.reshape(-1, earlier.shape[-1])
    whole = pl.BlockSpec(own.shape, lambda i: (0, 0))
    return pl.pallas_call(
        pair_kernel,
        grid=(copies,),
        in_specs=[
            pl.BlockSpec(memory_space=pltpu.SMEM),
            whole,
            whole,
            pl.BlockSpec((16, 128), lambda i: (0, 0)),
        ],
        out_specs=pl.BlockSpec((1, 2) + own.shape, lambda i: (i, 0, 0, 0)),
        out_shape=jax.ShapeDtypeStruct((copies, 2) + own.shape, own.dtype),
    )(far, own, other, corner)


def on_device(queries, latents, positions, lengths, value_up, out_weight):
    toks, heads, width = queries.shape
    ends = jnp.cumsum(lengths).astype(jnp.int32)
    core = lax.axis_index("core").astype(jnp.int32)
    far = lax.axis_index("zh_lat").astype(jnp.int32)
    near = lax.axis_index("zl_lat").astype(jnp.int32)

    key_rows = prepare(key_kernel, positions, latents, 8)
    along_y = lax.all_to_all(key_rows, "y", 0, 0).reshape(8 * toks, WIDTH)

    q_own = prepare(query_kernel, positions, queries.transpose(1, 0, 2), heads)
    q = jnp.concatenate([q_own, swap(q_own, "core")], axis=1)

    w = out_weight.T
    w = pair(far.reshape(1), w, swap(w, "zh_lat"), q, 8)
    w = lax.all_to_all(w, "y", 0, 0)
    w = w.reshape(8, -1, w.shape[3])

    next_own = shift_z(along_y)
    next_other = shift_z(swap(along_y, "core"))
    beyond = shift_z(next_own)
    carry = attend(ends, q, along_y, value_up, weight=8)
    carry = attend(ends, q, next_own, value_up, carry, weight=8)
    carry = attend(ends, q, next_other, value_up, carry, weight=8)
    part = attend(ends, q, beyond, value_up, carry, last=True)

    values = merge(part, swap(part, "core"))

    partial = project(near, core, values, w)
    partial = project(1 - near, core, swap(values, "zl_lat"), w, partial)
    arrived = lax.all_to_all(
        partial.reshape((32,) + partial.shape[3:]), ("z_hi", "x", "zl_lat", "core"), 0, 0
    )
    return add_heads(arrived.reshape(partial.shape))


def solution(mesh):
    grid = Mesh(
        mesh.devices.reshape(8, 2, 2, 2, 2, 4), ("y", "zh_lat", "zl_lat", "core", "z_hi", "x")
    )
    seq, head = ("y", "zh_lat", "zl_lat", "core"), ("z_hi", "x")
    placed = (
        P(seq, head, None),
        P(seq, None),
        P(seq),
        P(),
        P(head, None, None),
        P(head, seq),
    )
    return jax.shard_map(
        on_device, mesh=grid, in_specs=placed, out_specs=P(seq, head), check_vma=False
    )
```

time: 126 us -> 122 us (0.968)
  the two profiles are of different devices: /device:TPU:72 before, /device:TPU:64 now
where the time goes in v4:
time: 122 us
  starting transfers between devices  43.7 us (36%)
  blocking collectives  30.1 us (25%)
  waiting for transfers between devices  21 us (17%)
  Pallas kernels  19.8 us (16%)
  local copies, waits for them, and re-layouts  5.46 us (4%)
  other arithmetic  1.51 us (1%)
    all_to_all x1, blocking collectives, on_device(): lax.all_to_all(partial.reshape((32,) + partial.shape[3:]), ('z_hi', 'x',...  30.1 us
    ppermute x5, starting transfers between devices, swap(): return lax.ppermute(x, axis, [(0, 1), (1, 0)])  17 us
    ppermute x3, starting transfers between devices, shift_z(): return lax.ppermute(x, ('zh_lat', 'zl_lat', 'core', 'z_hi'), perm)  14.1 us
    pallas_call x4, Pallas kernels, attend(): pl.pallas_call(functools.partial(attend_kernel, group, first, last), in_s...  10.7 us
    ppermute x3, waiting for transfers between devices, shift_z(): return lax.ppermute(x, ('zh_lat', 'zl_lat', 'core', 'z_hi'), perm)  8.2 us
    all_to_all x1, starting transfers between devices, on_device(): along_y = lax.all_to_all(key_rows, 'y', 0, 0).reshape(8 * toks, WIDTH)  7.23 us
    ppermute x5, waiting for transfers between devices, swap(): return lax.ppermute(x, axis, [(0, 1), (1, 0)])  6.28 us
    unnamed x25, local copies, waits for them, and re-layouts  5.46 us
  transfers between devices with their start and end apart: 10, of which 7 were waited for; matrix products, arithmetic and copies ran while one was open for 1% of the time, Pallas kernels for 14%

profile of v4, /device:TPU:64, one launch (start us, length us, event | category | flops | bytes accessed | tf_op | source)
XLA Modules:
  0.0 121.8 jit_solution(2017974660477480262)
XLA Ops:
  2.7 7.2 %all-to-all-start = ((bf16[8,64,640]{2,1,0:T(8,128)(2,1)}), bf16[8,64,640]{2,1,0:T(8,128)(2,1)S(1)}, u32[]{:S(2)}, u32[]{:S(2)}) async-start(bf16[8,64,640]{2,1,0:T(8,128)(2,1)} %shard_map.65), calls=%async_computation | async-start | bytes 1310720 | tf_op jit(solution)/shard_map/all_to_all | solution.py:309
  10.3 1.9 %collective-permute-start = (bf16[8,64,640]{2,1,0:T(8,128)(2,1)S(1)}, bf16[8,64,640]{2,1,0:T(8,128)(2,1)S(1)}, u32[]{:S(2)}, u32[]{:S(2)}) collective-permute-start(bf16[8,64,640]{2,1,0:T(8,128)(2,1)S(1)} %shard_map.64), channel_id=1, source_target_pairs={{0,8},{8,0},{1,9},{9,1},{2,10},{10,2},{3,11},{11,3},{4,12},{12,4},... | collective-permute-start | bytes 1966088 | tf_op jit(solution)/shard_map/ppermute | solution.py:91
  12.2 6.1 %collective-permute-start.7 = (bf16[64,1024]{1,0:T(8,128)(2,1)S(1)}, bf16[64,1024]{1,0:T(8,128)(2,1)S(1)}, u32[]{:S(2)}, u32[]{:S(2)}) collective-permute-start(bf16[64,1024]{1,0:T(8,128)(2,1)S(1)} %bitcast.32), channel_id=1, source_target_pairs={{0,32},{32,0},{1,33},{33,1},{2,34},{34,2},{3,35},{35,3},{4,36},{36... | collective-permute-start | bytes 393224 | tf_op jit(solution)/shard_map/ppermute | solution.py:91
  19.5 4.1 %collective-permute-done.7.other_ref = bf16[64,1024]{1,0:T(8,128)(2,1)S(1)} collective-permute-done((bf16[64,1024]{1,0:T(8,128)(2,1)S(1)}, bf16[64,1024]{1,0:T(8,128)(2,1)S(1)}, u32[]{:S(2)}, u32[]{:S(2)}) %collective-permute-start.7) | collective-permute-done | bytes 131104 | tf_op jit(solution)/shard_map/ppermute | solution.py:91
  24.3 4.0 %shard_map.71 = bf16[8,2,64,1024]{3,2,1,0:T(8,128)(2,1)} custom-call(s32[1]{0:T(128)} %bitcast.7.far_ref, bf16[64,1024]{1,0:T(8,128)(2,1)} %bitcast.31, bf16[64,1024]{1,0:T(8,128)(2,1)} %copy-done.10, bf16[1024,640]{1,0:T(8,128)(2,1)} %bitcast.18), custom_call_target="tpu_custom_call" | custom-call | tf_op jit(solution)/shard_map/pallas_call | solution.py:287
  28.3 1.9 %all-to-all-done = bf16[8,64,640]{2,1,0:T(8,128)(2,1)S(1)} async-done(((bf16[8,64,640]{2,1,0:T(8,128)(2,1)}), bf16[8,64,640]{2,1,0:T(8,128)(2,1)S(1)}, u32[]{:S(2)}, u32[]{:S(2)}) %all-to-all-start) | async-done | bytes 655392 | tf_op jit(solution)/shard_map/all_to_all | solution.py:309
  31.0 5.3 %all-to-all-start.1 = ((bf16[8,2,64,1024]{3,2,1,0:T(8,128)(2,1)}), bf16[8,2,64,1024]{3,2,1,0:T(8,128)(2,1)S(1)}, u32[]{:S(2)}, u32[]{:S(2)}) async-start(bf16[8,2,64,1024]{3,2,1,0:T(8,128)(2,1)} %shard_map.71), calls=%async_computation.1 | async-start | bytes 4194304 | tf_op jit(solution)/shard_map/all_to_all | solution.py:316
  36.5 2.6 %collective-permute-start.1 = (bf16[512,640]{1,0:T(8,128)(2,1)}, bf16[512,640]{1,0:T(8,128)(2,1)S(1)}, u32[]{:S(2)}, u32[]{:S(2)}) collective-permute-start(bf16[512,640]{1,0:T(8,128)(2,1)} %bitcast.22), channel_id=1, source_target_pairs={{0,16},{8,60},{16,32},{24,8},{32,48},{40,24},{48,4},{56,40},{4,20}... | collective-permute-start | bytes 1966088 | tf_op jit(solution)/shard_map/ppermute | solution.py:87
  39.1 1.9 %collective-permute-start.3 = (bf16[512,640]{1,0:T(8,128)(2,1)}, bf16[512,640]{1,0:T(8,128)(2,1)S(1)}, u32[]{:S(2)}, u32[]{:S(2)}) collective-permute-start(bf16[512,640]{1,0:T(8,128)(2,1)} %bitcast.23), channel_id=1, source_target_pairs={{0,8},{8,0},{1,9},{9,1},{2,10},{10,2},{3,11},{11,3},{4,12},{12,4},... | collective-permute-start | bytes 1966088 | tf_op jit(solution)/shard_map/ppermute | solution.py:91
  43.4 2.6 %shard_map.66 = (f32[8,128,128]{2,1,0:T(8,128)S(1)}, f32[8,128,128]{2,1,0:T(8,128)S(1)}, f32[8,128,128]{2,1,0:T(8,128)S(1)}) custom-call(s32[8]{0:T(128)S(1)} %bitcast.27, bf16[8,128,640]{2,1,0:T(8,128)(2,1)S(1)} %copy-done, bf16[512,640]{1,0:T(8,128)(2,1)S(1)} %bitcast.24, bf16[8,512,128]{2,1,0:T(8,128)(2,1)S(1)} %copy-done.1), custom_call_target="tpu_custom_call" | custom-call | flops 9663676416 | bytes 38797312 | tf_op jit(solution)/shard_map/pallas_call | solution.py:178
  46.0 5.1 %collective-permute-start.4 = (bf16[512,640]{1,0:T(8,128)(2,1)S(1)}, bf16[512,640]{1,0:T(8,128)(2,1)S(1)}, u32[]{:S(2)}, u32[]{:S(2)}) collective-permute-start(bf16[512,640]{1,0:T(8,128)(2,1)S(1)} %collective-permute-done.3), channel_id=1, source_target_pairs={{0,16},{8,60},{16,32},{24,8},{32,48},{40,24},{48,4},{56,40},{4,20}... | collective-permute-start | bytes 1966088 | tf_op jit(solution)/shard_map/ppermute | solution.py:87
  51.2 6.4 %collective-permute-start.2 = (bf16[512,640]{1,0:T(8,128)(2,1)S(1)}, bf16[512,640]{1,0:T(8,128)(2,1)S(1)}, u32[]{:S(2)}, u32[]{:S(2)}) collective-permute-start(bf16[512,640]{1,0:T(8,128)(2,1)S(1)} %collective-permute-done.1.key_ref), channel_id=1, source_target_pairs={{0,16},{8,60},{16,32},{24,8},{32,48},{40,24},{48,4},{56,40},{4,20}... | collective-permute-start | bytes 1966088 | tf_op jit(solution)/shard_map/ppermute | solution.py:87
  57.6 2.6 %shard_map.67 = (f32[8,128,128]{2,1,0:T(8,128)S(1)}, f32[8,128,128]{2,1,0:T(8,128)S(1)}, f32[8,128,128]{2,1,0:T(8,128)S(1)}) custom-call(s32[8]{0:T(128)S(1)} %bitcast.28, bf16[8,128,640]{2,1,0:T(8,128)(2,1)S(1)} %copy-done, bf16[512,640]{1,0:T(8,128)(2,1)S(1)} %collective-permute-done.1.key_ref, bf16[8,512,128]{2,1,0:T(8,128)(2,1)S(1)} %copy-done.2, ...), custom_call_target="tpu_custom_call" | custom-call | flops 9663676416 | bytes 38797312 | tf_op jit(solution)/shard_map/pallas_call | solution.py:178
  60.2 3.8 %collective-permute-done.4.key_ref = bf16[512,640]{1,0:T(8,128)(2,1)S(1)} collective-permute-done((bf16[512,640]{1,0:T(8,128)(2,1)S(1)}, bf16[512,640]{1,0:T(8,128)(2,1)S(1)}, u32[]{:S(2)}, u32[]{:S(2)}) %collective-permute-start.4) | collective-permute-done | bytes 655392 | tf_op jit(solution)/shard_map/ppermute | solution.py:87
  64.1 2.6 %shard_map.68 = (f32[8,128,128]{2,1,0:T(8,128)S(1)}, f32[8,128,128]{2,1,0:T(8,128)S(1)}, f32[8,128,128]{2,1,0:T(8,128)S(1)}) custom-call(s32[8]{0:T(128)S(1)} %bitcast.29, bf16[8,128,640]{2,1,0:T(8,128)(2,1)S(1)} %copy-done, bf16[512,640]{1,0:T(8,128)(2,1)S(1)} %collective-permute-done.4.key_ref, bf16[8,512,128]{2,1,0:T(8,128)(2,1)S(1)} %copy-done.2, ...), custom_call_target="tpu_custom_call" | custom-call | flops 9663676416 | bytes 38797312 | tf_op jit(solution)/shard_map/pallas_call | solution.py:178
  66.7 4.4 %collective-permute-done.2.key_ref = bf16[512,640]{1,0:T(8,128)(2,1)S(1)} collective-permute-done((bf16[512,640]{1,0:T(8,128)(2,1)S(1)}, bf16[512,640]{1,0:T(8,128)(2,1)S(1)}, u32[]{:S(2)}, u32[]{:S(2)}) %collective-permute-start.2) | collective-permute-done | bytes 655392 | tf_op jit(solution)/shard_map/ppermute | solution.py:87
  71.1 2.8 %shard_map.69.own_ref = bf16[2,64,1152]{2,1,0:T(8,128)(2,1)S(1)} custom-call(s32[8]{0:T(128)S(1)} %bitcast.30, bf16[8,128,640]{2,1,0:T(8,128)(2,1)S(1)} %copy-done, bf16[512,640]{1,0:T(8,128)(2,1)S(1)} %collective-permute-done.2.key_ref, bf16[8,512,128]{2,1,0:T(8,128)(2,1)S(1)} %copy-done.2, f32[8,128,128]{2,1,0:T(8,128)S(1)} %get-tuple-element.20.refs_0_, ...), custom_call_target="tpu_custom_call" | custom-call | flops 1207959552 | bytes 4849664 | tf_op jit(solution)/shard_map/pallas_call | solution.py:178
  73.9 1.9 %collective-permute-start.5 = (bf16[2,64,1152]{2,1,0:T(8,128)(2,1)S(1)}, bf16[2,64,1152]{2,1,0:T(8,128)(2,1)S(1)}, u32[]{:S(2)}, u32[]{:S(2)}) collective-permute-start(bf16[2,64,1152]{2,1,0:T(8,128)(2,1)S(1)} %shard_map.69.own_ref), channel_id=1, source_target_pairs={{0,8},{8,0},{1,9},{9,1},{2,10},{10,2},{3,11},{11,3},{4,12},{12,4},... | collective-permute-start | bytes 884744 | tf_op jit(solution)/shard_map/ppermute | solution.py:91
  75.8 1.5 %collective-permute-done.5.other_ref = bf16[2,64,1152]{2,1,0:T(8,128)(2,1)S(1)} collective-permute-done((bf16[2,64,1152]{2,1,0:T(8,128)(2,1)S(1)}, bf16[2,64,1152]{2,1,0:T(8,128)(2,1)S(1)}, u32[]{:S(2)}, u32[]{:S(2)}) %collective-permute-start.5) | collective-permute-done | bytes 294944 | tf_op jit(solution)/shard_map/ppermute | solution.py:91
  77.9 5.1 %collective-permute-start.6 = (bf16[128,1024]{1,0:T(8,128)(2,1)S(1)}, bf16[128,1024]{1,0:T(8,128)(2,1)S(1)}, u32[]{:S(2)}, u32[]{:S(2)}) collective-permute-start(bf16[128,1024]{1,0:T(8,128)(2,1)S(1)} %shard_map.70.v_ref), channel_id=1, source_target_pairs={{0,16},{16,0},{1,17},{17,1},{2,18},{18,2},{3,19},{19,3},{4,20},{20... | collective-permute-start | bytes 786440 | tf_op jit(solution)/shard_map/ppermute | solution.py:91
  83.2 4.6 %all-to-all-done.1 = bf16[8,2,64,1024]{3,2,1,0:T(8,128)(2,1)S(1)} async-done(((bf16[8,2,64,1024]{3,2,1,0:T(8,128)(2,1)}), bf16[8,2,64,1024]{3,2,1,0:T(8,128)(2,1)S(1)}, u32[]{:S(2)}, u32[]{:S(2)}) %all-to-all-start.1) | async-done | bytes 2097184 | tf_op jit(solution)/shard_map/all_to_all | solution.py:316
  87.8 1.2 %shard_map.72.refs_0_ = bf16[8,2,2,64,128]{4,3,2,1,0:T(8,128)(2,1)S(1)} custom-call(s32[2]{0:T(128)S(1)} %pad_add_fusion.1.slots_ref, bf16[128,1024]{1,0:T(8,128)(2,1)S(1)} %shard_map.70.v_ref, bf16[8,128,1024]{2,1,0:T(8,128)(2,1)S(1)} %bitcast.16), custom_call_target="tpu_custom_call" | custom-call | flops 268435456 | bytes 2097152 | tf_op jit(solution)/shard_map/pallas_call | solution.py:237
  89.6 1.2 %shard_map.73 = bf16[8,2,2,64,128]{4,3,2,1,0:T(8,128)(2,1)S(1)} custom-call(s32[2]{0:T(128)S(1)} %pad_add_fusion.slots_ref, bf16[128,1024]{1,0:T(8,128)(2,1)S(1)} %collective-permute-done.6.v_ref, bf16[8,128,1024]{2,1,0:T(8,128)(2,1)S(1)} %bitcast.17, bf16[8,2,2,64,128]{4,3,2,1,0:T(8,128)(2,1)S(1)} %shard_map.72.refs_0_), custom_call_target="tpu_custom_call", output_to_operand_aliasing={{}: (3, {})} | custom-call | flops 268435456 | bytes 2097152 | tf_op jit(solution)/shard_map/pallas_call | solution.py:237
  90.9 30.1 %all_to_all.15 = bf16[32,64,128]{2,1,0:T(8,128)(2,1)S(1)} all-to-all(bf16[32,64,128]{2,1,0:T(8,128)(2,1)S(1)} %bitcast.19), channel_id=1, replica_groups=mesh['y'=8,'zh_lat'=2,'zl_lat'=2,'core'=2,'z_hi'=2,'x'=4] {'z_hi','x','z..., dimensions={0} | all-to-all | bytes 1048576 | tf_op jit(solution)/shard_map/all_to_all | solution.py:331
  (37 shorter events, 10.3 us)
Async XLA Ops:
  0.0 10.0 %copy-start.7 = (s32[64]{0:T(128)S(1)}, s32[64]{0:T(128)}, u32[]{:S(2)}) copy-start(s32[64]{0:T(128)} %param.8) | copy-start | bytes 772
  0.0 0.9 copy-start.5
  0.9 0.7 copy-start.6
  1.6 8.3 %copy-start.8 = (bf16[64,8,576]{2,1,0:T(8,128)(2,1)S(1)}, bf16[64,8,576]{2,1,0:T(8,128)(2,1)}, u32[]{:S(2)}) copy-start(bf16[64,8,576]{2,1,0:T(8,128)(2,1)} %param.6) | copy-start | bytes 1769476
  2.7 9.6 %copy-start.9 = (bf16[1024,64]{0,1:T(8,128)(2,1)S(1)}, bf16[1024,64]{0,1:T(8,128)(2,1)}, u32[]{:S(2)}) copy-start(bf16[1024,64]{0,1:T(8,128)(2,1)} %param.11) | copy-start | bytes 393220
  2.7 27.5 %all-to-all-start = ((bf16[8,64,640]{2,1,0:T(8,128)(2,1)}), bf16[8,64,640]{2,1,0:T(8,128)(2,1)S(1)}, u32[]{:S(2)}, u32[]{:S(2)}) async-start(bf16[8,64,640]{2,1,0:T(8,128)(2,1)} %shard_map.65), calls=%async_computation | async-start | bytes 1310720 | tf_op jit(solution)/shard_map/all_to_all | solution.py:309
  10.3 8.0 %collective-permute-start = (bf16[8,64,640]{2,1,0:T(8,128)(2,1)S(1)}, bf16[8,64,640]{2,1,0:T(8,128)(2,1)S(1)}, u32[]{:S(2)}, u32[]{:S(2)}) collective-permute-start(bf16[8,64,640]{2,1,0:T(8,128)(2,1)S(1)} %shard_map.64), channel_id=1, source_target_pairs={{0,8},{8,0},{1,9},{9,1},{2,10},{10,2},{3,11},{11,3},{4,12},{12,4},... | collective-permute-start | bytes 1966088 | tf_op jit(solution)/shard_map/ppermute | solution.py:91
  12.2 11.4 %collective-permute-start.7 = (bf16[64,1024]{1,0:T(8,128)(2,1)S(1)}, bf16[64,1024]{1,0:T(8,128)(2,1)S(1)}, u32[]{:S(2)}, u32[]{:S(2)}) collective-permute-start(bf16[64,1024]{1,0:T(8,128)(2,1)S(1)} %bitcast.32), channel_id=1, source_target_pairs={{0,32},{32,0},{1,33},{33,1},{2,34},{34,2},{3,35},{35,3},{4,36},{36... | collective-permute-start | bytes 393224 | tf_op jit(solution)/shard_map/ppermute | solution.py:91
  23.7 0.7 copy-start.10
  28.3 8.1 %copy-start.11 = (s32[8]{0:T(128)S(1)}, s32[8]{0:T(128)}, u32[]{:S(2)}) copy-start(s32[8]{0:T(128)} %param.9) | copy-start | bytes 100
  28.3 12.8 %copy-start = (bf16[8,128,640]{2,1,0:T(8,128)(2,1)S(1)}, bf16[8,128,640]{2,1,0:T(8,128)(2,1)}, u32[]{:S(2)}) copy-start(bf16[8,128,640]{2,1,0:T(8,128)(2,1)} %pad_maximum_fusion.q_ref) | copy-start | bytes 3932164
  30.2 0.8 copy-start.3
  31.0 56.7 %all-to-all-start.1 = ((bf16[8,2,64,1024]{3,2,1,0:T(8,128)(2,1)}), bf16[8,2,64,1024]{3,2,1,0:T(8,128)(2,1)S(1)}, u32[]{:S(2)}, u32[]{:S(2)}) async-start(bf16[8,2,64,1024]{3,2,1,0:T(8,128)(2,1)} %shard_map.71), calls=%async_computation.1 | async-start | bytes 4194304 | tf_op jit(solution)/shard_map/all_to_all | solution.py:316
  36.5 14.6 %collective-permute-start.1 = (bf16[512,640]{1,0:T(8,128)(2,1)}, bf16[512,640]{1,0:T(8,128)(2,1)S(1)}, u32[]{:S(2)}, u32[]{:S(2)}) collective-permute-start(bf16[512,640]{1,0:T(8,128)(2,1)} %bitcast.22), channel_id=1, source_target_pairs={{0,16},{8,60},{16,32},{24,8},{32,48},{40,24},{48,4},{56,40},{4,20}... | collective-permute-start | bytes 1966088 | tf_op jit(solution)/shard_map/ppermute | solution.py:87
  39.1 6.9 %collective-permute-start.3 = (bf16[512,640]{1,0:T(8,128)(2,1)}, bf16[512,640]{1,0:T(8,128)(2,1)S(1)}, u32[]{:S(2)}, u32[]{:S(2)}) collective-permute-start(bf16[512,640]{1,0:T(8,128)(2,1)} %bitcast.23), channel_id=1, source_target_pairs={{0,8},{8,0},{1,9},{9,1},{2,10},{10,2},{3,11},{11,3},{4,12},{12,4},... | collective-permute-start | bytes 1966088 | tf_op jit(solution)/shard_map/ppermute | solution.py:91
  41.1 1.2 %copy-start.1 = (bf16[8,512,128]{2,1,0:T(8,128)(2,1)S(1)}, bf16[8,512,128]{2,1,0:T(8,128)(2,1)}, u32[]{:S(2)}) copy-start(bf16[8,512,128]{2,1,0:T(8,128)(2,1)} %up_ref.7) | copy-start | bytes 3145732
  42.3 1.1 copy-start.4
  43.4 14.2 %copy-start.2 = (bf16[8,512,128]{2,1,0:T(8,128)(2,1)S(1)}, bf16[8,512,128]{2,1,0:T(8,128)(2,1)}, u32[]{:S(2)}) copy-start(bf16[8,512,128]{2,1,0:T(8,128)(2,1)} %up_ref.7) | copy-start | bytes 3145732
  46.0 18.0 %collective-permute-start.4 = (bf16[512,640]{1,0:T(8,128)(2,1)S(1)}, bf16[512,640]{1,0:T(8,128)(2,1)S(1)}, u32[]{:S(2)}, u32[]{:S(2)}) collective-permute-start(bf16[512,640]{1,0:T(8,128)(2,1)S(1)} %collective-permute-done.3), channel_id=1, source_target_pairs={{0,16},{8,60},{16,32},{24,8},{32,48},{40,24},{48,4},{56,40},{4,20}... | collective-permute-start | bytes 1966088 | tf_op jit(solution)/shard_map/ppermute | solution.py:87
  51.2 19.9 %collective-permute-start.2 = (bf16[512,640]{1,0:T(8,128)(2,1)S(1)}, bf16[512,640]{1,0:T(8,128)(2,1)S(1)}, u32[]{:S(2)}, u32[]{:S(2)}) collective-permute-start(bf16[512,640]{1,0:T(8,128)(2,1)S(1)} %collective-permute-done.1.key_ref), channel_id=1, source_target_pairs={{0,16},{8,60},{16,32},{24,8},{32,48},{40,24},{48,4},{56,40},{4,20}... | collective-permute-start | bytes 1966088 | tf_op jit(solution)/shard_map/ppermute | solution.py:87
  73.9 3.5 %collective-permute-start.5 = (bf16[2,64,1152]{2,1,0:T(8,128)(2,1)S(1)}, bf16[2,64,1152]{2,1,0:T(8,128)(2,1)S(1)}, u32[]{:S(2)}, u32[]{:S(2)}) collective-permute-start(bf16[2,64,1152]{2,1,0:T(8,128)(2,1)S(1)} %shard_map.69.own_ref), channel_id=1, source_target_pairs={{0,8},{8,0},{1,9},{9,1},{2,10},{10,2},{3,11},{11,3},{4,12},{12,4},... | collective-permute-start | bytes 884744 | tf_op jit(solution)/shard_map/ppermute | solution.py:91
  77.9 11.7 %collective-permute-start.6 = (bf16[128,1024]{1,0:T(8,128)(2,1)S(1)}, bf16[128,1024]{1,0:T(8,128)(2,1)S(1)}, u32[]{:S(2)}, u32[]{:S(2)}) collective-permute-start(bf16[128,1024]{1,0:T(8,128)(2,1)S(1)} %shard_map.70.v_ref), channel_id=1, source_target_pairs={{0,16},{16,0},{1,17},{17,1},{2,18},{18,2},{3,19},{19,3},{4,20},{20... | collective-permute-start | bytes 786440 | tf_op jit(solution)/shard_map/ppermute | solution.py:91

commit v5 on v4

--- a/solution.py
+++ b/solution.py
@@ -17,6 +17,7 @@
 VMEM = 48 * 1024 * 1024
 NT = (((1,), (1,)), ((), ()))
 WHOLE = pl.BlockSpec(memory_space=pltpu.VMEM)
+ANYWHERE = pl.BlockSpec(memory_space=pl.ANY)
 
 
 def turns(where_ref):
@@ -43,16 +44,49 @@
     return high, where - 64.0 * high
 
 
-def key_kernel(where_ref, latents_ref, out_ref):
+def key_kernel(where_hbm, latents_hbm, out_hbm, where_ref, latents_ref, rows_ref, in_sems, out_sems):
+    arrivals = [
+        pltpu.make_async_copy(where_hbm, where_ref, in_sems.at[0]),
+        pltpu.make_async_copy(latents_hbm, latents_ref, in_sems.at[1]),
+    ]
+    for arrival in arrivals:
+        arrival.start()
+    for arrival in arrivals:
+        arrival.wait()
     where, cosines, sines = turns(where_ref)
     rotary = turned(latents_ref[:, LATENT:].astype(jnp.float32), cosines, sines)
     lane = lax.broadcasted_iota(jnp.int32, rotary.shape, 1)
     high, low = position_parts(where)
     tail = jnp.where(lane == 0, high, jnp.where(lane == 1, low, 0.0))
-    last = jnp.concatenate([rotary, tail], axis=1).astype(jnp.bfloat16)
-    for copy in range(out_ref.shape[0]):
-        out_ref[copy, :, :LATENT] = latents_ref[:, :LATENT]
-        out_ref[copy, :, LATENT:] = last
+    rows_ref[:, :LATENT] = latents_ref[:, :LATENT]
+    rows_ref[:, LATENT:] = jnp.concatenate([rotary, tail], axis=1).astype(jnp.bfloat16)
+    send_copies(rows_ref, out_hbm, out_sems)
+
+
+def send_copies(ref, out_hbm, sems):
+    copies = [pltpu.make_async_copy(ref, out_hbm.at[i], sems.at[i]) for i in range(out_hbm.shape[0])]
+    for copy in copies:
+        copy.start()
+    for copy in copies:
+        copy.wait()
+
+
+def prepare_keys(positions, latents, copies):
+    toks, width = latents.shape
+    return pl.pallas_call(
+        key_kernel,
+        in_specs=[pl.BlockSpec(memory_space=pltpu.HBM)] * 2,
+        out_specs=ANYWHERE,
+        out_shape=jax.ShapeDtypeStruct((copies, toks, WIDTH), latents.dtype),
+        scratch_shapes=[
+            pltpu.VMEM((1, toks), jnp.int32),
+            pltpu.VMEM((toks, width), latents.dtype),
+            pltpu.VMEM((toks, WIDTH), latents.dtype),
+            pltpu.SemaphoreType.DMA((2,)),
+            pltpu.SemaphoreType.DMA((copies,)),
+        ],
+        compiler_params=pltpu.CompilerParams(vmem_limit_bytes=VMEM),
+    )(positions.reshape(1, -1), latents)
 
 
 def query_kernel(where_ref, queries_ref, out_ref):
@@ -66,14 +100,15 @@
         out_ref[h, :, LATENT:] = jnp.concatenate([rotary, tail], axis=1).astype(jnp.bfloat16)
 
 
-def prepare(kernel, positions, rows, copies):
-    return pl.pallas_call(
-        kernel,
+def prepare_queries(positions, queries):
+    heads, toks, _ = queries.shape
+    return pl.pallas_call(
+        query_kernel,
         in_specs=[WHOLE] * 2,
         out_specs=WHOLE,
-        out_shape=jax.ShapeDtypeStruct((copies, rows.shape[-2], WIDTH), jnp.bfloat16),
-        compiler_params=pltpu.CompilerParams(vmem_limit_bytes=VMEM),
-    )(positions.reshape(1, -1), rows)
+        out_shape=jax.ShapeDtypeStruct((heads, toks, WIDTH), queries.dtype),
+        compiler_params=pltpu.CompilerParams(vmem_limit_bytes=VMEM),
+    )(positions.reshape(1, -1), queries)
 
 
 def shift_z(x):
@@ -219,82 +254,100 @@
     )(own, other)
 
 
-def project_kernel(slots_ref, v_ref, w_ref, *refs):
-    out_ref = refs[-1]
+def project_kernel(slots_ref, v_ref, w_ref, out_ref):
     near, core = slots_ref[0], slots_ref[1]
-    toks = v_ref.shape[0] // 2
+    toks = v_ref.shape[0] // 4
     for y in range(w_ref.shape[0]):
         part = lax.dot_general(v_ref[...], w_ref[y], NT, preferred_element_type=jnp.float32)
         part = part.astype(jnp.bfloat16)
-        out_ref[y, near, core] = part[:toks]
-        out_ref[y, near, 1 - core] = part[toks:]
-
-
-def project(near, core, v, w, into=None):
+        for k in range(4):
+            at_near = near if k < 2 else 1 - near
+            at_core = core if k % 2 == 0 else 1 - core
+            out_ref[at_near, y, at_core] = part[k * toks : (k + 1) * toks]
+
+
+def project(near, core, v, w):
     blocks, cols, depth = w.shape
-    toks = v.shape[0] // 2
-    args = [jnp.stack([near, core]), v, w] + ([] if into is None else [into])
+    toks = v.shape[0] // 4
     return pl.pallas_call(
         project_kernel,
-        in_specs=[pl.BlockSpec(memory_space=pltpu.SMEM)] + [WHOLE] * (len(args) - 1),
+        in_specs=[pl.BlockSpec(memory_space=pltpu.SMEM)] + [WHOLE] * 2,
         out_specs=WHOLE,
-        out_shape=jax.ShapeDtypeStruct((blocks, 2, 2, toks, cols), jnp.bfloat16),
-        input_output_aliases={} if into is None else {3: 0},
+        out_shape=jax.ShapeDtypeStruct((2, blocks, 2, toks, cols), jnp.bfloat16),
         compiler_params=pltpu.CompilerParams(vmem_limit_bytes=VMEM),
         cost_estimate=pl.CostEstimate(
-            flops=4 * toks * blocks * cols * depth,
+            flops=8 * toks * blocks * cols * depth,
             bytes_accessed=2 * blocks * cols * depth,
             transcendentals=0,
         ),
-    )(*args)
-
-
-def add_heads_kernel(parts_ref, out_ref):
-    heads = parts_ref.shape[0]
+    )(jnp.stack([near, core]), v, w)
+
+
+def add_heads_kernel(core_ref, parts_ref, keep_ref, give_ref):
+    core = core_ref[0]
     for near in range(2):
-        total = []
-        for core in range(2):
-            t = parts_ref[0, near, core].astype(jnp.float32)
-            for h in range(1, heads):
-                t += parts_ref[h, near, core].astype(jnp.float32)
-            total.append(t.astype(out_ref.dtype))
+        for whose, out_ref in ((core, keep_ref), (1 - core, give_ref)):
+            total = parts_ref[near, 0, whose].astype(jnp.float32)
+            for h in range(1, parts_ref.shape[1]):
+                total += parts_ref[near, h, whose].astype(jnp.float32)
+            out_ref[near] = total.astype(out_ref.dtype)
+
+
+def add_heads(core, parts):
+    half = jax.ShapeDtypeStruct((2,) + parts.shape[3:], parts.dtype)
+    return pl.pallas_call(
+        add_heads_kernel,
+        in_specs=[pl.BlockSpec(memory_space=pltpu.SMEM), WHOLE],
+        out_specs=[WHOLE] * 2,
+        out_shape=[half] * 2,
+        compiler_params=pltpu.CompilerParams(vmem_limit_bytes=VMEM),
+    )(core, parts)
+
+
+def lay_out_kernel(core_ref, own_ref, other_ref, out_ref):
+    first = core_ref[0] == 0
+    for near in range(2):
+        own, other = own_ref[near], other_ref[near]
         for far in range(2):
+            lanes = slice(far * 64, far * 64 + 64)
             at = far * 256 + near * 128
-            lanes = slice(far * 64, far * 64 + 64)
-            out_ref[:, at : at + 128] = jnp.concatenate([t[:, lanes] for t in total], axis=1)
-
-
-def add_heads(parts):
-    toks, cols = parts.shape[3:]
-    return pl.pallas_call(
-        add_heads_kernel,
-        in_specs=[WHOLE],
+            out_ref[:, at : at + 128] = jnp.where(
+                first,
+                jnp.concatenate([own[:, lanes], other[:, lanes]], axis=1),
+                jnp.concatenate([other[:, lanes], own[:, lanes]], axis=1),
+            )
+
+
+def lay_out(core, own, other):
+    _, toks, cols = own.shape
+    return pl.pallas_call(
+        lay_out_kernel,
+        in_specs=[pl.BlockSpec(memory_space=pltpu.SMEM)] + [WHOLE] * 2,
         out_specs=WHOLE,
-        out_shape=jax.ShapeDtypeStruct((toks, 4 * cols), parts.dtype),
-        compiler_params=pltpu.CompilerParams(vmem_limit_bytes=VMEM),
-    )(parts)
-
-
-def pair_kernel(far_ref, own_ref, other_ref, _, out_ref):
+        out_shape=jax.ShapeDtypeStruct((toks, 4 * cols), own.dtype),
+        compiler_params=pltpu.CompilerParams(vmem_limit_bytes=VMEM),
+    )(core, own, other)
+
+
+def pair_kernel(far_ref, own_ref, other_ref, _, out_hbm, both_ref, sems):
     far = far_ref[0]
-    out_ref[0, far] = own_ref[...]
-    out_ref[0, 1 - far] = other_ref[...]
+    both_ref[far] = own_ref[...]
+    both_ref[1 - far] = other_ref[...]
+    send_copies(both_ref, out_hbm, sems)
 
 
 def pair(far, own, other, earlier, copies):
-    corner = earlier.reshape(-1, earlier.shape[-1])
-    whole = pl.BlockSpec(own.shape, lambda i: (0, 0))
+    corner = earlier.reshape(-1, earlier.shape[-1])[:16, :128]
     return pl.pallas_call(
         pair_kernel,
-        grid=(copies,),
-        in_specs=[
-            pl.BlockSpec(memory_space=pltpu.SMEM),
-            whole,
-            whole,
-            pl.BlockSpec((16, 128), lambda i: (0, 0)),
+        in_specs=[pl.BlockSpec(memory_space=pltpu.SMEM)] + [WHOLE] * 3,
+        out_specs=ANYWHERE,
+        out_shape=jax.ShapeDtypeStruct((copies, 2) + own.shape, own.dtype),
+        scratch_shapes=[
+            pltpu.VMEM((2,) + own.shape, own.dtype),
+            pltpu.SemaphoreType.DMA((copies,)),
         ],
-        out_specs=pl.BlockSpec((1, 2) + own.shape, lambda i: (i, 0, 0, 0)),
-        out_shape=jax.ShapeDtypeStruct((copies, 2) + own.shape, own.dtype),
+        compiler_params=pltpu.CompilerParams(vmem_limit_bytes=VMEM),
     )(far, own, other, corner)
 
 
@@ -305,10 +358,10 @@
     far = lax.axis_index("zh_lat").astype(jnp.int32)
     near = lax.axis_index("zl_lat").astype(jnp.int32)
 
-    key_rows = prepare(key_kernel, positions, latents, 8)
+    key_rows = prepare_keys(positions, latents, 8)
     along_y = lax.all_to_all(key_rows, "y", 0, 0).reshape(8 * toks, WIDTH)
 
-    q_own = prepare(query_kernel, positions, queries.transpose(1, 0, 2), heads)
+    q_own = prepare_queries(positions, queries.transpose(1, 0, 2))
     q = jnp.concatenate([q_own, swap(q_own, "core")], axis=1)
 
     w = out_weight.T
@@ -319,19 +372,21 @@
     next_own = shift_z(along_y)
     next_other = shift_z(swap(along_y, "core"))
     beyond = shift_z(next_own)
-    carry = attend(ends, q, along_y, value_up, weight=8)
-    carry = attend(ends, q, next_own, value_up, carry, weight=8)
-    carry = attend(ends, q, next_other, value_up, carry, weight=8)
+    carry = attend(ends, q, along_y, value_up, weight=3)
+    carry = attend(ends, q, next_own, value_up, carry, weight=3)
+    carry = attend(ends, q, next_other, value_up, carry, weight=3)
     part = attend(ends, q, beyond, value_up, carry, last=True)
 
     values = merge(part, swap(part, "core"))
 
-    partial = project(near, core, values, w)
-    partial = project(1 - near, core, swap(values, "zl_lat"), w, partial)
+    v = jnp.concatenate([values, swap(values, "zl_lat")], axis=0)
+
+    partial = project(near, core, v, w)
     arrived = lax.all_to_all(
-        partial.reshape((32,) + partial.shape[3:]), ("z_hi", "x", "zl_lat", "core"), 0, 0
+        partial.reshape((16,) + partial.shape[2:]), ("zl_lat", "z_hi", "x"), 0, 0
     )
-    return add_heads(arrived.reshape(partial.shape))
+    keep, give = add_heads(core.reshape(1), arrived.reshape(partial.shape))
+    return lay_out(core.reshape(1), keep, swap(give, "core"))
 
 
 def solution(mesh):

time: 122 us -> 121 us (level)
  the two profiles are of different devices: /device:TPU:64 before, /device:TPU:73 now
where the time goes in v5:
time: 121 us; the launch traced here: 120 us
  starting transfers between devices  57 us (47%)
  blocking collectives  23.9 us (20%)
  Pallas kernels  18 us (15%)
  waiting for transfers between devices  16.1 us (13%)
  local copies, waits for them, and re-layouts  4.42 us (4%)
    ppermute x6, starting transfers between devices, swap(): return lax.ppermute(x, axis, [(0, 1), (1, 0)])  27.9 us
    all_to_all x1, blocking collectives, on_device(): lax.all_to_all(partial.reshape((16,) + partial.shape[2:]), ('zl_lat', 'z_...  23.9 us
    ppermute x3, starting transfers between devices, shift_z(): return lax.ppermute(x, ('zh_lat', 'zl_lat', 'core', 'z_hi'), perm)  15.1 us
    ppermute x6, waiting for transfers between devices, swap(): return lax.ppermute(x, axis, [(0, 1), (1, 0)])  13.3 us
    pallas_call x4, Pallas kernels, attend(): pl.pallas_call(functools.partial(attend_kernel, group, first, last), in_s...  11.9 us
    all_to_all x1, starting transfers between devices, on_device(): along_y = lax.all_to_all(key_rows, 'y', 0, 0).reshape(8 * toks, WIDTH)  7.13 us
    all_to_all x1, starting transfers between devices, on_device(): w = lax.all_to_all(w, 'y', 0, 0)  6.85 us
    unnamed x21, local copies, waits for them, and re-layouts  4.42 us
  transfers between devices with their start and end apart: 11, of which 5 were waited for; matrix products, arithmetic and copies ran while one was open for 0% of the time, Pallas kernels for 12%

profile of v5, /device:TPU:73, one launch (start us, length us, event | category | flops | bytes accessed | tf_op | source)
XLA Modules:
  0.0 120.2 jit_solution(16577110590845969286)
XLA Ops:
  1.6 1.2 %shard_map.65 = bf16[8,64,640]{2,1,0:T(8,128)(2,1)} custom-call(s32[1,64]{1,0:T(1,128)S(1)} %bitcast.22, bf16[64,576]{1,0:T(8,128)(2,1)S(1)} %copy-done.5), custom_call_target="tpu_custom_call" | custom-call | tf_op jit(solution)/shard_map/pallas_call | solution.py:76
  2.8 7.1 %all-to-all-start = ((bf16[8,64,640]{2,1,0:T(8,128)(2,1)}), bf16[8,64,640]{2,1,0:T(8,128)(2,1)}, u32[]{:S(2)}, u32[]{:S(2)}) async-start(bf16[8,64,640]{2,1,0:T(8,128)(2,1)} %shard_map.65), calls=%async_computation | async-start | bytes 1310720 | tf_op jit(solution)/shard_map/all_to_all | solution.py:362
  10.4 3.1 %collective-permute-start = (bf16[8,64,640]{2,1,0:T(8,128)(2,1)S(1)}, bf16[8,64,640]{2,1,0:T(8,128)(2,1)S(1)}, u32[]{:S(2)}, u32[]{:S(2)}) collective-permute-start(bf16[8,64,640]{2,1,0:T(8,128)(2,1)S(1)} %shard_map.64), channel_id=1, source_target_pairs={{0,8},{8,0},{1,9},{9,1},{2,10},{10,2},{3,11},{11,3},{4,12},{12,4},... | collective-permute-start | bytes 1966088 | tf_op jit(solution)/shard_map/ppermute | solution.py:126
  13.5 5.8 %collective-permute-start.7 = (bf16[64,1024]{1,0:T(8,128)(2,1)S(1)}, bf16[64,1024]{1,0:T(8,128)(2,1)S(1)}, u32[]{:S(2)}, u32[]{:S(2)}) collective-permute-start(bf16[64,1024]{1,0:T(8,128)(2,1)S(1)} %bitcast.20), channel_id=1, source_target_pairs={{0,32},{32,0},{1,33},{33,1},{2,34},{34,2},{3,35},{35,3},{4,36},{36... | collective-permute-start | bytes 393224 | tf_op jit(solution)/shard_map/ppermute | solution.py:126
  19.5 5.0 %collective-permute-done.7.other_ref = bf16[64,1024]{1,0:T(8,128)(2,1)S(1)} collective-permute-done((bf16[64,1024]{1,0:T(8,128)(2,1)S(1)}, bf16[64,1024]{1,0:T(8,128)(2,1)S(1)}, u32[]{:S(2)}, u32[]{:S(2)}) %collective-permute-start.7) | collective-permute-done | bytes 131104 | tf_op jit(solution)/shard_map/ppermute | solution.py:126
  26.0 1.4 %shard_map.71 = bf16[8,2,64,1024]{3,2,1,0:T(8,128)(2,1)} custom-call(s32[1]{0:T(128)} %bitcast.7.far_ref, bf16[64,1024]{1,0:T(8,128)(2,1)S(1)} %bitcast.21, bf16[64,1024]{1,0:T(8,128)(2,1)S(1)} %copy-done.4, bf16[16,128]{1,0:T(8,128)(2,1)S(1)} %slice.4._), custom_call_target="tpu_custom_call" | custom-call | tf_op jit(solution)/shard_map/pallas_call | solution.py:341
  27.5 6.8 %all-to-all-start.1 = ((bf16[8,2,64,1024]{3,2,1,0:T(8,128)(2,1)}), bf16[8,2,64,1024]{3,2,1,0:T(8,128)(2,1)S(1)}, u32[]{:S(2)}, u32[]{:S(2)}) async-start(bf16[8,2,64,1024]{3,2,1,0:T(8,128)(2,1)} %shard_map.71), calls=%async_computation.1 | async-start | bytes 4194304 | tf_op jit(solution)/shard_map/all_to_all | solution.py:369
  34.3 2.7 %collective-permute-start.3 = (bf16[512,640]{1,0:T(8,128)(2,1)}, bf16[512,640]{1,0:T(8,128)(2,1)}, u32[]{:S(2)}, u32[]{:S(2)}) collective-permute-start(bf16[512,640]{1,0:T(8,128)(2,1)} %bitcast.6.key_ref), channel_id=1, source_target_pairs={{0,8},{8,0},{1,9},{9,1},{2,10},{10,2},{3,11},{11,3},{4,12},{12,4},... | collective-permute-start | bytes 1966088 | tf_op jit(solution)/shard_map/ppermute | solution.py:126
  37.1 3.7 %collective-permute-start.1 = (bf16[512,640]{1,0:T(8,128)(2,1)}, bf16[512,640]{1,0:T(8,128)(2,1)}, u32[]{:S(2)}, u32[]{:S(2)}) collective-permute-start(bf16[512,640]{1,0:T(8,128)(2,1)} %bitcast.6.key_ref), channel_id=1, source_target_pairs={{0,16},{8,60},{16,32},{24,8},{32,48},{40,24},{48,4},{56,40},{4,20}... | collective-permute-start | bytes 1966088 | tf_op jit(solution)/shard_map/ppermute | solution.py:122
  41.0 8.3 %collective-permute-start.4 = (bf16[512,640]{1,0:T(8,128)(2,1)}, bf16[512,640]{1,0:T(8,128)(2,1)S(1)}, u32[]{:S(2)}, u32[]{:S(2)}) collective-permute-start(bf16[512,640]{1,0:T(8,128)(2,1)} %collective-permute-done.3), channel_id=1, source_target_pairs={{0,16},{8,60},{16,32},{24,8},{32,48},{40,24},{48,4},{56,40},{4,20}... | collective-permute-start | bytes 1966088 | tf_op jit(solution)/shard_map/ppermute | solution.py:122
  49.3 1.2 %copy-done = bf16[8,512,128]{2,1,0:T(8,128)(2,1)S(1)} copy-done((bf16[8,512,128]{2,1,0:T(8,128)(2,1)S(1)}, bf16[8,512,128]{2,1,0:T(8,128)(2,1)}, u32[]{:S(2)}) %copy-start) | copy-done | bytes 1048600
  50.5 3.2 %shard_map.66 = (f32[8,128,128]{2,1,0:T(8,128)S(1)}, f32[8,128,128]{2,1,0:T(8,128)S(1)}, f32[8,128,128]{2,1,0:T(8,128)S(1)}) custom-call(s32[8]{0:T(128)S(1)} %bitcast.24, bf16[8,128,640]{2,1,0:T(8,128)(2,1)S(1)} %pad_maximum_fusion.q_ref, bf16[512,640]{1,0:T(8,128)(2,1)} %bitcast.6.key_ref, bf16[8,512,128]{2,1,0:T(8,128)(2,1)S(1)} %copy-done), custom_call_target="tpu_custom_call" | custom-call | flops 3623878656 | bytes 14548992 | tf_op jit(solution)/shard_map/pallas_call | solution.py:213
  53.8 3.1 %collective-permute-start.2 = (bf16[512,640]{1,0:T(8,128)(2,1)}, bf16[512,640]{1,0:T(8,128)(2,1)S(1)}, u32[]{:S(2)}, u32[]{:S(2)}) collective-permute-start(bf16[512,640]{1,0:T(8,128)(2,1)} %collective-permute-done.1.key_ref), channel_id=1, source_target_pairs={{0,16},{8,60},{16,32},{24,8},{32,48},{40,24},{48,4},{56,40},{4,20}... | collective-permute-start | bytes 1966088 | tf_op jit(solution)/shard_map/ppermute | solution.py:122
  56.9 3.2 %shard_map.67 = (f32[8,128,128]{2,1,0:T(8,128)S(1)}, f32[8,128,128]{2,1,0:T(8,128)S(1)}, f32[8,128,128]{2,1,0:T(8,128)S(1)}) custom-call(s32[8]{0:T(128)S(1)} %bitcast.25, bf16[8,128,640]{2,1,0:T(8,128)(2,1)S(1)} %pad_maximum_fusion.q_ref, bf16[512,640]{1,0:T(8,128)(2,1)} %collective-permute-done.1.key_ref, bf16[8,512,128]{2,1,0:T(8,128)(2,1)S(1)} %copy-done.1, ...), custom_call_target="tpu_custom_call" | custom-call | flops 3623878656 | bytes 14548992 | tf_op jit(solution)/shard_map/pallas_call | solution.py:213
  60.2 2.7 %shard_map.68 = (f32[8,128,128]{2,1,0:T(8,128)S(1)}, f32[8,128,128]{2,1,0:T(8,128)S(1)}, f32[8,128,128]{2,1,0:T(8,128)S(1)}) custom-call(s32[8]{0:T(128)S(1)} %bitcast.26, bf16[8,128,640]{2,1,0:T(8,128)(2,1)S(1)} %pad_maximum_fusion.q_ref, bf16[512,640]{1,0:T(8,128)(2,1)S(1)} %collective-permute-done.4.key_ref, bf16[8,512,128]{2,1,0:T(8,128)(2,1)S(1)} %copy-done.1, ...), custom_call_target="tpu_custom_call" | custom-call | flops 3623878656 | bytes 14548992 | tf_op jit(solution)/shard_map/pallas_call | solution.py:213
  62.9 2.8 %collective-permute-done.2.key_ref = bf16[512,640]{1,0:T(8,128)(2,1)S(1)} collective-permute-done((bf16[512,640]{1,0:T(8,128)(2,1)}, bf16[512,640]{1,0:T(8,128)(2,1)S(1)}, u32[]{:S(2)}, u32[]{:S(2)}) %collective-permute-start.2) | collective-permute-done | bytes 655392 | tf_op jit(solution)/shard_map/ppermute | solution.py:122
  65.6 2.8 %shard_map.69.own_ref = bf16[2,64,1152]{2,1,0:T(8,128)(2,1)S(1)} custom-call(s32[8]{0:T(128)S(1)} %bitcast.27, bf16[8,128,640]{2,1,0:T(8,128)(2,1)S(1)} %pad_maximum_fusion.q_ref, bf16[512,640]{1,0:T(8,128)(2,1)S(1)} %collective-permute-done.2.key_ref, bf16[8,512,128]{2,1,0:T(8,128)(2,1)S(1)} %copy-done.1, f32[8,128,128]{2,1,0:T(8,128)S(1)} %get-tuple-element.22.refs_0_, ...), custom_call_target="tpu_custom_call" | custom-call | flops 1207959552 | bytes 4849664 | tf_op jit(solution)/shard_map/pallas_call | solution.py:213
  68.4 3.6 %collective-permute-start.5 = (bf16[2,64,1152]{2,1,0:T(8,128)(2,1)S(1)}, bf16[2,64,1152]{2,1,0:T(8,128)(2,1)S(1)}, u32[]{:S(2)}, u32[]{:S(2)}) collective-permute-start(bf16[2,64,1152]{2,1,0:T(8,128)(2,1)S(1)} %shard_map.69.own_ref), channel_id=1, source_target_pairs={{0,8},{8,0},{1,9},{9,1},{2,10},{10,2},{3,11},{11,3},{4,12},{12,4},... | collective-permute-start | bytes 884744 | tf_op jit(solution)/shard_map/ppermute | solution.py:126
  72.0 1.2 collective-permute-done.5.other_ref
  73.7 4.9 %collective-permute-start.6 = (bf16[128,1024]{1,0:T(8,128)(2,1)S(1)}, bf16[128,1024]{1,0:T(8,128)(2,1)S(1)}, u32[]{:S(2)}, u32[]{:S(2)}) collective-permute-start(bf16[128,1024]{1,0:T(8,128)(2,1)S(1)} %shard_map.70), channel_id=1, source_target_pairs={{0,16},{16,0},{1,17},{17,1},{2,18},{18,2},{3,19},{19,3},{4,20},{20... | collective-permute-start | bytes 786440 | tf_op jit(solution)/shard_map/ppermute | solution.py:126
  78.7 6.3 %collective-permute-done.6 = bf16[128,1024]{1,0:T(8,128)(2,1)S(1)} collective-permute-done((bf16[128,1024]{1,0:T(8,128)(2,1)S(1)}, bf16[128,1024]{1,0:T(8,128)(2,1)S(1)}, u32[]{:S(2)}, u32[]{:S(2)}) %collective-permute-start.6) | collective-permute-done | bytes 262176 | tf_op jit(solution)/shard_map/ppermute | solution.py:126
  85.1 1.8 %shard_map.72 = bf16[2,8,2,64,128]{4,3,2,1,0:T(8,128)(2,1)S(1)} custom-call(s32[2]{0:T(128)S(1)} %pad_add_fusion.slots_ref, bf16[256,1024]{1,0:T(8,128)(2,1)S(1)} %pad_maximum_fusion.1.v_ref, bf16[8,128,1024]{2,1,0:T(8,128)(2,1)S(1)} %bitcast.15), custom_call_target="tpu_custom_call" | custom-call | flops 536870912 | bytes 2097152 | tf_op jit(solution)/shard_map/pallas_call | solution.py:272
  86.9 23.9 %all_to_all.15 = bf16[16,2,64,128]{3,2,1,0:T(8,128)(2,1)S(1)} all-to-all(bf16[16,2,64,128]{3,2,1,0:T(8,128)(2,1)S(1)} %bitcast.19), channel_id=1, replica_groups=mesh['y'=8,'zh_lat'=2,'zl_lat'=2,'core'=2,'z_hi'=2,'x'=4] {'zl_lat','z_h..., dimensions={0} | all-to-all | bytes 1048576 | tf_op jit(solution)/shard_map/all_to_all | solution.py:385
  110.9 7.7 %collective-permute-start.8 = (bf16[2,64,128]{2,1,0:T(8,128)(2,1)S(1)}, bf16[2,64,128]{2,1,0:T(8,128)(2,1)S(1)}, u32[]{:S(2)}, u32[]{:S(2)}) collective-permute-start(bf16[2,64,128]{2,1,0:T(8,128)(2,1)S(1)} %get-tuple-element.26), channel_id=1, source_target_pairs={{0,8},{8,0},{1,9},{9,1},{2,10},{10,2},{3,11},{11,3},{4,12},{12,4},... | collective-permute-start | bytes 98312 | tf_op jit(solution)/shard_map/ppermute | solution.py:126
  (36 shorter events, 6.1 us)
Async XLA Ops:
  0.0 10.0 %copy-start.7 = (s32[64]{0:T(128)S(1)}, s32[64]{0:T(128)}, u32[]{:S(2)}) copy-start(s32[64]{0:T(128)} %param.8) | copy-start | bytes 772
  0.0 0.9 copy-start.5
  0.9 0.7 copy-start.6
  1.6 8.4 %copy-start.8 = (bf16[64,8,576]{2,1,0:T(8,128)(2,1)S(1)}, bf16[64,8,576]{2,1,0:T(8,128)(2,1)}, u32[]{:S(2)}) copy-start(bf16[64,8,576]{2,1,0:T(8,128)(2,1)} %param.6) | copy-start | bytes 1769476
  2.8 10.7 %copy-start.2 = (bf16[1024,64]{0,1:T(8,128)(2,1)S(1)}, bf16[1024,64]{0,1:T(8,128)(2,1)}, u32[]{:S(2)}) copy-start(bf16[1024,64]{0,1:T(8,128)(2,1)} %param.11) | copy-start | bytes 393220
  2.8 24.7 %all-to-all-start = ((bf16[8,64,640]{2,1,0:T(8,128)(2,1)}), bf16[8,64,640]{2,1,0:T(8,128)(2,1)}, u32[]{:S(2)}, u32[]{:S(2)}) async-start(bf16[8,64,640]{2,1,0:T(8,128)(2,1)} %shard_map.65), calls=%async_computation | async-start | bytes 1310720 | tf_op jit(solution)/shard_map/all_to_all | solution.py:362
  10.4 9.0 %collective-permute-start = (bf16[8,64,640]{2,1,0:T(8,128)(2,1)S(1)}, bf16[8,64,640]{2,1,0:T(8,128)(2,1)S(1)}, u32[]{:S(2)}, u32[]{:S(2)}) collective-permute-start(bf16[8,64,640]{2,1,0:T(8,128)(2,1)S(1)} %shard_map.64), channel_id=1, source_target_pairs={{0,8},{8,0},{1,9},{9,1},{2,10},{10,2},{3,11},{11,3},{4,12},{12,4},... | collective-permute-start | bytes 1966088 | tf_op jit(solution)/shard_map/ppermute | solution.py:126
  13.5 11.0 %collective-permute-start.7 = (bf16[64,1024]{1,0:T(8,128)(2,1)S(1)}, bf16[64,1024]{1,0:T(8,128)(2,1)S(1)}, u32[]{:S(2)}, u32[]{:S(2)}) collective-permute-start(bf16[64,1024]{1,0:T(8,128)(2,1)S(1)} %bitcast.20), channel_id=1, source_target_pairs={{0,32},{32,0},{1,33},{33,1},{2,34},{34,2},{3,35},{35,3},{4,36},{36... | collective-permute-start | bytes 393224 | tf_op jit(solution)/shard_map/ppermute | solution.py:126
  24.5 0.6 copy-start.3
  25.1 0.9 copy-start.4
  27.5 13.4 %copy-start.9 = (s32[8]{0:T(128)S(1)}, s32[8]{0:T(128)}, u32[]{:S(2)}) copy-start(s32[8]{0:T(128)} %param.9) | copy-start | bytes 100
  27.5 57.6 %all-to-all-start.1 = ((bf16[8,2,64,1024]{3,2,1,0:T(8,128)(2,1)}), bf16[8,2,64,1024]{3,2,1,0:T(8,128)(2,1)S(1)}, u32[]{:S(2)}, u32[]{:S(2)}) async-start(bf16[8,2,64,1024]{3,2,1,0:T(8,128)(2,1)} %shard_map.71), calls=%async_computation.1 | async-start | bytes 4194304 | tf_op jit(solution)/shard_map/all_to_all | solution.py:369
  34.3 6.7 %collective-permute-start.3 = (bf16[512,640]{1,0:T(8,128)(2,1)}, bf16[512,640]{1,0:T(8,128)(2,1)}, u32[]{:S(2)}, u32[]{:S(2)}) collective-permute-start(bf16[512,640]{1,0:T(8,128)(2,1)} %bitcast.6.key_ref), channel_id=1, source_target_pairs={{0,8},{8,0},{1,9},{9,1},{2,10},{10,2},{3,11},{11,3},{4,12},{12,4},... | collective-permute-start | bytes 1966088 | tf_op jit(solution)/shard_map/ppermute | solution.py:126
  37.1 16.7 %collective-permute-start.1 = (bf16[512,640]{1,0:T(8,128)(2,1)}, bf16[512,640]{1,0:T(8,128)(2,1)}, u32[]{:S(2)}, u32[]{:S(2)}) collective-permute-start(bf16[512,640]{1,0:T(8,128)(2,1)} %bitcast.6.key_ref), channel_id=1, source_target_pairs={{0,16},{8,60},{16,32},{24,8},{32,48},{40,24},{48,4},{56,40},{4,20}... | collective-permute-start | bytes 1966088 | tf_op jit(solution)/shard_map/ppermute | solution.py:122
  41.0 19.2 %collective-permute-start.4 = (bf16[512,640]{1,0:T(8,128)(2,1)}, bf16[512,640]{1,0:T(8,128)(2,1)S(1)}, u32[]{:S(2)}, u32[]{:S(2)}) collective-permute-start(bf16[512,640]{1,0:T(8,128)(2,1)} %collective-permute-done.3), channel_id=1, source_target_pairs={{0,16},{8,60},{16,32},{24,8},{32,48},{40,24},{48,4},{56,40},{4,20}... | collective-permute-start | bytes 1966088 | tf_op jit(solution)/shard_map/ppermute | solution.py:122
  49.3 1.2 %copy-start = (bf16[8,512,128]{2,1,0:T(8,128)(2,1)S(1)}, bf16[8,512,128]{2,1,0:T(8,128)(2,1)}, u32[]{:S(2)}) copy-start(bf16[8,512,128]{2,1,0:T(8,128)(2,1)} %up_ref.7) | copy-start | bytes 3145732
  50.5 6.4 %copy-start.1 = (bf16[8,512,128]{2,1,0:T(8,128)(2,1)S(1)}, bf16[8,512,128]{2,1,0:T(8,128)(2,1)}, u32[]{:S(2)}) copy-start(bf16[8,512,128]{2,1,0:T(8,128)(2,1)} %up_ref.7) | copy-start | bytes 3145732
  53.8 11.8 %collective-permute-start.2 = (bf16[512,640]{1,0:T(8,128)(2,1)}, bf16[512,640]{1,0:T(8,128)(2,1)S(1)}, u32[]{:S(2)}, u32[]{:S(2)}) collective-permute-start(bf16[512,640]{1,0:T(8,128)(2,1)} %collective-permute-done.1.key_ref), channel_id=1, source_target_pairs={{0,16},{8,60},{16,32},{24,8},{32,48},{40,24},{48,4},{56,40},{4,20}... | collective-permute-start | bytes 1966088 | tf_op jit(solution)/shard_map/ppermute | solution.py:122
  68.4 4.8 %collective-permute-start.5 = (bf16[2,64,1152]{2,1,0:T(8,128)(2,1)S(1)}, bf16[2,64,1152]{2,1,0:T(8,128)(2,1)S(1)}, u32[]{:S(2)}, u32[]{:S(2)}) collective-permute-start(bf16[2,64,1152]{2,1,0:T(8,128)(2,1)S(1)} %shard_map.69.own_ref), channel_id=1, source_target_pairs={{0,8},{8,0},{1,9},{9,1},{2,10},{10,2},{3,11},{11,3},{4,12},{12,4},... | collective-permute-start | bytes 884744 | tf_op jit(solution)/shard_map/ppermute | solution.py:126
  73.7 11.3 %collective-permute-start.6 = (bf16[128,1024]{1,0:T(8,128)(2,1)S(1)}, bf16[128,1024]{1,0:T(8,128)(2,1)S(1)}, u32[]{:S(2)}, u32[]{:S(2)}) collective-permute-start(bf16[128,1024]{1,0:T(8,128)(2,1)S(1)} %shard_map.70), channel_id=1, source_target_pairs={{0,16},{16,0},{1,17},{17,1},{2,18},{18,2},{3,19},{19,3},{4,20},{20... | collective-permute-start | bytes 786440 | tf_op jit(solution)/shard_map/ppermute | solution.py:126
  110.9 8.6 %collective-permute-start.8 = (bf16[2,64,128]{2,1,0:T(8,128)(2,1)S(1)}, bf16[2,64,128]{2,1,0:T(8,128)(2,1)S(1)}, u32[]{:S(2)}, u32[]{:S(2)}) collective-permute-start(bf16[2,64,128]{2,1,0:T(8,128)(2,1)S(1)} %get-tuple-element.26), channel_id=1, source_target_pairs={{0,8},{8,0},{1,9},{9,1},{2,10},{10,2},{3,11},{11,3},{4,12},{12,4},... | collective-permute-start | bytes 98312 | tf_op jit(solution)/shard_map/ppermute | solution.py:126

commit v6 on v5

--- a/solution.py
+++ b/solution.py
@@ -85,7 +85,7 @@
             pltpu.SemaphoreType.DMA((2,)),
             pltpu.SemaphoreType.DMA((copies,)),
         ],
-        compiler_params=pltpu.CompilerParams(vmem_limit_bytes=VMEM),
+        compiler_params=pltpu.CompilerParams(vmem_limit_bytes=60 * 1024 * 1024),
     )(positions.reshape(1, -1), latents)
 
 
@@ -263,7 +263,7 @@
         for k in range(4):
             at_near = near if k < 2 else 1 - near
             at_core = core if k % 2 == 0 else 1 - core
-            out_ref[at_near, y, at_core] = part[k * toks : (k + 1) * toks]
+            out_ref[y % 4, at_near, at_core, y // 4] = part[k * toks : (k + 1) * toks]
 
 
 def project(near, core, v, w):
@@ -273,7 +273,7 @@
         project_kernel,
         in_specs=[pl.BlockSpec(memory_space=pltpu.SMEM)] + [WHOLE] * 2,
         out_specs=WHOLE,
-        out_shape=jax.ShapeDtypeStruct((2, blocks, 2, toks, cols), jnp.bfloat16),
+        out_shape=jax.ShapeDtypeStruct((4, 2, 2, blocks // 4, toks, cols), jnp.bfloat16),
         compiler_params=pltpu.CompilerParams(vmem_limit_bytes=VMEM),
         cost_estimate=pl.CostEstimate(
             flops=8 * toks * blocks * cols * depth,
@@ -283,50 +283,36 @@
     )(jnp.stack([near, core]), v, w)
 
 
-def add_heads_kernel(core_ref, parts_ref, keep_ref, give_ref):
-    core = core_ref[0]
-    for near in range(2):
-        for whose, out_ref in ((core, keep_ref), (1 - core, give_ref)):
-            total = parts_ref[near, 0, whose].astype(jnp.float32)
-            for h in range(1, parts_ref.shape[1]):
-                total += parts_ref[near, h, whose].astype(jnp.float32)
-            out_ref[near] = total.astype(out_ref.dtype)
-
-
-def add_heads(core, parts):
-    half = jax.ShapeDtypeStruct((2,) + parts.shape[3:], parts.dtype)
-    return pl.pallas_call(
-        add_heads_kernel,
+def add_x_kernel(here_ref, parts_ref, keep_ref, give_ref):
+    here = here_ref[0]
+    for whose, out_ref in ((1 - here, give_ref), (here, keep_ref)):
+        for near in range(2):
+            total = []
+            for core in range(2):
+                t = parts_ref[0, near, core, whose].astype(jnp.float32)
+                for x in range(1, parts_ref.shape[0]):
+                    t += parts_ref[x, near, core, whose].astype(jnp.float32)
+                total.append(t)
+            for far in range(2):
+                at = far * 256 + near * 128
+                lanes = slice(far * 64, far * 64 + 64)
+                out_ref[:, at : at + 128] = jnp.concatenate(
+                    [t[:, lanes] for t in total], axis=1
+                ).astype(out_ref.dtype)
+
+
+def add_x(here, parts):
+    toks, cols = parts.shape[4:]
+    return pl.pallas_call(
+        add_x_kernel,
         in_specs=[pl.BlockSpec(memory_space=pltpu.SMEM), WHOLE],
         out_specs=[WHOLE] * 2,
-        out_shape=[half] * 2,
-        compiler_params=pltpu.CompilerParams(vmem_limit_bytes=VMEM),
-    )(core, parts)
-
-
-def lay_out_kernel(core_ref, own_ref, other_ref, out_ref):
-    first = core_ref[0] == 0
-    for near in range(2):
-        own, other = own_ref[near], other_ref[near]
-        for far in range(2):
-            lanes = slice(far * 64, far * 64 + 64)
-            at = far * 256 + near * 128
-            out_ref[:, at : at + 128] = jnp.where(
-                first,
-                jnp.concatenate([own[:, lanes], other[:, lanes]], axis=1),
-                jnp.concatenate([other[:, lanes], own[:, lanes]], axis=1),
-            )
-
-
-def lay_out(core, own, other):
-    _, toks, cols = own.shape
-    return pl.pallas_call(
-        lay_out_kernel,
-        in_specs=[pl.BlockSpec(memory_space=pltpu.SMEM)] + [WHOLE] * 2,
-        out_specs=WHOLE,
-        out_shape=jax.ShapeDtypeStruct((toks, 4 * cols), own.dtype),
-        compiler_params=pltpu.CompilerParams(vmem_limit_bytes=VMEM),
-    )(core, own, other)
+        out_shape=[
+            jax.ShapeDtypeStruct((toks, 4 * cols), jnp.float32),
+            jax.ShapeDtypeStruct((toks, 4 * cols), parts.dtype),
+        ],
+        compiler_params=pltpu.CompilerParams(vmem_limit_bytes=VMEM),
+    )(here, parts)
 
 
 def pair_kernel(far_ref, own_ref, other_ref, _, out_hbm, both_ref, sems):
@@ -382,11 +368,12 @@
     v = jnp.concatenate([values, swap(values, "zl_lat")], axis=0)
 
     partial = project(near, core, v, w)
-    arrived = lax.all_to_all(
-        partial.reshape((16,) + partial.shape[2:]), ("zl_lat", "z_hi", "x"), 0, 0
-    )
-    keep, give = add_heads(core.reshape(1), arrived.reshape(partial.shape))
-    return lay_out(core.reshape(1), keep, swap(give, "core"))
+    parts = lax.all_to_all(
+        partial.reshape((16,) + partial.shape[3:]), ("x", "zl_lat", "core"), 0, 0
+    )
+    z_hi = lax.axis_index("z_hi").astype(jnp.int32)
+    keep, give = add_x(z_hi.reshape(1), parts.reshape(partial.shape))
+    return (keep + swap(give, "z_hi").astype(jnp.float32)).astype(jnp.bfloat16)
 
 
 def solution(mesh):

time: 121 us -> 119 us (0.983)
  the two profiles are of different devices: /device:TPU:73 before, /device:TPU:8 now
where the time goes in v6:
time: 119 us; the launch traced here: 118 us
  starting transfers between devices  50.6 us (43%)
  waiting for transfers between devices  43.1 us (36%)
  Pallas kernels  18.4 us (15%)
  local copies, waits for them, and re-layouts  3.26 us (3%)
  other arithmetic  2.15 us (2%)
    ppermute x6, starting transfers between devices, swap(): return lax.ppermute(x, axis, [(0, 1), (1, 0)])  21.3 us
    ppermute x6, waiting for transfers between devices, swap(): return lax.ppermute(x, axis, [(0, 1), (1, 0)])  18.1 us
    ppermute x3, waiting for transfers between devices, shift_z(): return lax.ppermute(x, ('zh_lat', 'zl_lat', 'core', 'z_hi'), perm)  12.3 us
    pallas_call x4, Pallas kernels, attend(): pl.pallas_call(functools.partial(attend_kernel, group, first, last), in_s...  11.3 us
    all_to_all x1, waiting for transfers between devices, on_device(): lax.all_to_all(partial.reshape((16,) + partial.shape[3:]), ('x', 'zl_lat'...  10.9 us
    ppermute x3, starting transfers between devices, shift_z(): return lax.ppermute(x, ('zh_lat', 'zl_lat', 'core', 'z_hi'), perm)  10 us
    all_to_all x1, starting transfers between devices, on_device(): along_y = lax.all_to_all(key_rows, 'y', 0, 0).reshape(8 * toks, WIDTH)  9.41 us
    all_to_all x1, starting transfers between devices, on_device(): w = lax.all_to_all(w, 'y', 0, 0)  5.4 us
  transfers between devices with their start and end apart: 12, of which 9 were waited for; matrix products, arithmetic and copies ran while one was open for 1% of the time, Pallas kernels for 11%

profile of v6, /device:TPU:8, one launch (start us, length us, event | category | flops | bytes accessed | tf_op | source)
XLA Modules:
  0.0 117.7 jit_solution(9521340067899177817)
XLA Ops:
  0.0 2.1 %shard_map.65 = bf16[8,64,640]{2,1,0:T(8,128)(2,1)} custom-call(s32[1,64]{1,0:T(1,128)} %bitcast.25, bf16[64,576]{1,0:T(8,128)(2,1)} %latents_hbm.1), custom_call_target="tpu_custom_call" | custom-call | tf_op jit(solution)/shard_map/pallas_call | solution.py:76
  2.2 9.4 %all-to-all-start = ((bf16[8,64,640]{2,1,0:T(8,128)(2,1)}), bf16[8,64,640]{2,1,0:T(8,128)(2,1)S(1)}, u32[]{:S(2)}, u32[]{:S(2)}) async-start(bf16[8,64,640]{2,1,0:T(8,128)(2,1)} %shard_map.65), calls=%async_computation | async-start | bytes 1310720 | tf_op jit(solution)/shard_map/all_to_all | solution.py:348
  12.0 1.9 %collective-permute-start = (bf16[8,64,640]{2,1,0:T(8,128)(2,1)S(1)}, bf16[8,64,640]{2,1,0:T(8,128)(2,1)}, u32[]{:S(2)}, u32[]{:S(2)}) collective-permute-start(bf16[8,64,640]{2,1,0:T(8,128)(2,1)S(1)} %shard_map.64), channel_id=1, source_target_pairs={{0,8},{8,0},{1,9},{9,1},{2,10},{10,2},{3,11},{11,3},{4,12},{12,4},... | collective-permute-start | bytes 1966088 | tf_op jit(solution)/shard_map/ppermute | solution.py:126
  13.9 4.4 %collective-permute-start.7 = (bf16[64,1024]{1,0:T(8,128)(2,1)S(1)}, bf16[64,1024]{1,0:T(8,128)(2,1)S(1)}, u32[]{:S(2)}, u32[]{:S(2)}) collective-permute-start(bf16[64,1024]{1,0:T(8,128)(2,1)S(1)} %bitcast.23), channel_id=1, source_target_pairs={{0,32},{32,0},{1,33},{33,1},{2,34},{34,2},{3,35},{35,3},{4,36},{36... | collective-permute-start | bytes 393224 | tf_op jit(solution)/shard_map/ppermute | solution.py:126
  19.5 5.9 %collective-permute-done.7.other_ref = bf16[64,1024]{1,0:T(8,128)(2,1)S(1)} collective-permute-done((bf16[64,1024]{1,0:T(8,128)(2,1)S(1)}, bf16[64,1024]{1,0:T(8,128)(2,1)S(1)}, u32[]{:S(2)}, u32[]{:S(2)}) %collective-permute-start.7) | collective-permute-done | bytes 131104 | tf_op jit(solution)/shard_map/ppermute | solution.py:126
  29.5 5.4 %all-to-all-start.1 = ((bf16[8,2,64,1024]{3,2,1,0:T(8,128)(2,1)}), bf16[8,2,64,1024]{3,2,1,0:T(8,128)(2,1)S(1)}, u32[]{:S(2)}, u32[]{:S(2)}) async-start(bf16[8,2,64,1024]{3,2,1,0:T(8,128)(2,1)} %shard_map.71), calls=%async_computation.1 | async-start | bytes 4194304 | tf_op jit(solution)/shard_map/all_to_all | solution.py:355
  34.9 1.9 %collective-permute-start.3 = (bf16[512,640]{1,0:T(8,128)(2,1)}, bf16[512,640]{1,0:T(8,128)(2,1)}, u32[]{:S(2)}, u32[]{:S(2)}) collective-permute-start(bf16[512,640]{1,0:T(8,128)(2,1)} %bitcast.20), channel_id=1, source_target_pairs={{0,8},{8,0},{1,9},{9,1},{2,10},{10,2},{3,11},{11,3},{4,12},{12,4},... | collective-permute-start | bytes 1966088 | tf_op jit(solution)/shard_map/ppermute | solution.py:126
  36.9 3.9 %collective-permute-start.1 = (bf16[512,640]{1,0:T(8,128)(2,1)}, bf16[512,640]{1,0:T(8,128)(2,1)}, u32[]{:S(2)}, u32[]{:S(2)}) collective-permute-start(bf16[512,640]{1,0:T(8,128)(2,1)} %bitcast.21), channel_id=1, source_target_pairs={{0,16},{8,60},{16,32},{24,8},{32,48},{40,24},{48,4},{56,40},{4,20}... | collective-permute-start | bytes 1966088 | tf_op jit(solution)/shard_map/ppermute | solution.py:122
  40.9 4.3 %collective-permute-start.4 = (bf16[512,640]{1,0:T(8,128)(2,1)}, bf16[512,640]{1,0:T(8,128)(2,1)S(1)}, u32[]{:S(2)}, u32[]{:S(2)}) collective-permute-start(bf16[512,640]{1,0:T(8,128)(2,1)} %collective-permute-done.3), channel_id=1, source_target_pairs={{0,16},{8,60},{16,32},{24,8},{32,48},{40,24},{48,4},{56,40},{4,20}... | collective-permute-start | bytes 1966088 | tf_op jit(solution)/shard_map/ppermute | solution.py:122
  47.5 2.6 %shard_map.66 = (f32[8,128,128]{2,1,0:T(8,128)S(1)}, f32[8,128,128]{2,1,0:T(8,128)S(1)}, f32[8,128,128]{2,1,0:T(8,128)S(1)}) custom-call(s32[8]{0:T(128)S(1)} %bitcast.27, bf16[8,128,640]{2,1,0:T(8,128)(2,1)S(1)} %pad_maximum_fusion.q_ref, bf16[512,640]{1,0:T(8,128)(2,1)S(1)} %bitcast.22, bf16[8,512,128]{2,1,0:T(8,128)(2,1)S(1)} %copy-done), custom_call_target="tpu_custom_call" | custom-call | flops 3623878656 | bytes 14548992 | tf_op jit(solution)/shard_map/pallas_call | solution.py:213
  50.1 6.1 %collective-permute-done.1.key_ref = bf16[512,640]{1,0:T(8,128)(2,1)} collective-permute-done((bf16[512,640]{1,0:T(8,128)(2,1)}, bf16[512,640]{1,0:T(8,128)(2,1)}, u32[]{:S(2)}, u32[]{:S(2)}) %collective-permute-start.1) | collective-permute-done | bytes 655392 | tf_op jit(solution)/shard_map/ppermute | solution.py:122
  56.3 1.9 %collective-permute-start.2 = (bf16[512,640]{1,0:T(8,128)(2,1)}, bf16[512,640]{1,0:T(8,128)(2,1)S(1)}, u32[]{:S(2)}, u32[]{:S(2)}) collective-permute-start(bf16[512,640]{1,0:T(8,128)(2,1)} %collective-permute-done.1.key_ref), channel_id=1, source_target_pairs={{0,16},{8,60},{16,32},{24,8},{32,48},{40,24},{48,4},{56,40},{4,20}... | collective-permute-start | bytes 1966088 | tf_op jit(solution)/shard_map/ppermute | solution.py:122
  58.2 3.2 %shard_map.67 = (f32[8,128,128]{2,1,0:T(8,128)S(1)}, f32[8,128,128]{2,1,0:T(8,128)S(1)}, f32[8,128,128]{2,1,0:T(8,128)S(1)}) custom-call(s32[8]{0:T(128)S(1)} %bitcast.28, bf16[8,128,640]{2,1,0:T(8,128)(2,1)S(1)} %pad_maximum_fusion.q_ref, bf16[512,640]{1,0:T(8,128)(2,1)} %collective-permute-done.1.key_ref, bf16[8,512,128]{2,1,0:T(8,128)(2,1)S(1)} %copy-done.1, ...), custom_call_target="tpu_custom_call" | custom-call | flops 3623878656 | bytes 14548992 | tf_op jit(solution)/shard_map/pallas_call | solution.py:213
  63.2 2.6 %shard_map.68 = (f32[8,128,128]{2,1,0:T(8,128)S(1)}, f32[8,128,128]{2,1,0:T(8,128)S(1)}, f32[8,128,128]{2,1,0:T(8,128)S(1)}) custom-call(s32[8]{0:T(128)S(1)} %bitcast.29, bf16[8,128,640]{2,1,0:T(8,128)(2,1)S(1)} %pad_maximum_fusion.q_ref, bf16[512,640]{1,0:T(8,128)(2,1)S(1)} %collective-permute-done.4.key_ref, bf16[8,512,128]{2,1,0:T(8,128)(2,1)S(1)} %copy-done.1, ...), custom_call_target="tpu_custom_call" | custom-call | flops 3623878656 | bytes 14548992 | tf_op jit(solution)/shard_map/pallas_call | solution.py:213
  65.8 4.4 %collective-permute-done.2.key_ref = bf16[512,640]{1,0:T(8,128)(2,1)S(1)} collective-permute-done((bf16[512,640]{1,0:T(8,128)(2,1)}, bf16[512,640]{1,0:T(8,128)(2,1)S(1)}, u32[]{:S(2)}, u32[]{:S(2)}) %collective-permute-start.2) | collective-permute-done | bytes 655392 | tf_op jit(solution)/shard_map/ppermute | solution.py:122
  70.2 2.8 %shard_map.69.own_ref = bf16[2,64,1152]{2,1,0:T(8,128)(2,1)S(1)} custom-call(s32[8]{0:T(128)S(1)} %bitcast.30, bf16[8,128,640]{2,1,0:T(8,128)(2,1)S(1)} %pad_maximum_fusion.q_ref, bf16[512,640]{1,0:T(8,128)(2,1)S(1)} %collective-permute-done.2.key_ref, bf16[8,512,128]{2,1,0:T(8,128)(2,1)S(1)} %copy-done.1, f32[8,128,128]{2,1,0:T(8,128)S(1)} %get-tuple-element.22.refs_0_, ...), custom_call_target="tpu_custom_call" | custom-call | flops 1207959552 | bytes 4849664 | tf_op jit(solution)/shard_map/pallas_call | solution.py:213
  73.0 1.9 %collective-permute-start.5 = (bf16[2,64,1152]{2,1,0:T(8,128)(2,1)S(1)}, bf16[2,64,1152]{2,1,0:T(8,128)(2,1)S(1)}, u32[]{:S(2)}, u32[]{:S(2)}) collective-permute-start(bf16[2,64,1152]{2,1,0:T(8,128)(2,1)S(1)} %shard_map.69.own_ref), channel_id=1, source_target_pairs={{0,8},{8,0},{1,9},{9,1},{2,10},{10,2},{3,11},{11,3},{4,12},{12,4},... | collective-permute-start | bytes 884744 | tf_op jit(solution)/shard_map/ppermute | solution.py:126
  77.0 1.9 %collective-permute-start.6 = (bf16[128,1024]{1,0:T(8,128)(2,1)S(1)}, bf16[128,1024]{1,0:T(8,128)(2,1)S(1)}, u32[]{:S(2)}, u32[]{:S(2)}) collective-permute-start(bf16[128,1024]{1,0:T(8,128)(2,1)S(1)} %shard_map.70), channel_id=1, source_target_pairs={{0,16},{16,0},{1,17},{17,1},{2,18},{18,2},{3,19},{19,3},{4,20},{20... | collective-permute-start | bytes 786440 | tf_op jit(solution)/shard_map/ppermute | solution.py:126
  79.0 8.2 %collective-permute-done.6 = bf16[128,1024]{1,0:T(8,128)(2,1)S(1)} collective-permute-done((bf16[128,1024]{1,0:T(8,128)(2,1)S(1)}, bf16[128,1024]{1,0:T(8,128)(2,1)S(1)}, u32[]{:S(2)}, u32[]{:S(2)}) %collective-permute-start.6) | collective-permute-done | bytes 262176 | tf_op jit(solution)/shard_map/ppermute | solution.py:126
  87.3 2.6 %shard_map.72 = bf16[4,2,2,2,64,128]{5,4,3,2,1,0:T(8,128)(2,1)} custom-call(s32[2]{0:T(128)S(1)} %pad_add_fusion.slots_ref, bf16[256,1024]{1,0:T(8,128)(2,1)S(1)} %pad_maximum_fusion.1.v_ref, bf16[8,128,1024]{2,1,0:T(8,128)(2,1)S(1)} %bitcast.16), custom_call_target="tpu_custom_call" | custom-call | flops 536870912 | bytes 2097152 | tf_op jit(solution)/shard_map/pallas_call | solution.py:272
  89.9 4.4 %all-to-all-start.2 = ((bf16[16,2,64,128]{3,2,1,0:T(8,128)(2,1)}), bf16[16,2,64,128]{3,2,1,0:T(8,128)(2,1)S(1)}, u32[]{:S(2)}, u32[]{:S(2)}) async-start(bf16[16,2,64,128]{3,2,1,0:T(8,128)(2,1)} %bitcast.12), calls=%async_computation.2 | async-start | bytes 1048576 | tf_op jit(solution)/shard_map/all_to_all | solution.py:371
  94.3 10.9 %all-to-all-done.2 = bf16[16,2,64,128]{3,2,1,0:T(8,128)(2,1)S(1)} async-done(((bf16[16,2,64,128]{3,2,1,0:T(8,128)(2,1)}), bf16[16,2,64,128]{3,2,1,0:T(8,128)(2,1)S(1)}, u32[]{:S(2)}, u32[]{:S(2)}) %all-to-all-start.2) | async-done | bytes 524320 | tf_op jit(solution)/shard_map/all_to_all | solution.py:371
  105.3 9.3 %collective-permute-start.8 = (bf16[64,512]{1,0:T(8,128)(2,1)S(1)}, bf16[64,512]{1,0:T(8,128)(2,1)S(1)}, u32[]{:S(2)}, u32[]{:S(2)}) collective-permute-start(bf16[64,512]{1,0:T(8,128)(2,1)S(1)} %get-tuple-element.26), channel_id=1, source_target_pairs={{0,4},{4,0},{1,5},{5,1},{2,6},{6,2},{3,7},{7,3},{8,12},{12,8},{9,1... | collective-permute-start | bytes 196616 | tf_op jit(solution)/shard_map/ppermute | solution.py:126
  114.6 2.5 %collective-permute-done.8 = bf16[64,512]{1,0:T(8,128)(2,1)S(1)} collective-permute-done((bf16[64,512]{1,0:T(8,128)(2,1)S(1)}, bf16[64,512]{1,0:T(8,128)(2,1)S(1)}, u32[]{:S(2)}, u32[]{:S(2)}) %collective-permute-start.8) | collective-permute-done | bytes 65568 | tf_op jit(solution)/shard_map/ppermute | solution.py:126
  (33 shorter events, 12.9 us)
Async XLA Ops:
  0.0 11.6 %copy-start.5 = (s32[64]{0:T(128)S(1)}, s32[64]{0:T(128)}, u32[]{:S(2)}) copy-start(s32[64]{0:T(128)} %param.8) | copy-start | bytes 772
  0.0 11.6 %copy-start.6 = (bf16[64,8,576]{2,1,0:T(8,128)(2,1)S(1)}, bf16[64,8,576]{2,1,0:T(8,128)(2,1)}, u32[]{:S(2)}) copy-start(bf16[64,8,576]{2,1,0:T(8,128)(2,1)} %param.6) | copy-start | bytes 1769476
  2.1 11.8 %copy-start.4 = (bf16[1024,64]{0,1:T(8,128)(2,1)S(1)}, bf16[1024,64]{0,1:T(8,128)(2,1)}, u32[]{:S(2)}) copy-start(bf16[1024,64]{0,1:T(8,128)(2,1)} %param.11) | copy-start | bytes 393220
  2.2 26.5 %all-to-all-start = ((bf16[8,64,640]{2,1,0:T(8,128)(2,1)}), bf16[8,64,640]{2,1,0:T(8,128)(2,1)S(1)}, u32[]{:S(2)}, u32[]{:S(2)}) async-start(bf16[8,64,640]{2,1,0:T(8,128)(2,1)} %shard_map.65), calls=%async_computation | async-start | bytes 1310720 | tf_op jit(solution)/shard_map/all_to_all | solution.py:348
  12.0 6.3 %collective-permute-start = (bf16[8,64,640]{2,1,0:T(8,128)(2,1)S(1)}, bf16[8,64,640]{2,1,0:T(8,128)(2,1)}, u32[]{:S(2)}, u32[]{:S(2)}) collective-permute-start(bf16[8,64,640]{2,1,0:T(8,128)(2,1)S(1)} %shard_map.64), channel_id=1, source_target_pairs={{0,8},{8,0},{1,9},{9,1},{2,10},{10,2},{3,11},{11,3},{4,12},{12,4},... | collective-permute-start | bytes 1966088 | tf_op jit(solution)/shard_map/ppermute | solution.py:126
  13.9 11.5 %collective-permute-start.7 = (bf16[64,1024]{1,0:T(8,128)(2,1)S(1)}, bf16[64,1024]{1,0:T(8,128)(2,1)S(1)}, u32[]{:S(2)}, u32[]{:S(2)}) collective-permute-start(bf16[64,1024]{1,0:T(8,128)(2,1)S(1)} %bitcast.23), channel_id=1, source_target_pairs={{0,32},{32,0},{1,33},{33,1},{2,34},{34,2},{3,35},{35,3},{4,36},{36... | collective-permute-start | bytes 393224 | tf_op jit(solution)/shard_map/ppermute | solution.py:126
  26.8 13.9 %copy-start.7 = (s32[8]{0:T(128)S(1)}, s32[8]{0:T(128)}, u32[]{:S(2)}) copy-start(s32[8]{0:T(128)} %param.9) | copy-start | bytes 100
  28.7 0.9 copy-start.2
  29.5 57.7 %all-to-all-start.1 = ((bf16[8,2,64,1024]{3,2,1,0:T(8,128)(2,1)}), bf16[8,2,64,1024]{3,2,1,0:T(8,128)(2,1)S(1)}, u32[]{:S(2)}, u32[]{:S(2)}) async-start(bf16[8,2,64,1024]{3,2,1,0:T(8,128)(2,1)} %shard_map.71), calls=%async_computation.1 | async-start | bytes 4194304 | tf_op jit(solution)/shard_map/all_to_all | solution.py:355
  34.9 6.0 %collective-permute-start.3 = (bf16[512,640]{1,0:T(8,128)(2,1)}, bf16[512,640]{1,0:T(8,128)(2,1)}, u32[]{:S(2)}, u32[]{:S(2)}) collective-permute-start(bf16[512,640]{1,0:T(8,128)(2,1)} %bitcast.20), channel_id=1, source_target_pairs={{0,8},{8,0},{1,9},{9,1},{2,10},{10,2},{3,11},{11,3},{4,12},{12,4},... | collective-permute-start | bytes 1966088 | tf_op jit(solution)/shard_map/ppermute | solution.py:126
  36.9 19.4 %collective-permute-start.1 = (bf16[512,640]{1,0:T(8,128)(2,1)}, bf16[512,640]{1,0:T(8,128)(2,1)}, u32[]{:S(2)}, u32[]{:S(2)}) collective-permute-start(bf16[512,640]{1,0:T(8,128)(2,1)} %bitcast.21), channel_id=1, source_target_pairs={{0,16},{8,60},{16,32},{24,8},{32,48},{40,24},{48,4},{56,40},{4,20}... | collective-permute-start | bytes 1966088 | tf_op jit(solution)/shard_map/ppermute | solution.py:122
  40.9 22.3 %collective-permute-start.4 = (bf16[512,640]{1,0:T(8,128)(2,1)}, bf16[512,640]{1,0:T(8,128)(2,1)S(1)}, u32[]{:S(2)}, u32[]{:S(2)}) collective-permute-start(bf16[512,640]{1,0:T(8,128)(2,1)} %collective-permute-done.3), channel_id=1, source_target_pairs={{0,16},{8,60},{16,32},{24,8},{32,48},{40,24},{48,4},{56,40},{4,20}... | collective-permute-start | bytes 1966088 | tf_op jit(solution)/shard_map/ppermute | solution.py:122
  45.2 1.2 %copy-start = (bf16[8,512,128]{2,1,0:T(8,128)(2,1)S(1)}, bf16[8,512,128]{2,1,0:T(8,128)(2,1)}, u32[]{:S(2)}) copy-start(bf16[8,512,128]{2,1,0:T(8,128)(2,1)} %up_ref.7) | copy-start | bytes 3145732
  46.4 1.1 copy-start.3
  47.5 10.7 %copy-start.1 = (bf16[8,512,128]{2,1,0:T(8,128)(2,1)S(1)}, bf16[8,512,128]{2,1,0:T(8,128)(2,1)}, u32[]{:S(2)}) copy-start(bf16[8,512,128]{2,1,0:T(8,128)(2,1)} %up_ref.7) | copy-start | bytes 3145732
  56.3 13.9 %collective-permute-start.2 = (bf16[512,640]{1,0:T(8,128)(2,1)}, bf16[512,640]{1,0:T(8,128)(2,1)S(1)}, u32[]{:S(2)}, u32[]{:S(2)}) collective-permute-start(bf16[512,640]{1,0:T(8,128)(2,1)} %collective-permute-done.1.key_ref), channel_id=1, source_target_pairs={{0,16},{8,60},{16,32},{24,8},{32,48},{40,24},{48,4},{56,40},{4,20}... | collective-permute-start | bytes 1966088 | tf_op jit(solution)/shard_map/ppermute | solution.py:122
  73.0 3.5 %collective-permute-start.5 = (bf16[2,64,1152]{2,1,0:T(8,128)(2,1)S(1)}, bf16[2,64,1152]{2,1,0:T(8,128)(2,1)S(1)}, u32[]{:S(2)}, u32[]{:S(2)}) collective-permute-start(bf16[2,64,1152]{2,1,0:T(8,128)(2,1)S(1)} %shard_map.69.own_ref), channel_id=1, source_target_pairs={{0,8},{8,0},{1,9},{9,1},{2,10},{10,2},{3,11},{11,3},{4,12},{12,4},... | collective-permute-start | bytes 884744 | tf_op jit(solution)/shard_map/ppermute | solution.py:126
  77.0 10.2 %collective-permute-start.6 = (bf16[128,1024]{1,0:T(8,128)(2,1)S(1)}, bf16[128,1024]{1,0:T(8,128)(2,1)S(1)}, u32[]{:S(2)}, u32[]{:S(2)}) collective-permute-start(bf16[128,1024]{1,0:T(8,128)(2,1)S(1)} %shard_map.70), channel_id=1, source_target_pairs={{0,16},{16,0},{1,17},{17,1},{2,18},{18,2},{3,19},{19,3},{4,20},{20... | collective-permute-start | bytes 786440 | tf_op jit(solution)/shard_map/ppermute | solution.py:126
  89.9 15.3 %all-to-all-start.2 = ((bf16[16,2,64,128]{3,2,1,0:T(8,128)(2,1)}), bf16[16,2,64,128]{3,2,1,0:T(8,128)(2,1)S(1)}, u32[]{:S(2)}, u32[]{:S(2)}) async-start(bf16[16,2,64,128]{3,2,1,0:T(8,128)(2,1)} %bitcast.12), calls=%async_computation.2 | async-start | bytes 1048576 | tf_op jit(solution)/shard_map/all_to_all | solution.py:371
  105.3 11.7 %collective-permute-start.8 = (bf16[64,512]{1,0:T(8,128)(2,1)S(1)}, bf16[64,512]{1,0:T(8,128)(2,1)S(1)}, u32[]{:S(2)}, u32[]{:S(2)}) collective-permute-start(bf16[64,512]{1,0:T(8,128)(2,1)S(1)} %get-tuple-element.26), channel_id=1, source_target_pairs={{0,4},{4,0},{1,5},{5,1},{2,6},{6,2},{3,7},{7,3},{8,12},{12,8},{9,1... | collective-permute-start | bytes 196616 | tf_op jit(solution)/shard_map/ppermute | solution.py:126

commit v7 on v6

--- a/solution.py
+++ b/solution.py
@@ -127,13 +127,19 @@
 
 
 def attend_kernel(group, first, last, ends_ref, q_ref, key_ref, up_ref, *refs):
-    if not first:
+    if first:
+        key_hbm = key_ref
+        top_out, total_out, part_out, key_ref, sem = refs
+        arrival = pltpu.make_async_copy(key_hbm, key_ref, sem.at[0])
+        arrival.start()
+        arrival.wait()
+    else:
         top_in, total_in, part_in = refs[:3]
         refs = refs[3:]
-    if last:
-        (out_ref,) = refs
-    else:
-        top_out, total_out, part_out = refs
+        if last:
+            (out_ref,) = refs
+        else:
+            top_out, total_out, part_out = refs
     heads, toks, _ = q_ref.shape
     half = toks // 2
     meta = q_ref[0, :, LATENT:].astype(jnp.float32)
@@ -212,10 +218,20 @@
     rows, count = heads * toks, keys.shape[0]
     return pl.pallas_call(
         functools.partial(attend_kernel, group, first, last),
-        in_specs=[pl.BlockSpec(memory_space=pltpu.SMEM)] + [WHOLE] * (len(args) - 1),
+        in_specs=[
+            pl.BlockSpec(memory_space=pltpu.SMEM),
+            WHOLE,
+            pl.BlockSpec(memory_space=pltpu.HBM) if first else WHOLE,
+        ]
+        + [WHOLE] * (len(args) - 3),
         out_specs=WHOLE if last else [WHOLE] * 3,
         out_shape=out_shape,
-        compiler_params=pltpu.CompilerParams(vmem_limit_bytes=VMEM),
+        scratch_shapes=[pltpu.VMEM(keys.shape, keys.dtype), pltpu.SemaphoreType.DMA((1,))]
+        if first
+        else [],
+        compiler_params=pltpu.CompilerParams(
+            vmem_limit_bytes=56 * 1024 * 1024 if first else VMEM
+        ),
         cost_estimate=pl.CostEstimate(
             flops=2 * weight * rows * count * (WIDTH + LATENT),
             bytes_accessed=weight * (2 * count * WIDTH + rows * 4096),

time: 119 us -> 118 us (level)
  waiting for transfers between devices: 43.1 us -> 40.2 us
  Pallas kernels: 18.4 us -> 21.1 us
    ppermute x3, waiting for transfers between devices: 12.3 us -> 8.23 us  [shift_z(): return lax.ppermute(x, ('zh_lat', 'zl_lat', 'core', 'z_hi'), perm)]
    pallas_call x4, Pallas kernels: 11.3 us -> 14 us  [attend(): pl.pallas_call(functools.partial(attend_kernel, group, first, last), in_s...]
    ppermute x6, waiting for transfers between devices: 18.1 us -> 19.8 us  [swap(): return lax.ppermute(x, axis, [(0, 1), (1, 0)])]
    unnamed x17 -> x23, local copies, waits for them, and re-layouts: 3.26 us -> 3.23 us
  transfers between devices with their start and end apart: 12 -> 12, of which waited for: 9 -> 8; matrix products, arithmetic and copies ran while one was open for 1% -> 1% of each run, Pallas kernels for 11% -> 14%
where the time goes in v7:
time: 118 us; the launch traced here: 117 us
  starting transfers between devices  50.5 us (43%)
  waiting for transfers between devices  40.2 us (34%)
  Pallas kernels  21.1 us (18%)
  local copies, waits for them, and re-layouts  3.23 us (3%)
  other arithmetic  1.56 us (1%)
    ppermute x6, starting transfers between devices, swap(): return lax.ppermute(x, axis, [(0, 1), (1, 0)])  20.6 us
    ppermute x6, waiting for transfers between devices, swap(): return lax.ppermute(x, axis, [(0, 1), (1, 0)])  19.8 us
    pallas_call x4, Pallas kernels, attend(): pl.pallas_call(functools.partial(attend_kernel, group, first, last), in_s...  14 us
    all_to_all x1, waiting for transfers between devices, on_device(): lax.all_to_all(partial.reshape((16,) + partial.shape[3:]), ('x', 'zl_lat'...  10.9 us
    all_to_all x1, starting transfers between devices, on_device(): along_y = lax.all_to_all(key_rows, 'y', 0, 0).reshape(8 * toks, WIDTH)  10 us
    ppermute x3, starting transfers between devices, shift_z(): return lax.ppermute(x, ('zh_lat', 'zl_lat', 'core', 'z_hi'), perm)  9.49 us
    ppermute x3, waiting for transfers between devices, shift_z(): return lax.ppermute(x, ('zh_lat', 'zl_lat', 'core', 'z_hi'), perm)  8.23 us
    all_to_all x1, starting transfers between devices, on_device(): w = lax.all_to_all(w, 'y', 0, 0)  5.94 us
  transfers between devices with their start and end apart: 12, of which 8 were waited for; matrix products, arithmetic and copies ran while one was open for 1% of the time, Pallas kernels for 14%

profile of v7, /device:TPU:8, one launch (start us, length us, event | category | flops | bytes accessed | tf_op | source)
XLA Modules:
  0.0 117.0 jit_solution(10782571989954653185)
XLA Ops:
  0.0 2.1 %shard_map.65 = bf16[8,64,640]{2,1,0:T(8,128)(2,1)} custom-call(s32[1,64]{1,0:T(1,128)} %bitcast.22, bf16[64,576]{1,0:T(8,128)(2,1)} %latents_hbm.1), custom_call_target="tpu_custom_call" | custom-call | tf_op jit(solution)/shard_map/pallas_call | solution.py:76
  2.1 10.0 %all-to-all-start = ((bf16[8,64,640]{2,1,0:T(8,128)(2,1)}), bf16[8,64,640]{2,1,0:T(8,128)(2,1)}, u32[]{:S(2)}, u32[]{:S(2)}) async-start(bf16[8,64,640]{2,1,0:T(8,128)(2,1)} %shard_map.65), calls=%async_computation | async-start | bytes 1310720 | tf_op jit(solution)/shard_map/all_to_all | solution.py:364
  12.6 1.9 %collective-permute-start = (bf16[8,64,640]{2,1,0:T(8,128)(2,1)S(1)}, bf16[8,64,640]{2,1,0:T(8,128)(2,1)S(1)}, u32[]{:S(2)}, u32[]{:S(2)}) collective-permute-start(bf16[8,64,640]{2,1,0:T(8,128)(2,1)S(1)} %shard_map.64), channel_id=1, source_target_pairs={{0,8},{8,0},{1,9},{9,1},{2,10},{10,2},{3,11},{11,3},{4,12},{12,4},... | collective-permute-start | bytes 1966088 | tf_op jit(solution)/shard_map/ppermute | solution.py:126
  14.5 3.7 %collective-permute-start.7 = (bf16[64,1024]{1,0:T(8,128)(2,1)S(1)}, bf16[64,1024]{1,0:T(8,128)(2,1)S(1)}, u32[]{:S(2)}, u32[]{:S(2)}) collective-permute-start(bf16[64,1024]{1,0:T(8,128)(2,1)S(1)} %bitcast.20), channel_id=1, source_target_pairs={{0,32},{32,0},{1,33},{33,1},{2,34},{34,2},{3,35},{35,3},{4,36},{36... | collective-permute-start | bytes 393224 | tf_op jit(solution)/shard_map/ppermute | solution.py:126
  18.4 7.6 %collective-permute-done.7.other_ref = bf16[64,1024]{1,0:T(8,128)(2,1)S(1)} collective-permute-done((bf16[64,1024]{1,0:T(8,128)(2,1)S(1)}, bf16[64,1024]{1,0:T(8,128)(2,1)S(1)}, u32[]{:S(2)}, u32[]{:S(2)}) %collective-permute-start.7) | collective-permute-done | bytes 131104 | tf_op jit(solution)/shard_map/ppermute | solution.py:126
  28.8 5.9 %all-to-all-start.1 = ((bf16[8,2,64,1024]{3,2,1,0:T(8,128)(2,1)}), bf16[8,2,64,1024]{3,2,1,0:T(8,128)(2,1)S(1)}, u32[]{:S(2)}, u32[]{:S(2)}) async-start(bf16[8,2,64,1024]{3,2,1,0:T(8,128)(2,1)} %shard_map.71), calls=%async_computation.1 | async-start | bytes 4194304 | tf_op jit(solution)/shard_map/all_to_all | solution.py:371
  34.7 1.9 %collective-permute-start.3 = (bf16[512,640]{1,0:T(8,128)(2,1)}, bf16[512,640]{1,0:T(8,128)(2,1)S(1)}, u32[]{:S(2)}, u32[]{:S(2)}) collective-permute-start(bf16[512,640]{1,0:T(8,128)(2,1)} %bitcast.7.key_ref), channel_id=1, source_target_pairs={{0,8},{8,0},{1,9},{9,1},{2,10},{10,2},{3,11},{11,3},{4,12},{12,4},... | collective-permute-start | bytes 1966088 | tf_op jit(solution)/shard_map/ppermute | solution.py:126
  36.6 3.3 %collective-permute-start.1 = (bf16[512,640]{1,0:T(8,128)(2,1)}, bf16[512,640]{1,0:T(8,128)(2,1)S(1)}, u32[]{:S(2)}, u32[]{:S(2)}) collective-permute-start(bf16[512,640]{1,0:T(8,128)(2,1)} %bitcast.7.key_ref), channel_id=1, source_target_pairs={{0,16},{8,60},{16,32},{24,8},{32,48},{40,24},{48,4},{56,40},{4,20}... | collective-permute-start | bytes 1966088 | tf_op jit(solution)/shard_map/ppermute | solution.py:122
  40.7 4.3 %collective-permute-start.4 = (bf16[512,640]{1,0:T(8,128)(2,1)S(1)}, bf16[512,640]{1,0:T(8,128)(2,1)S(1)}, u32[]{:S(2)}, u32[]{:S(2)}) collective-permute-start(bf16[512,640]{1,0:T(8,128)(2,1)S(1)} %collective-permute-done.3), channel_id=1, source_target_pairs={{0,16},{8,60},{16,32},{24,8},{32,48},{40,24},{48,4},{56,40},{4,20}... | collective-permute-start | bytes 1966088 | tf_op jit(solution)/shard_map/ppermute | solution.py:122
  45.0 5.8 %shard_map.66 = (f32[8,128,128]{2,1,0:T(8,128)}, f32[8,128,128]{2,1,0:T(8,128)}, f32[8,128,128]{2,1,0:T(8,128)}) custom-call(s32[8]{0:T(128)} %bitcast.24, bf16[8,128,640]{2,1,0:T(8,128)(2,1)} %copy-done, bf16[512,640]{1,0:T(8,128)(2,1)} %bitcast.7.key_ref, bf16[8,512,128]{2,1,0:T(8,128)(2,1)} %up_ref.7), custom_call_target="tpu_custom_call" | custom-call | flops 3623878656 | bytes 14548992 | tf_op jit(solution)/shard_map/pallas_call | solution.py:219
  50.7 4.6 %collective-permute-done.1.key_ref = bf16[512,640]{1,0:T(8,128)(2,1)S(1)} collective-permute-done((bf16[512,640]{1,0:T(8,128)(2,1)}, bf16[512,640]{1,0:T(8,128)(2,1)S(1)}, u32[]{:S(2)}, u32[]{:S(2)}) %collective-permute-start.1) | collective-permute-done | bytes 655392 | tf_op jit(solution)/shard_map/ppermute | solution.py:122
  55.4 1.9 %collective-permute-start.2 = (bf16[512,640]{1,0:T(8,128)(2,1)S(1)}, bf16[512,640]{1,0:T(8,128)(2,1)S(1)}, u32[]{:S(2)}, u32[]{:S(2)}) collective-permute-start(bf16[512,640]{1,0:T(8,128)(2,1)S(1)} %collective-permute-done.1.key_ref), channel_id=1, source_target_pairs={{0,16},{8,60},{16,32},{24,8},{32,48},{40,24},{48,4},{56,40},{4,20}... | collective-permute-start | bytes 1966088 | tf_op jit(solution)/shard_map/ppermute | solution.py:122
  60.5 2.7 %shard_map.67 = (f32[8,128,128]{2,1,0:T(8,128)S(1)}, f32[8,128,128]{2,1,0:T(8,128)S(1)}, f32[8,128,128]{2,1,0:T(8,128)S(1)}) custom-call(s32[8]{0:T(128)S(1)} %bitcast.25, bf16[8,128,640]{2,1,0:T(8,128)(2,1)S(1)} %copy-done.1, bf16[512,640]{1,0:T(8,128)(2,1)S(1)} %collective-permute-done.1.key_ref, bf16[8,512,128]{2,1,0:T(8,128)(2,1)S(1)} %copy-done.2, ...), custom_call_target="tpu_custom_call" | custom-call | flops 3623878656 | bytes 14548992 | tf_op jit(solution)/shard_map/pallas_call | solution.py:219
  63.1 2.7 %shard_map.68 = (f32[8,128,128]{2,1,0:T(8,128)S(1)}, f32[8,128,128]{2,1,0:T(8,128)S(1)}, f32[8,128,128]{2,1,0:T(8,128)S(1)}) custom-call(s32[8]{0:T(128)S(1)} %bitcast.26, bf16[8,128,640]{2,1,0:T(8,128)(2,1)S(1)} %copy-done.1, bf16[512,640]{1,0:T(8,128)(2,1)S(1)} %collective-permute-done.4.key_ref, bf16[8,512,128]{2,1,0:T(8,128)(2,1)S(1)} %copy-done.2, ...), custom_call_target="tpu_custom_call" | custom-call | flops 3623878656 | bytes 14548992 | tf_op jit(solution)/shard_map/pallas_call | solution.py:219
  65.8 3.6 %collective-permute-done.2.key_ref = bf16[512,640]{1,0:T(8,128)(2,1)S(1)} collective-permute-done((bf16[512,640]{1,0:T(8,128)(2,1)S(1)}, bf16[512,640]{1,0:T(8,128)(2,1)S(1)}, u32[]{:S(2)}, u32[]{:S(2)}) %collective-permute-start.2) | collective-permute-done | bytes 655392 | tf_op jit(solution)/shard_map/ppermute | solution.py:122
  69.4 2.9 %shard_map.69.own_ref = bf16[2,64,1152]{2,1,0:T(8,128)(2,1)S(1)} custom-call(s32[8]{0:T(128)S(1)} %bitcast.27, bf16[8,128,640]{2,1,0:T(8,128)(2,1)S(1)} %copy-done.1, bf16[512,640]{1,0:T(8,128)(2,1)S(1)} %collective-permute-done.2.key_ref, bf16[8,512,128]{2,1,0:T(8,128)(2,1)S(1)} %copy-done.2, f32[8,128,128]{2,1,0:T(8,128)S(1)} %get-tuple-element.22.refs_0_, ...), custom_call_target="tpu_custom_call" | custom-call | flops 1207959552 | bytes 4849664 | tf_op jit(solution)/shard_map/pallas_call | solution.py:219
  72.3 1.9 %collective-permute-start.5 = (bf16[2,64,1152]{2,1,0:T(8,128)(2,1)S(1)}, bf16[2,64,1152]{2,1,0:T(8,128)(2,1)S(1)}, u32[]{:S(2)}, u32[]{:S(2)}) collective-permute-start(bf16[2,64,1152]{2,1,0:T(8,128)(2,1)S(1)} %shard_map.69.own_ref), channel_id=1, source_target_pairs={{0,8},{8,0},{1,9},{9,1},{2,10},{10,2},{3,11},{11,3},{4,12},{12,4},... | collective-permute-start | bytes 884744 | tf_op jit(solution)/shard_map/ppermute | solution.py:126
  76.3 1.9 %collective-permute-start.6 = (bf16[128,1024]{1,0:T(8,128)(2,1)S(1)}, bf16[128,1024]{1,0:T(8,128)(2,1)S(1)}, u32[]{:S(2)}, u32[]{:S(2)}) collective-permute-start(bf16[128,1024]{1,0:T(8,128)(2,1)S(1)} %shard_map.70), channel_id=1, source_target_pairs={{0,16},{16,0},{1,17},{17,1},{2,18},{18,2},{3,19},{19,3},{4,20},{20... | collective-permute-start | bytes 786440 | tf_op jit(solution)/shard_map/ppermute | solution.py:126
  78.3 8.2 %collective-permute-done.6 = bf16[128,1024]{1,0:T(8,128)(2,1)S(1)} collective-permute-done((bf16[128,1024]{1,0:T(8,128)(2,1)S(1)}, bf16[128,1024]{1,0:T(8,128)(2,1)S(1)}, u32[]{:S(2)}, u32[]{:S(2)}) %collective-permute-start.6) | collective-permute-done | bytes 262176 | tf_op jit(solution)/shard_map/ppermute | solution.py:126
  86.6 2.6 %shard_map.72 = bf16[4,2,2,2,64,128]{5,4,3,2,1,0:T(8,128)(2,1)} custom-call(s32[2]{0:T(128)S(1)} %pad_add_fusion.slots_ref, bf16[256,1024]{1,0:T(8,128)(2,1)S(1)} %pad_maximum_fusion.1.v_ref, bf16[8,128,1024]{2,1,0:T(8,128)(2,1)S(1)} %bitcast.16), custom_call_target="tpu_custom_call" | custom-call | flops 536870912 | bytes 2097152 | tf_op jit(solution)/shard_map/pallas_call | solution.py:288
  89.2 4.4 %all-to-all-start.2 = ((bf16[16,2,64,128]{3,2,1,0:T(8,128)(2,1)}), bf16[16,2,64,128]{3,2,1,0:T(8,128)(2,1)S(1)}, u32[]{:S(2)}, u32[]{:S(2)}) async-start(bf16[16,2,64,128]{3,2,1,0:T(8,128)(2,1)} %bitcast.12), calls=%async_computation.2 | async-start | bytes 1048576 | tf_op jit(solution)/shard_map/all_to_all | solution.py:387
  93.6 10.9 %all-to-all-done.2 = bf16[16,2,64,128]{3,2,1,0:T(8,128)(2,1)S(1)} async-done(((bf16[16,2,64,128]{3,2,1,0:T(8,128)(2,1)}), bf16[16,2,64,128]{3,2,1,0:T(8,128)(2,1)S(1)}, u32[]{:S(2)}, u32[]{:S(2)}) %all-to-all-start.2) | async-done | bytes 524320 | tf_op jit(solution)/shard_map/all_to_all | solution.py:387
  104.6 9.2 %collective-permute-start.8 = (bf16[64,512]{1,0:T(8,128)(2,1)S(1)}, bf16[64,512]{1,0:T(8,128)(2,1)S(1)}, u32[]{:S(2)}, u32[]{:S(2)}) collective-permute-start(bf16[64,512]{1,0:T(8,128)(2,1)S(1)} %get-tuple-element.26), channel_id=1, source_target_pairs={{0,4},{4,0},{1,5},{5,1},{2,6},{6,2},{3,7},{7,3},{8,12},{12,8},{9,1... | collective-permute-start | bytes 196616 | tf_op jit(solution)/shard_map/ppermute | solution.py:126
  113.9 2.5 %collective-permute-done.8 = bf16[64,512]{1,0:T(8,128)(2,1)S(1)} collective-permute-done((bf16[64,512]{1,0:T(8,128)(2,1)S(1)}, bf16[64,512]{1,0:T(8,128)(2,1)S(1)}, u32[]{:S(2)}, u32[]{:S(2)}) %collective-permute-start.8) | collective-permute-done | bytes 65568 | tf_op jit(solution)/shard_map/ppermute | solution.py:126
  (39 shorter events, 10.1 us)
Async XLA Ops:
  0.0 12.3 %copy-start.4 = (s32[64]{0:T(128)S(1)}, s32[64]{0:T(128)}, u32[]{:S(2)}) copy-start(s32[64]{0:T(128)} %param.8) | copy-start | bytes 772
  0.0 12.2 %copy-start.9 = (bf16[64,8,576]{2,1,0:T(8,128)(2,1)S(1)}, bf16[64,8,576]{2,1,0:T(8,128)(2,1)}, u32[]{:S(2)}) copy-start(bf16[64,8,576]{2,1,0:T(8,128)(2,1)} %param.6) | copy-start | bytes 1769476
  2.1 12.4 %copy-start.3 = (bf16[1024,64]{0,1:T(8,128)(2,1)S(1)}, bf16[1024,64]{0,1:T(8,128)(2,1)}, u32[]{:S(2)}) copy-start(bf16[1024,64]{0,1:T(8,128)(2,1)} %param.11) | copy-start | bytes 393220
  2.1 26.6 %all-to-all-start = ((bf16[8,64,640]{2,1,0:T(8,128)(2,1)}), bf16[8,64,640]{2,1,0:T(8,128)(2,1)}, u32[]{:S(2)}, u32[]{:S(2)}) async-start(bf16[8,64,640]{2,1,0:T(8,128)(2,1)} %shard_map.65), calls=%async_computation | async-start | bytes 1310720 | tf_op jit(solution)/shard_map/all_to_all | solution.py:364
  12.6 5.7 %collective-permute-start = (bf16[8,64,640]{2,1,0:T(8,128)(2,1)S(1)}, bf16[8,64,640]{2,1,0:T(8,128)(2,1)S(1)}, u32[]{:S(2)}, u32[]{:S(2)}) collective-permute-start(bf16[8,64,640]{2,1,0:T(8,128)(2,1)S(1)} %shard_map.64), channel_id=1, source_target_pairs={{0,8},{8,0},{1,9},{9,1},{2,10},{10,2},{3,11},{11,3},{4,12},{12,4},... | collective-permute-start | bytes 1966088 | tf_op jit(solution)/shard_map/ppermute | solution.py:126
  14.5 11.5 %collective-permute-start.7 = (bf16[64,1024]{1,0:T(8,128)(2,1)S(1)}, bf16[64,1024]{1,0:T(8,128)(2,1)S(1)}, u32[]{:S(2)}, u32[]{:S(2)}) collective-permute-start(bf16[64,1024]{1,0:T(8,128)(2,1)S(1)} %bitcast.20), channel_id=1, source_target_pairs={{0,32},{32,0},{1,33},{33,1},{2,34},{34,2},{3,35},{35,3},{4,36},{36... | collective-permute-start | bytes 393224 | tf_op jit(solution)/shard_map/ppermute | solution.py:126
  18.4 10.4 %copy-start = (bf16[8,128,640]{2,1,0:T(8,128)(2,1)}, bf16[8,128,640]{2,1,0:T(8,128)(2,1)S(1)}, u32[]{:S(2)}) copy-start(bf16[8,128,640]{2,1,0:T(8,128)(2,1)S(1)} %pad_maximum_fusion.q_ref) | copy-start | bytes 3932164
  27.5 12.5 %copy-start.10 = (s32[8]{0:T(128)S(1)}, s32[8]{0:T(128)}, u32[]{:S(2)}) copy-start(s32[8]{0:T(128)} %param.9) | copy-start | bytes 100
  28.8 57.8 %all-to-all-start.1 = ((bf16[8,2,64,1024]{3,2,1,0:T(8,128)(2,1)}), bf16[8,2,64,1024]{3,2,1,0:T(8,128)(2,1)S(1)}, u32[]{:S(2)}, u32[]{:S(2)}) async-start(bf16[8,2,64,1024]{3,2,1,0:T(8,128)(2,1)} %shard_map.71), calls=%async_computation.1 | async-start | bytes 4194304 | tf_op jit(solution)/shard_map/all_to_all | solution.py:371
  34.7 5.9 %collective-permute-start.3 = (bf16[512,640]{1,0:T(8,128)(2,1)}, bf16[512,640]{1,0:T(8,128)(2,1)S(1)}, u32[]{:S(2)}, u32[]{:S(2)}) collective-permute-start(bf16[512,640]{1,0:T(8,128)(2,1)} %bitcast.7.key_ref), channel_id=1, source_target_pairs={{0,8},{8,0},{1,9},{9,1},{2,10},{10,2},{3,11},{11,3},{4,12},{12,4},... | collective-permute-start | bytes 1966088 | tf_op jit(solution)/shard_map/ppermute | solution.py:126
  36.6 18.7 %collective-permute-start.1 = (bf16[512,640]{1,0:T(8,128)(2,1)}, bf16[512,640]{1,0:T(8,128)(2,1)S(1)}, u32[]{:S(2)}, u32[]{:S(2)}) collective-permute-start(bf16[512,640]{1,0:T(8,128)(2,1)} %bitcast.7.key_ref), channel_id=1, source_target_pairs={{0,16},{8,60},{16,32},{24,8},{32,48},{40,24},{48,4},{56,40},{4,20}... | collective-permute-start | bytes 1966088 | tf_op jit(solution)/shard_map/ppermute | solution.py:122
  40.7 22.5 %collective-permute-start.4 = (bf16[512,640]{1,0:T(8,128)(2,1)S(1)}, bf16[512,640]{1,0:T(8,128)(2,1)S(1)}, u32[]{:S(2)}, u32[]{:S(2)}) collective-permute-start(bf16[512,640]{1,0:T(8,128)(2,1)S(1)} %collective-permute-done.3), channel_id=1, source_target_pairs={{0,16},{8,60},{16,32},{24,8},{32,48},{40,24},{48,4},{56,40},{4,20}... | collective-permute-start | bytes 1966088 | tf_op jit(solution)/shard_map/ppermute | solution.py:122
  44.9 12.4 %copy-start.1 = (bf16[8,128,640]{2,1,0:T(8,128)(2,1)S(1)}, bf16[8,128,640]{2,1,0:T(8,128)(2,1)}, u32[]{:S(2)}) copy-start(bf16[8,128,640]{2,1,0:T(8,128)(2,1)} %copy-done) | copy-start | bytes 3932164
  44.9 12.4 %copy-start.2 = (bf16[8,512,128]{2,1,0:T(8,128)(2,1)S(1)}, bf16[8,512,128]{2,1,0:T(8,128)(2,1)}, u32[]{:S(2)}) copy-start(bf16[8,512,128]{2,1,0:T(8,128)(2,1)} %up_ref.7) | copy-start | bytes 3145732
  45.0 12.4 %copy-start.5 = (s32[8,1]{0,1:T(1,128)S(1)}, s32[8,1]{0,1:T(1,128)}, u32[]{:S(2)}) copy-start(s32[8,1]{0,1:T(1,128)} %reduce-window.9) | copy-start | bytes 100
  55.4 14.0 %collective-permute-start.2 = (bf16[512,640]{1,0:T(8,128)(2,1)S(1)}, bf16[512,640]{1,0:T(8,128)(2,1)S(1)}, u32[]{:S(2)}, u32[]{:S(2)}) collective-permute-start(bf16[512,640]{1,0:T(8,128)(2,1)S(1)} %collective-permute-done.1.key_ref), channel_id=1, source_target_pairs={{0,16},{8,60},{16,32},{24,8},{32,48},{40,24},{48,4},{56,40},{4,20}... | collective-permute-start | bytes 1966088 | tf_op jit(solution)/shard_map/ppermute | solution.py:122
  57.3 1.0 copy-start.6
  58.4 1.0 copy-start.7
  59.4 1.0 copy-start.8
  72.3 3.5 %collective-permute-start.5 = (bf16[2,64,1152]{2,1,0:T(8,128)(2,1)S(1)}, bf16[2,64,1152]{2,1,0:T(8,128)(2,1)S(1)}, u32[]{:S(2)}, u32[]{:S(2)}) collective-permute-start(bf16[2,64,1152]{2,1,0:T(8,128)(2,1)S(1)} %shard_map.69.own_ref), channel_id=1, source_target_pairs={{0,8},{8,0},{1,9},{9,1},{2,10},{10,2},{3,11},{11,3},{4,12},{12,4},... | collective-permute-start | bytes 884744 | tf_op jit(solution)/shard_map/ppermute | solution.py:126
  76.3 10.2 %collective-permute-start.6 = (bf16[128,1024]{1,0:T(8,128)(2,1)S(1)}, bf16[128,1024]{1,0:T(8,128)(2,1)S(1)}, u32[]{:S(2)}, u32[]{:S(2)}) collective-permute-start(bf16[128,1024]{1,0:T(8,128)(2,1)S(1)} %shard_map.70), channel_id=1, source_target_pairs={{0,16},{16,0},{1,17},{17,1},{2,18},{18,2},{3,19},{19,3},{4,20},{20... | collective-permute-start | bytes 786440 | tf_op jit(solution)/shard_map/ppermute | solution.py:126
  89.2 15.3 %all-to-all-start.2 = ((bf16[16,2,64,128]{3,2,1,0:T(8,128)(2,1)}), bf16[16,2,64,128]{3,2,1,0:T(8,128)(2,1)S(1)}, u32[]{:S(2)}, u32[]{:S(2)}) async-start(bf16[16,2,64,128]{3,2,1,0:T(8,128)(2,1)} %bitcast.12), calls=%async_computation.2 | async-start | bytes 1048576 | tf_op jit(solution)/shard_map/all_to_all | solution.py:387
  104.6 11.7 %collective-permute-start.8 = (bf16[64,512]{1,0:T(8,128)(2,1)S(1)}, bf16[64,512]{1,0:T(8,128)(2,1)S(1)}, u32[]{:S(2)}, u32[]{:S(2)}) collective-permute-start(bf16[64,512]{1,0:T(8,128)(2,1)S(1)} %get-tuple-element.26), channel_id=1, source_target_pairs={{0,4},{4,0},{1,5},{5,1},{2,6},{6,2},{3,7},{7,3},{8,12},{12,8},{9,1... | collective-permute-start | bytes 196616 | tf_op jit(solution)/shard_map/ppermute | solution.py:126

commit v8 on v7

--- a/solution.py
+++ b/solution.py
@@ -282,7 +282,7 @@
             out_ref[y % 4, at_near, at_core, y // 4] = part[k * toks : (k + 1) * toks]
 
 
-def project(near, core, v, w):
+def project(slots, v, w):
     blocks, cols, depth = w.shape
     toks = v.shape[0] // 4
     return pl.pallas_call(
@@ -296,11 +296,11 @@
             bytes_accessed=2 * blocks * cols * depth,
             transcendentals=0,
         ),
-    )(jnp.stack([near, core]), v, w)
-
-
-def add_x_kernel(here_ref, parts_ref, keep_ref, give_ref):
-    here = here_ref[0]
+    )(slots, v, w)
+
+
+def add_x_kernel(slots_ref, parts_ref, keep_ref, give_ref):
+    here = slots_ref[2]
     for whose, out_ref in ((1 - here, give_ref), (here, keep_ref)):
         for near in range(2):
             total = []
@@ -317,7 +317,7 @@
                 ).astype(out_ref.dtype)
 
 
-def add_x(here, parts):
+def add_x(slots, parts):
     toks, cols = parts.shape[4:]
     return pl.pallas_call(
         add_x_kernel,
@@ -328,7 +328,7 @@
             jax.ShapeDtypeStruct((toks, 4 * cols), parts.dtype),
         ],
         compiler_params=pltpu.CompilerParams(vmem_limit_bytes=VMEM),
-    )(here, parts)
+    )(slots, parts)
 
 
 def pair_kernel(far_ref, own_ref, other_ref, _, out_hbm, both_ref, sems):
@@ -383,12 +383,13 @@
 
     v = jnp.concatenate([values, swap(values, "zl_lat")], axis=0)
 
-    partial = project(near, core, v, w)
+    z_hi = lax.axis_index("z_hi").astype(jnp.int32)
+    slots = jnp.stack([near, core, z_hi])
+    partial = project(slots, v, w)
     parts = lax.all_to_all(
         partial.reshape((16,) + partial.shape[3:]), ("x", "zl_lat", "core"), 0, 0
     )
-    z_hi = lax.axis_index("z_hi").astype(jnp.int32)
-    keep, give = add_x(z_hi.reshape(1), parts.reshape(partial.shape))
+    keep, give = add_x(slots, parts.reshape(partial.shape))
     return (keep + swap(give, "z_hi").astype(jnp.float32)).astype(jnp.bfloat16)
 
 

time: 118 us -> 117 us (level)
  blocking collectives: 0 us -> 15.1 us
  waiting for transfers between devices: 40.2 us -> 29.4 us
  starting transfers between devices: 50.5 us -> 46.1 us
    all_to_all x0 -> x1, blocking collectives: none -> 15.1 us  [on_device(): lax.all_to_all(partial.reshape((16,) + partial.shape[3:]), ('x', 'zl_lat'...]
    all_to_all x1 -> x0, waiting for transfers between devices: 10.9 us -> none  [on_device(): lax.all_to_all(partial.reshape((16,) + partial.shape[3:]), ('x', 'zl_lat'...]
    all_to_all x1 -> x0, starting transfers between devices: 4.4 us -> none  [on_device(): lax.all_to_all(partial.reshape((16,) + partial.shape[3:]), ('x', 'zl_lat'...]
  transfers between devices with their start and end apart: 12 -> 11, of which waited for: 8 -> 7; matrix products, arithmetic and copies ran while one was open for 1% -> 1% of each run, Pallas kernels for 14% -> 14%
where the time goes in v8:
time: 117 us; the launch traced here: 116 us
  starting transfers between devices  46.1 us (39%)
  waiting for transfers between devices  29.4 us (25%)
  Pallas kernels  20.9 us (18%)
  blocking collectives  15.1 us (13%)
  local copies, waits for them, and re-layouts  3.23 us (3%)
  other arithmetic  1.56 us (1%)
    ppermute x6, starting transfers between devices, swap(): return lax.ppermute(x, axis, [(0, 1), (1, 0)])  20.6 us
    ppermute x6, waiting for transfers between devices, swap(): return lax.ppermute(x, axis, [(0, 1), (1, 0)])  19.8 us
    all_to_all x1, blocking collectives, on_device(): lax.all_to_all(partial.reshape((16,) + partial.shape[3:]), ('x', 'zl_lat'...  15.1 us
    pallas_call x4, Pallas kernels, attend(): pl.pallas_call(functools.partial(attend_kernel, group, first, last), in_s...  14 us
    all_to_all x1, starting transfers between devices, on_device(): along_y = lax.all_to_all(key_rows, 'y', 0, 0).reshape(8 * toks, WIDTH)  10 us
    ppermute x3, starting transfers between devices, shift_z(): return lax.ppermute(x, ('zh_lat', 'zl_lat', 'core', 'z_hi'), perm)  9.5 us
    ppermute x3, waiting for transfers between devices, shift_z(): return lax.ppermute(x, ('zh_lat', 'zl_lat', 'core', 'z_hi'), perm)  8.23 us
    all_to_all x1, starting transfers between devices, on_device(): w = lax.all_to_all(w, 'y', 0, 0)  5.93 us
  transfers between devices with their start and end apart: 11, of which 7 were waited for; matrix products, arithmetic and copies ran while one was open for 1% of the time, Pallas kernels for 14%

profile of v8, /device:TPU:8, one launch (start us, length us, event | category | flops | bytes accessed | tf_op | source)
XLA Modules:
  0.0 116.5 jit_solution(16682612679128338157)
XLA Ops:
  0.0 2.1 %shard_map.65 = bf16[8,64,640]{2,1,0:T(8,128)(2,1)} custom-call(s32[1,64]{1,0:T(1,128)} %bitcast.23, bf16[64,576]{1,0:T(8,128)(2,1)} %latents_hbm.1), custom_call_target="tpu_custom_call" | custom-call | tf_op jit(solution)/shard_map/pallas_call | solution.py:76
  2.1 10.0 %all-to-all-start = ((bf16[8,64,640]{2,1,0:T(8,128)(2,1)}), bf16[8,64,640]{2,1,0:T(8,128)(2,1)}, u32[]{:S(2)}, u32[]{:S(2)}) async-start(bf16[8,64,640]{2,1,0:T(8,128)(2,1)} %shard_map.65), calls=%async_computation | async-start | bytes 1310720 | tf_op jit(solution)/shard_map/all_to_all | solution.py:364
  12.6 1.9 %collective-permute-start = (bf16[8,64,640]{2,1,0:T(8,128)(2,1)S(1)}, bf16[8,64,640]{2,1,0:T(8,128)(2,1)S(1)}, u32[]{:S(2)}, u32[]{:S(2)}) collective-permute-start(bf16[8,64,640]{2,1,0:T(8,128)(2,1)S(1)} %shard_map.64), channel_id=1, source_target_pairs={{0,8},{8,0},{1,9},{9,1},{2,10},{10,2},{3,11},{11,3},{4,12},{12,4},... | collective-permute-start | bytes 1966088 | tf_op jit(solution)/shard_map/ppermute | solution.py:126
  14.5 3.7 %collective-permute-start.7 = (bf16[64,1024]{1,0:T(8,128)(2,1)S(1)}, bf16[64,1024]{1,0:T(8,128)(2,1)S(1)}, u32[]{:S(2)}, u32[]{:S(2)}) collective-permute-start(bf16[64,1024]{1,0:T(8,128)(2,1)S(1)} %bitcast.21), channel_id=1, source_target_pairs={{0,32},{32,0},{1,33},{33,1},{2,34},{34,2},{3,35},{35,3},{4,36},{36... | collective-permute-start | bytes 393224 | tf_op jit(solution)/shard_map/ppermute | solution.py:126
  18.4 7.6 %collective-permute-done.7.other_ref = bf16[64,1024]{1,0:T(8,128)(2,1)S(1)} collective-permute-done((bf16[64,1024]{1,0:T(8,128)(2,1)S(1)}, bf16[64,1024]{1,0:T(8,128)(2,1)S(1)}, u32[]{:S(2)}, u32[]{:S(2)}) %collective-permute-start.7) | collective-permute-done | bytes 131104 | tf_op jit(solution)/shard_map/ppermute | solution.py:126
  28.8 5.9 %all-to-all-start.1 = ((bf16[8,2,64,1024]{3,2,1,0:T(8,128)(2,1)}), bf16[8,2,64,1024]{3,2,1,0:T(8,128)(2,1)S(1)}, u32[]{:S(2)}, u32[]{:S(2)}) async-start(bf16[8,2,64,1024]{3,2,1,0:T(8,128)(2,1)} %shard_map.71), calls=%async_computation.1 | async-start | bytes 4194304 | tf_op jit(solution)/shard_map/all_to_all | solution.py:371
  34.7 1.9 %collective-permute-start.3 = (bf16[512,640]{1,0:T(8,128)(2,1)}, bf16[512,640]{1,0:T(8,128)(2,1)S(1)}, u32[]{:S(2)}, u32[]{:S(2)}) collective-permute-start(bf16[512,640]{1,0:T(8,128)(2,1)} %bitcast.7.key_ref), channel_id=1, source_target_pairs={{0,8},{8,0},{1,9},{9,1},{2,10},{10,2},{3,11},{11,3},{4,12},{12,4},... | collective-permute-start | bytes 1966088 | tf_op jit(solution)/shard_map/ppermute | solution.py:126
  36.6 3.3 %collective-permute-start.1 = (bf16[512,640]{1,0:T(8,128)(2,1)}, bf16[512,640]{1,0:T(8,128)(2,1)S(1)}, u32[]{:S(2)}, u32[]{:S(2)}) collective-permute-start(bf16[512,640]{1,0:T(8,128)(2,1)} %bitcast.7.key_ref), channel_id=1, source_target_pairs={{0,16},{8,60},{16,32},{24,8},{32,48},{40,24},{48,4},{56,40},{4,20}... | collective-permute-start | bytes 1966088 | tf_op jit(solution)/shard_map/ppermute | solution.py:122
  40.7 4.3 %collective-permute-start.4 = (bf16[512,640]{1,0:T(8,128)(2,1)S(1)}, bf16[512,640]{1,0:T(8,128)(2,1)S(1)}, u32[]{:S(2)}, u32[]{:S(2)}) collective-permute-start(bf16[512,640]{1,0:T(8,128)(2,1)S(1)} %collective-permute-done.3), channel_id=1, source_target_pairs={{0,16},{8,60},{16,32},{24,8},{32,48},{40,24},{48,4},{56,40},{4,20}... | collective-permute-start | bytes 1966088 | tf_op jit(solution)/shard_map/ppermute | solution.py:122
  45.0 5.8 %shard_map.66 = (f32[8,128,128]{2,1,0:T(8,128)}, f32[8,128,128]{2,1,0:T(8,128)}, f32[8,128,128]{2,1,0:T(8,128)}) custom-call(s32[8]{0:T(128)} %bitcast.25, bf16[8,128,640]{2,1,0:T(8,128)(2,1)} %copy-done, bf16[512,640]{1,0:T(8,128)(2,1)} %bitcast.7.key_ref, bf16[8,512,128]{2,1,0:T(8,128)(2,1)} %up_ref.7), custom_call_target="tpu_custom_call" | custom-call | flops 3623878656 | bytes 14548992 | tf_op jit(solution)/shard_map/pallas_call | solution.py:219
  50.7 4.6 %collective-permute-done.1.key_ref = bf16[512,640]{1,0:T(8,128)(2,1)S(1)} collective-permute-done((bf16[512,640]{1,0:T(8,128)(2,1)}, bf16[512,640]{1,0:T(8,128)(2,1)S(1)}, u32[]{:S(2)}, u32[]{:S(2)}) %collective-permute-start.1) | collective-permute-done | bytes 655392 | tf_op jit(solution)/shard_map/ppermute | solution.py:122
  55.4 1.9 %collective-permute-start.2 = (bf16[512,640]{1,0:T(8,128)(2,1)S(1)}, bf16[512,640]{1,0:T(8,128)(2,1)S(1)}, u32[]{:S(2)}, u32[]{:S(2)}) collective-permute-start(bf16[512,640]{1,0:T(8,128)(2,1)S(1)} %collective-permute-done.1.key_ref), channel_id=1, source_target_pairs={{0,16},{8,60},{16,32},{24,8},{32,48},{40,24},{48,4},{56,40},{4,20}... | collective-permute-start | bytes 1966088 | tf_op jit(solution)/shard_map/ppermute | solution.py:122
  60.5 2.7 %shard_map.67 = (f32[8,128,128]{2,1,0:T(8,128)S(1)}, f32[8,128,128]{2,1,0:T(8,128)S(1)}, f32[8,128,128]{2,1,0:T(8,128)S(1)}) custom-call(s32[8]{0:T(128)S(1)} %bitcast.26, bf16[8,128,640]{2,1,0:T(8,128)(2,1)S(1)} %copy-done.1, bf16[512,640]{1,0:T(8,128)(2,1)S(1)} %collective-permute-done.1.key_ref, bf16[8,512,128]{2,1,0:T(8,128)(2,1)S(1)} %copy-done.2, ...), custom_call_target="tpu_custom_call" | custom-call | flops 3623878656 | bytes 14548992 | tf_op jit(solution)/shard_map/pallas_call | solution.py:219
  63.1 2.7 %shard_map.68 = (f32[8,128,128]{2,1,0:T(8,128)S(1)}, f32[8,128,128]{2,1,0:T(8,128)S(1)}, f32[8,128,128]{2,1,0:T(8,128)S(1)}) custom-call(s32[8]{0:T(128)S(1)} %bitcast.27, bf16[8,128,640]{2,1,0:T(8,128)(2,1)S(1)} %copy-done.1, bf16[512,640]{1,0:T(8,128)(2,1)S(1)} %collective-permute-done.4.key_ref, bf16[8,512,128]{2,1,0:T(8,128)(2,1)S(1)} %copy-done.2, ...), custom_call_target="tpu_custom_call" | custom-call | flops 3623878656 | bytes 14548992 | tf_op jit(solution)/shard_map/pallas_call | solution.py:219
  65.8 3.6 %collective-permute-done.2.key_ref = bf16[512,640]{1,0:T(8,128)(2,1)S(1)} collective-permute-done((bf16[512,640]{1,0:T(8,128)(2,1)S(1)}, bf16[512,640]{1,0:T(8,128)(2,1)S(1)}, u32[]{:S(2)}, u32[]{:S(2)}) %collective-permute-start.2) | collective-permute-done | bytes 655392 | tf_op jit(solution)/shard_map/ppermute | solution.py:122
  69.4 2.9 %shard_map.69.own_ref = bf16[2,64,1152]{2,1,0:T(8,128)(2,1)S(1)} custom-call(s32[8]{0:T(128)S(1)} %bitcast.28, bf16[8,128,640]{2,1,0:T(8,128)(2,1)S(1)} %copy-done.1, bf16[512,640]{1,0:T(8,128)(2,1)S(1)} %collective-permute-done.2.key_ref, bf16[8,512,128]{2,1,0:T(8,128)(2,1)S(1)} %copy-done.2, f32[8,128,128]{2,1,0:T(8,128)S(1)} %get-tuple-element.22.refs_0_, ...), custom_call_target="tpu_custom_call" | custom-call | flops 1207959552 | bytes 4849664 | tf_op jit(solution)/shard_map/pallas_call | solution.py:219
  72.3 1.9 %collective-permute-start.5 = (bf16[2,64,1152]{2,1,0:T(8,128)(2,1)S(1)}, bf16[2,64,1152]{2,1,0:T(8,128)(2,1)S(1)}, u32[]{:S(2)}, u32[]{:S(2)}) collective-permute-start(bf16[2,64,1152]{2,1,0:T(8,128)(2,1)S(1)} %shard_map.69.own_ref), channel_id=1, source_target_pairs={{0,8},{8,0},{1,9},{9,1},{2,10},{10,2},{3,11},{11,3},{4,12},{12,4},... | collective-permute-start | bytes 884744 | tf_op jit(solution)/shard_map/ppermute | solution.py:126
  74.2 1.5 %collective-permute-done.5.other_ref = bf16[2,64,1152]{2,1,0:T(8,128)(2,1)S(1)} collective-permute-done((bf16[2,64,1152]{2,1,0:T(8,128)(2,1)S(1)}, bf16[2,64,1152]{2,1,0:T(8,128)(2,1)S(1)}, u32[]{:S(2)}, u32[]{:S(2)}) %collective-permute-start.5) | collective-permute-done | bytes 294944 | tf_op jit(solution)/shard_map/ppermute | solution.py:126
  76.3 1.9 %collective-permute-start.6 = (bf16[128,1024]{1,0:T(8,128)(2,1)S(1)}, bf16[128,1024]{1,0:T(8,128)(2,1)S(1)}, u32[]{:S(2)}, u32[]{:S(2)}) collective-permute-start(bf16[128,1024]{1,0:T(8,128)(2,1)S(1)} %shard_map.70), channel_id=1, source_target_pairs={{0,16},{16,0},{1,17},{17,1},{2,18},{18,2},{3,19},{19,3},{4,20},{20... | collective-permute-start | bytes 786440 | tf_op jit(solution)/shard_map/ppermute | solution.py:126
  78.3 8.2 %collective-permute-done.6 = bf16[128,1024]{1,0:T(8,128)(2,1)S(1)} collective-permute-done((bf16[128,1024]{1,0:T(8,128)(2,1)S(1)}, bf16[128,1024]{1,0:T(8,128)(2,1)S(1)}, u32[]{:S(2)}, u32[]{:S(2)}) %collective-permute-start.6) | collective-permute-done | bytes 262176 | tf_op jit(solution)/shard_map/ppermute | solution.py:126
  86.6 1.8 %shard_map.72 = bf16[4,2,2,2,64,128]{5,4,3,2,1,0:T(8,128)(2,1)S(1)} custom-call(s32[3]{0:T(128)S(1)} %pad_add_fusion.slots_ref, bf16[256,1024]{1,0:T(8,128)(2,1)S(1)} %pad_maximum_fusion.1.v_ref, bf16[8,128,1024]{2,1,0:T(8,128)(2,1)S(1)} %bitcast.16), custom_call_target="tpu_custom_call" | custom-call | flops 536870912 | bytes 2097152 | tf_op jit(solution)/shard_map/pallas_call | solution.py:288
  88.4 15.1 %all_to_all.15 = bf16[16,2,64,128]{3,2,1,0:T(8,128)(2,1)S(1)} all-to-all(bf16[16,2,64,128]{3,2,1,0:T(8,128)(2,1)S(1)} %bitcast.20), channel_id=1, replica_groups=mesh['y'=8,'zh_lat'=2,'zl_lat'=2,'core'=2,'z_hi'=2,'x'=4] {'x','zl_lat',..., dimensions={0} | all-to-all | bytes 1048576 | tf_op jit(solution)/shard_map/all_to_all | solution.py:389
  104.2 9.2 %collective-permute-start.8 = (bf16[64,512]{1,0:T(8,128)(2,1)S(1)}, bf16[64,512]{1,0:T(8,128)(2,1)S(1)}, u32[]{:S(2)}, u32[]{:S(2)}) collective-permute-start(bf16[64,512]{1,0:T(8,128)(2,1)S(1)} %get-tuple-element.26), channel_id=1, source_target_pairs={{0,4},{4,0},{1,5},{5,1},{2,6},{6,2},{3,7},{7,3},{8,12},{12,8},{9,1... | collective-permute-start | bytes 196616 | tf_op jit(solution)/shard_map/ppermute | solution.py:126
  113.4 2.5 %collective-permute-done.8 = bf16[64,512]{1,0:T(8,128)(2,1)S(1)} collective-permute-done((bf16[64,512]{1,0:T(8,128)(2,1)S(1)}, bf16[64,512]{1,0:T(8,128)(2,1)S(1)}, u32[]{:S(2)}, u32[]{:S(2)}) %collective-permute-start.8) | collective-permute-done | bytes 65568 | tf_op jit(solution)/shard_map/ppermute | solution.py:126
  (38 shorter events, 9.1 us)
Async XLA Ops:
  0.0 12.3 %copy-start.4 = (s32[64]{0:T(128)S(1)}, s32[64]{0:T(128)}, u32[]{:S(2)}) copy-start(s32[64]{0:T(128)} %param.8) | copy-start | bytes 772
  0.0 12.2 %copy-start.9 = (bf16[64,8,576]{2,1,0:T(8,128)(2,1)S(1)}, bf16[64,8,576]{2,1,0:T(8,128)(2,1)}, u32[]{:S(2)}) copy-start(bf16[64,8,576]{2,1,0:T(8,128)(2,1)} %param.6) | copy-start | bytes 1769476
  2.1 12.4 %copy-start.3 = (bf16[1024,64]{0,1:T(8,128)(2,1)S(1)}, bf16[1024,64]{0,1:T(8,128)(2,1)}, u32[]{:S(2)}) copy-start(bf16[1024,64]{0,1:T(8,128)(2,1)} %param.11) | copy-start | bytes 393220
  2.1 26.6 %all-to-all-start = ((bf16[8,64,640]{2,1,0:T(8,128)(2,1)}), bf16[8,64,640]{2,1,0:T(8,128)(2,1)}, u32[]{:S(2)}, u32[]{:S(2)}) async-start(bf16[8,64,640]{2,1,0:T(8,128)(2,1)} %shard_map.65), calls=%async_computation | async-start | bytes 1310720 | tf_op jit(solution)/shard_map/all_to_all | solution.py:364
  12.6 5.7 %collective-permute-start = (bf16[8,64,640]{2,1,0:T(8,128)(2,1)S(1)}, bf16[8,64,640]{2,1,0:T(8,128)(2,1)S(1)}, u32[]{:S(2)}, u32[]{:S(2)}) collective-permute-start(bf16[8,64,640]{2,1,0:T(8,128)(2,1)S(1)} %shard_map.64), channel_id=1, source_target_pairs={{0,8},{8,0},{1,9},{9,1},{2,10},{10,2},{3,11},{11,3},{4,12},{12,4},... | collective-permute-start | bytes 1966088 | tf_op jit(solution)/shard_map/ppermute | solution.py:126
  14.5 11.5 %collective-permute-start.7 = (bf16[64,1024]{1,0:T(8,128)(2,1)S(1)}, bf16[64,1024]{1,0:T(8,128)(2,1)S(1)}, u32[]{:S(2)}, u32[]{:S(2)}) collective-permute-start(bf16[64,1024]{1,0:T(8,128)(2,1)S(1)} %bitcast.21), channel_id=1, source_target_pairs={{0,32},{32,0},{1,33},{33,1},{2,34},{34,2},{3,35},{35,3},{4,36},{36... | collective-permute-start | bytes 393224 | tf_op jit(solution)/shard_map/ppermute | solution.py:126
  18.4 10.4 %copy-start = (bf16[8,128,640]{2,1,0:T(8,128)(2,1)}, bf16[8,128,640]{2,1,0:T(8,128)(2,1)S(1)}, u32[]{:S(2)}) copy-start(bf16[8,128,640]{2,1,0:T(8,128)(2,1)S(1)} %pad_maximum_fusion.q_ref) | copy-start | bytes 3932164
  27.4 12.5 %copy-start.10 = (s32[8]{0:T(128)S(1)}, s32[8]{0:T(128)}, u32[]{:S(2)}) copy-start(s32[8]{0:T(128)} %param.9) | copy-start | bytes 100
  28.8 57.8 %all-to-all-start.1 = ((bf16[8,2,64,1024]{3,2,1,0:T(8,128)(2,1)}), bf16[8,2,64,1024]{3,2,1,0:T(8,128)(2,1)S(1)}, u32[]{:S(2)}, u32[]{:S(2)}) async-start(bf16[8,2,64,1024]{3,2,1,0:T(8,128)(2,1)} %shard_map.71), calls=%async_computation.1 | async-start | bytes 4194304 | tf_op jit(solution)/shard_map/all_to_all | solution.py:371
  34.7 5.9 %collective-permute-start.3 = (bf16[512,640]{1,0:T(8,128)(2,1)}, bf16[512,640]{1,0:T(8,128)(2,1)S(1)}, u32[]{:S(2)}, u32[]{:S(2)}) collective-permute-start(bf16[512,640]{1,0:T(8,128)(2,1)} %bitcast.7.key_ref), channel_id=1, source_target_pairs={{0,8},{8,0},{1,9},{9,1},{2,10},{10,2},{3,11},{11,3},{4,12},{12,4},... | collective-permute-start | bytes 1966088 | tf_op jit(solution)/shard_map/ppermute | solution.py:126
  36.6 18.8 %collective-permute-start.1 = (bf16[512,640]{1,0:T(8,128)(2,1)}, bf16[512,640]{1,0:T(8,128)(2,1)S(1)}, u32[]{:S(2)}, u32[]{:S(2)}) collective-permute-start(bf16[512,640]{1,0:T(8,128)(2,1)} %bitcast.7.key_ref), channel_id=1, source_target_pairs={{0,16},{8,60},{16,32},{24,8},{32,48},{40,24},{48,4},{56,40},{4,20}... | collective-permute-start | bytes 1966088 | tf_op jit(solution)/shard_map/ppermute | solution.py:122
  40.7 22.5 %collective-permute-start.4 = (bf16[512,640]{1,0:T(8,128)(2,1)S(1)}, bf16[512,640]{1,0:T(8,128)(2,1)S(1)}, u32[]{:S(2)}, u32[]{:S(2)}) collective-permute-start(bf16[512,640]{1,0:T(8,128)(2,1)S(1)} %collective-permute-done.3), channel_id=1, source_target_pairs={{0,16},{8,60},{16,32},{24,8},{32,48},{40,24},{48,4},{56,40},{4,20}... | collective-permute-start | bytes 1966088 | tf_op jit(solution)/shard_map/ppermute | solution.py:122
  44.9 12.4 %copy-start.1 = (bf16[8,128,640]{2,1,0:T(8,128)(2,1)S(1)}, bf16[8,128,640]{2,1,0:T(8,128)(2,1)}, u32[]{:S(2)}) copy-start(bf16[8,128,640]{2,1,0:T(8,128)(2,1)} %copy-done) | copy-start | bytes 3932164
  44.9 12.4 %copy-start.2 = (bf16[8,512,128]{2,1,0:T(8,128)(2,1)S(1)}, bf16[8,512,128]{2,1,0:T(8,128)(2,1)}, u32[]{:S(2)}) copy-start(bf16[8,512,128]{2,1,0:T(8,128)(2,1)} %up_ref.7) | copy-start | bytes 3145732
  45.0 12.4 %copy-start.5 = (s32[8,1]{0,1:T(1,128)S(1)}, s32[8,1]{0,1:T(1,128)}, u32[]{:S(2)}) copy-start(s32[8,1]{0,1:T(1,128)} %reduce-window.9) | copy-start | bytes 100
  55.4 14.0 %collective-permute-start.2 = (bf16[512,640]{1,0:T(8,128)(2,1)S(1)}, bf16[512,640]{1,0:T(8,128)(2,1)S(1)}, u32[]{:S(2)}, u32[]{:S(2)}) collective-permute-start(bf16[512,640]{1,0:T(8,128)(2,1)S(1)} %collective-permute-done.1.key_ref), channel_id=1, source_target_pairs={{0,16},{8,60},{16,32},{24,8},{32,48},{40,24},{48,4},{56,40},{4,20}... | collective-permute-start | bytes 1966088 | tf_op jit(solution)/shard_map/ppermute | solution.py:122
  57.3 1.0 copy-start.6
  58.4 1.0 copy-start.7
  59.4 1.0 copy-start.8
  72.3 3.5 %collective-permute-start.5 = (bf16[2,64,1152]{2,1,0:T(8,128)(2,1)S(1)}, bf16[2,64,1152]{2,1,0:T(8,128)(2,1)S(1)}, u32[]{:S(2)}, u32[]{:S(2)}) collective-permute-start(bf16[2,64,1152]{2,1,0:T(8,128)(2,1)S(1)} %shard_map.69.own_ref), channel_id=1, source_target_pairs={{0,8},{8,0},{1,9},{9,1},{2,10},{10,2},{3,11},{11,3},{4,12},{12,4},... | collective-permute-start | bytes 884744 | tf_op jit(solution)/shard_map/ppermute | solution.py:126
  76.3 10.2 %collective-permute-start.6 = (bf16[128,1024]{1,0:T(8,128)(2,1)S(1)}, bf16[128,1024]{1,0:T(8,128)(2,1)S(1)}, u32[]{:S(2)}, u32[]{:S(2)}) collective-permute-start(bf16[128,1024]{1,0:T(8,128)(2,1)S(1)} %shard_map.70), channel_id=1, source_target_pairs={{0,16},{16,0},{1,17},{17,1},{2,18},{18,2},{3,19},{19,3},{4,20},{20... | collective-permute-start | bytes 786440 | tf_op jit(solution)/shard_map/ppermute | solution.py:126
  104.2 11.7 %collective-permute-start.8 = (bf16[64,512]{1,0:T(8,128)(2,1)S(1)}, bf16[64,512]{1,0:T(8,128)(2,1)S(1)}, u32[]{:S(2)}, u32[]{:S(2)}) collective-permute-start(bf16[64,512]{1,0:T(8,128)(2,1)S(1)} %get-tuple-element.26), channel_id=1, source_target_pairs={{0,4},{4,0},{1,5},{5,1},{2,6},{6,2},{3,7},{7,3},{8,12},{12,8},{9,1... | collective-permute-start | bytes 196616 | tf_op jit(solution)/shard_map/ppermute | solution.py:126

commit v9 on v8

--- a/solution.py
+++ b/solution.py
@@ -44,23 +44,41 @@
     return high, where - 64.0 * high
 
 
-def key_kernel(where_hbm, latents_hbm, out_hbm, where_ref, latents_ref, rows_ref, in_sems, out_sems):
+def key_kernel(
+    where_hbm, latents_hbm, out_hbm, where_ref, latents_ref, rows_ref, last_ref, in_sems, out_sems
+):
     arrivals = [
         pltpu.make_async_copy(where_hbm, where_ref, in_sems.at[0]),
         pltpu.make_async_copy(latents_hbm, latents_ref, in_sems.at[1]),
     ]
     for arrival in arrivals:
         arrival.start()
-    for arrival in arrivals:
-        arrival.wait()
+    arrivals[0].wait()
     where, cosines, sines = turns(where_ref)
+    arrivals[1].wait()
+    rows_ref[...] = latents_ref[:, :LATENT]
+    copies = range(out_hbm.shape[0])
+    plain = [
+        pltpu.make_async_copy(
+            rows_ref, out_hbm.at[i, :, pl.ds(0, LATENT)], out_sems.at[0, i]
+        )
+        for i in copies
+    ]
+    for copy in plain:
+        copy.start()
     rotary = turned(latents_ref[:, LATENT:].astype(jnp.float32), cosines, sines)
     lane = lax.broadcasted_iota(jnp.int32, rotary.shape, 1)
     high, low = position_parts(where)
     tail = jnp.where(lane == 0, high, jnp.where(lane == 1, low, 0.0))
-    rows_ref[:, :LATENT] = latents_ref[:, :LATENT]
-    rows_ref[:, LATENT:] = jnp.concatenate([rotary, tail], axis=1).astype(jnp.bfloat16)
-    send_copies(rows_ref, out_hbm, out_sems)
+    last_ref[...] = jnp.concatenate([rotary, tail], axis=1).astype(jnp.bfloat16)
+    rest = [
+        pltpu.make_async_copy(last_ref, out_hbm.at[i, :, pl.ds(LATENT, 128)], out_sems.at[1, i])
+        for i in copies
+    ]
+    for copy in rest:
+        copy.start()
+    for copy in plain + rest:
+        copy.wait()
 
 
 def send_copies(ref, out_hbm, sems):
@@ -81,9 +99,10 @@
         scratch_shapes=[
             pltpu.VMEM((1, toks), jnp.int32),
             pltpu.VMEM((toks, width), latents.dtype),
-            pltpu.VMEM((toks, WIDTH), latents.dtype),
+            pltpu.VMEM((toks, LATENT), latents.dtype),
+            pltpu.VMEM((toks, WIDTH - LATENT), latents.dtype),
             pltpu.SemaphoreType.DMA((2,)),
-            pltpu.SemaphoreType.DMA((copies,)),
+            pltpu.SemaphoreType.DMA((2, copies)),
         ],
         compiler_params=pltpu.CompilerParams(vmem_limit_bytes=60 * 1024 * 1024),
     )(positions.reshape(1, -1), latents)

time: 117 us -> 117 us (level)
  no operation moved by 1% of the time
where the time goes in v9:
time: 117 us; the launch traced here: 116 us
  starting transfers between devices  46.1 us (39%)
  waiting for transfers between devices  29.4 us (25%)
  Pallas kernels  20.7 us (18%)
  blocking collectives  15.1 us (13%)
  local copies, waits for them, and re-layouts  3.23 us (3%)
  other arithmetic  1.56 us (1%)
    ppermute x6, starting transfers between devices, swap(): return lax.ppermute(x, axis, [(0, 1), (1, 0)])  20.6 us
    ppermute x6, waiting for transfers between devices, swap(): return lax.ppermute(x, axis, [(0, 1), (1, 0)])  19.8 us
    all_to_all x1, blocking collectives, on_device(): lax.all_to_all(partial.reshape((16,) + partial.shape[3:]), ('x', 'zl_lat'...  15.1 us
    pallas_call x4, Pallas kernels, attend(): pl.pallas_call(functools.partial(attend_kernel, group, first, last), in_s...  14 us
    all_to_all x1, starting transfers between devices, on_device(): along_y = lax.all_to_all(key_rows, 'y', 0, 0).reshape(8 * toks, WIDTH)  10 us
    ppermute x3, starting transfers between devices, shift_z(): return lax.ppermute(x, ('zh_lat', 'zl_lat', 'core', 'z_hi'), perm)  9.5 us
    ppermute x3, waiting for transfers between devices, shift_z(): return lax.ppermute(x, ('zh_lat', 'zl_lat', 'core', 'z_hi'), perm)  8.21 us
    all_to_all x1, starting transfers between devices, on_device(): w = lax.all_to_all(w, 'y', 0, 0)  5.93 us
  transfers between devices with their start and end apart: 11, of which 7 were waited for; matrix products, arithmetic and copies ran while one was open for 1% of the time, Pallas kernels for 14%

profile of v9, /device:TPU:8, one launch (start us, length us, event | category | flops | bytes accessed | tf_op | source)
XLA Modules:
  0.0 116.4 jit_solution(1343434707552019557)
XLA Ops:
  0.0 2.0 %shard_map.65 = bf16[8,64,640]{2,1,0:T(8,128)(2,1)} custom-call(s32[1,64]{1,0:T(1,128)} %bitcast.23, bf16[64,576]{1,0:T(8,128)(2,1)} %latents_hbm.1), custom_call_target="tpu_custom_call" | custom-call | tf_op jit(solution)/shard_map/pallas_call | solution.py:94
  2.0 10.0 %all-to-all-start = ((bf16[8,64,640]{2,1,0:T(8,128)(2,1)}), bf16[8,64,640]{2,1,0:T(8,128)(2,1)}, u32[]{:S(2)}, u32[]{:S(2)}) async-start(bf16[8,64,640]{2,1,0:T(8,128)(2,1)} %shard_map.65), calls=%async_computation | async-start | bytes 1310720 | tf_op jit(solution)/shard_map/all_to_all | solution.py:383
  12.5 1.9 %collective-permute-start = (bf16[8,64,640]{2,1,0:T(8,128)(2,1)S(1)}, bf16[8,64,640]{2,1,0:T(8,128)(2,1)S(1)}, u32[]{:S(2)}, u32[]{:S(2)}) collective-permute-start(bf16[8,64,640]{2,1,0:T(8,128)(2,1)S(1)} %shard_map.64), channel_id=1, source_target_pairs={{0,8},{8,0},{1,9},{9,1},{2,10},{10,2},{3,11},{11,3},{4,12},{12,4},... | collective-permute-start | bytes 1966088 | tf_op jit(solution)/shard_map/ppermute | solution.py:145
  14.4 3.7 %collective-permute-start.7 = (bf16[64,1024]{1,0:T(8,128)(2,1)S(1)}, bf16[64,1024]{1,0:T(8,128)(2,1)S(1)}, u32[]{:S(2)}, u32[]{:S(2)}) collective-permute-start(bf16[64,1024]{1,0:T(8,128)(2,1)S(1)} %bitcast.21), channel_id=1, source_target_pairs={{0,32},{32,0},{1,33},{33,1},{2,34},{34,2},{3,35},{35,3},{4,36},{36... | collective-permute-start | bytes 393224 | tf_op jit(solution)/shard_map/ppermute | solution.py:145
  18.3 7.6 %collective-permute-done.7.other_ref = bf16[64,1024]{1,0:T(8,128)(2,1)S(1)} collective-permute-done((bf16[64,1024]{1,0:T(8,128)(2,1)S(1)}, bf16[64,1024]{1,0:T(8,128)(2,1)S(1)}, u32[]{:S(2)}, u32[]{:S(2)}) %collective-permute-start.7) | collective-permute-done | bytes 131104 | tf_op jit(solution)/shard_map/ppermute | solution.py:145
  28.7 5.9 %all-to-all-start.1 = ((bf16[8,2,64,1024]{3,2,1,0:T(8,128)(2,1)}), bf16[8,2,64,1024]{3,2,1,0:T(8,128)(2,1)S(1)}, u32[]{:S(2)}, u32[]{:S(2)}) async-start(bf16[8,2,64,1024]{3,2,1,0:T(8,128)(2,1)} %shard_map.71), calls=%async_computation.1 | async-start | bytes 4194304 | tf_op jit(solution)/shard_map/all_to_all | solution.py:390
  34.6 1.9 %collective-permute-start.3 = (bf16[512,640]{1,0:T(8,128)(2,1)}, bf16[512,640]{1,0:T(8,128)(2,1)S(1)}, u32[]{:S(2)}, u32[]{:S(2)}) collective-permute-start(bf16[512,640]{1,0:T(8,128)(2,1)} %bitcast.7.key_ref), channel_id=1, source_target_pairs={{0,8},{8,0},{1,9},{9,1},{2,10},{10,2},{3,11},{11,3},{4,12},{12,4},... | collective-permute-start | bytes 1966088 | tf_op jit(solution)/shard_map/ppermute | solution.py:145
  36.5 3.3 %collective-permute-start.1 = (bf16[512,640]{1,0:T(8,128)(2,1)}, bf16[512,640]{1,0:T(8,128)(2,1)S(1)}, u32[]{:S(2)}, u32[]{:S(2)}) collective-permute-start(bf16[512,640]{1,0:T(8,128)(2,1)} %bitcast.7.key_ref), channel_id=1, source_target_pairs={{0,16},{8,60},{16,32},{24,8},{32,48},{40,24},{48,4},{56,40},{4,20}... | collective-permute-start | bytes 1966088 | tf_op jit(solution)/shard_map/ppermute | solution.py:141
  40.5 4.3 %collective-permute-start.4 = (bf16[512,640]{1,0:T(8,128)(2,1)S(1)}, bf16[512,640]{1,0:T(8,128)(2,1)S(1)}, u32[]{:S(2)}, u32[]{:S(2)}) collective-permute-start(bf16[512,640]{1,0:T(8,128)(2,1)S(1)} %collective-permute-done.3), channel_id=1, source_target_pairs={{0,16},{8,60},{16,32},{24,8},{32,48},{40,24},{48,4},{56,40},{4,20}... | collective-permute-start | bytes 1966088 | tf_op jit(solution)/shard_map/ppermute | solution.py:141
  44.8 5.8 %shard_map.66 = (f32[8,128,128]{2,1,0:T(8,128)}, f32[8,128,128]{2,1,0:T(8,128)}, f32[8,128,128]{2,1,0:T(8,128)}) custom-call(s32[8]{0:T(128)} %bitcast.25, bf16[8,128,640]{2,1,0:T(8,128)(2,1)} %copy-done, bf16[512,640]{1,0:T(8,128)(2,1)} %bitcast.7.key_ref, bf16[8,512,128]{2,1,0:T(8,128)(2,1)} %up_ref.7), custom_call_target="tpu_custom_call" | custom-call | flops 3623878656 | bytes 14548992 | tf_op jit(solution)/shard_map/pallas_call | solution.py:238
  50.6 4.6 %collective-permute-done.1.key_ref = bf16[512,640]{1,0:T(8,128)(2,1)S(1)} collective-permute-done((bf16[512,640]{1,0:T(8,128)(2,1)}, bf16[512,640]{1,0:T(8,128)(2,1)S(1)}, u32[]{:S(2)}, u32[]{:S(2)}) %collective-permute-start.1) | collective-permute-done | bytes 655392 | tf_op jit(solution)/shard_map/ppermute | solution.py:141
  55.3 1.9 %collective-permute-start.2 = (bf16[512,640]{1,0:T(8,128)(2,1)S(1)}, bf16[512,640]{1,0:T(8,128)(2,1)S(1)}, u32[]{:S(2)}, u32[]{:S(2)}) collective-permute-start(bf16[512,640]{1,0:T(8,128)(2,1)S(1)} %collective-permute-done.1.key_ref), channel_id=1, source_target_pairs={{0,16},{8,60},{16,32},{24,8},{32,48},{40,24},{48,4},{56,40},{4,20}... | collective-permute-start | bytes 1966088 | tf_op jit(solution)/shard_map/ppermute | solution.py:141
  60.3 2.7 %shard_map.67 = (f32[8,128,128]{2,1,0:T(8,128)S(1)}, f32[8,128,128]{2,1,0:T(8,128)S(1)}, f32[8,128,128]{2,1,0:T(8,128)S(1)}) custom-call(s32[8]{0:T(128)S(1)} %bitcast.26, bf16[8,128,640]{2,1,0:T(8,128)(2,1)S(1)} %copy-done.1, bf16[512,640]{1,0:T(8,128)(2,1)S(1)} %collective-permute-done.1.key_ref, bf16[8,512,128]{2,1,0:T(8,128)(2,1)S(1)} %copy-done.2, ...), custom_call_target="tpu_custom_call" | custom-call | flops 3623878656 | bytes 14548992 | tf_op jit(solution)/shard_map/pallas_call | solution.py:238
  63.0 2.7 %shard_map.68 = (f32[8,128,128]{2,1,0:T(8,128)S(1)}, f32[8,128,128]{2,1,0:T(8,128)S(1)}, f32[8,128,128]{2,1,0:T(8,128)S(1)}) custom-call(s32[8]{0:T(128)S(1)} %bitcast.27, bf16[8,128,640]{2,1,0:T(8,128)(2,1)S(1)} %copy-done.1, bf16[512,640]{1,0:T(8,128)(2,1)S(1)} %collective-permute-done.4.key_ref, bf16[8,512,128]{2,1,0:T(8,128)(2,1)S(1)} %copy-done.2, ...), custom_call_target="tpu_custom_call" | custom-call | flops 3623878656 | bytes 14548992 | tf_op jit(solution)/shard_map/pallas_call | solution.py:238
  65.7 3.6 %collective-permute-done.2.key_ref = bf16[512,640]{1,0:T(8,128)(2,1)S(1)} collective-permute-done((bf16[512,640]{1,0:T(8,128)(2,1)S(1)}, bf16[512,640]{1,0:T(8,128)(2,1)S(1)}, u32[]{:S(2)}, u32[]{:S(2)}) %collective-permute-start.2) | collective-permute-done | bytes 655392 | tf_op jit(solution)/shard_map/ppermute | solution.py:141
  69.3 2.8 %shard_map.69.own_ref = bf16[2,64,1152]{2,1,0:T(8,128)(2,1)S(1)} custom-call(s32[8]{0:T(128)S(1)} %bitcast.28, bf16[8,128,640]{2,1,0:T(8,128)(2,1)S(1)} %copy-done.1, bf16[512,640]{1,0:T(8,128)(2,1)S(1)} %collective-permute-done.2.key_ref, bf16[8,512,128]{2,1,0:T(8,128)(2,1)S(1)} %copy-done.2, f32[8,128,128]{2,1,0:T(8,128)S(1)} %get-tuple-element.22.refs_0_, ...), custom_call_target="tpu_custom_call" | custom-call | flops 1207959552 | bytes 4849664 | tf_op jit(solution)/shard_map/pallas_call | solution.py:238
  72.2 1.9 %collective-permute-start.5 = (bf16[2,64,1152]{2,1,0:T(8,128)(2,1)S(1)}, bf16[2,64,1152]{2,1,0:T(8,128)(2,1)S(1)}, u32[]{:S(2)}, u32[]{:S(2)}) collective-permute-start(bf16[2,64,1152]{2,1,0:T(8,128)(2,1)S(1)} %shard_map.69.own_ref), channel_id=1, source_target_pairs={{0,8},{8,0},{1,9},{9,1},{2,10},{10,2},{3,11},{11,3},{4,12},{12,4},... | collective-permute-start | bytes 884744 | tf_op jit(solution)/shard_map/ppermute | solution.py:145
  74.1 1.5 %collective-permute-done.5.other_ref = bf16[2,64,1152]{2,1,0:T(8,128)(2,1)S(1)} collective-permute-done((bf16[2,64,1152]{2,1,0:T(8,128)(2,1)S(1)}, bf16[2,64,1152]{2,1,0:T(8,128)(2,1)S(1)}, u32[]{:S(2)}, u32[]{:S(2)}) %collective-permute-start.5) | collective-permute-done | bytes 294944 | tf_op jit(solution)/shard_map/ppermute | solution.py:145
  76.2 1.9 %collective-permute-start.6 = (bf16[128,1024]{1,0:T(8,128)(2,1)S(1)}, bf16[128,1024]{1,0:T(8,128)(2,1)S(1)}, u32[]{:S(2)}, u32[]{:S(2)}) collective-permute-start(bf16[128,1024]{1,0:T(8,128)(2,1)S(1)} %shard_map.70), channel_id=1, source_target_pairs={{0,16},{16,0},{1,17},{17,1},{2,18},{18,2},{3,19},{19,3},{4,20},{20... | collective-permute-start | bytes 786440 | tf_op jit(solution)/shard_map/ppermute | solution.py:145
  78.2 8.2 %collective-permute-done.6 = bf16[128,1024]{1,0:T(8,128)(2,1)S(1)} collective-permute-done((bf16[128,1024]{1,0:T(8,128)(2,1)S(1)}, bf16[128,1024]{1,0:T(8,128)(2,1)S(1)}, u32[]{:S(2)}, u32[]{:S(2)}) %collective-permute-start.6) | collective-permute-done | bytes 262176 | tf_op jit(solution)/shard_map/ppermute | solution.py:145
  86.5 1.8 %shard_map.72 = bf16[4,2,2,2,64,128]{5,4,3,2,1,0:T(8,128)(2,1)S(1)} custom-call(s32[3]{0:T(128)S(1)} %pad_add_fusion.slots_ref, bf16[256,1024]{1,0:T(8,128)(2,1)S(1)} %pad_maximum_fusion.1.v_ref, bf16[8,128,1024]{2,1,0:T(8,128)(2,1)S(1)} %bitcast.16), custom_call_target="tpu_custom_call" | custom-call | flops 536870912 | bytes 2097152 | tf_op jit(solution)/shard_map/pallas_call | solution.py:307
  88.3 15.1 %all_to_all.15 = bf16[16,2,64,128]{3,2,1,0:T(8,128)(2,1)S(1)} all-to-all(bf16[16,2,64,128]{3,2,1,0:T(8,128)(2,1)S(1)} %bitcast.20), channel_id=1, replica_groups=mesh['y'=8,'zh_lat'=2,'zl_lat'=2,'core'=2,'z_hi'=2,'x'=4] {'x','zl_lat',..., dimensions={0} | all-to-all | bytes 1048576 | tf_op jit(solution)/shard_map/all_to_all | solution.py:408
  104.0 9.2 %collective-permute-start.8 = (bf16[64,512]{1,0:T(8,128)(2,1)S(1)}, bf16[64,512]{1,0:T(8,128)(2,1)S(1)}, u32[]{:S(2)}, u32[]{:S(2)}) collective-permute-start(bf16[64,512]{1,0:T(8,128)(2,1)S(1)} %get-tuple-element.26), channel_id=1, source_target_pairs={{0,4},{4,0},{1,5},{5,1},{2,6},{6,2},{3,7},{7,3},{8,12},{12,8},{9,1... | collective-permute-start | bytes 196616 | tf_op jit(solution)/shard_map/ppermute | solution.py:145
  113.3 2.5 %collective-permute-done.8 = bf16[64,512]{1,0:T(8,128)(2,1)S(1)} collective-permute-done((bf16[64,512]{1,0:T(8,128)(2,1)S(1)}, bf16[64,512]{1,0:T(8,128)(2,1)S(1)}, u32[]{:S(2)}, u32[]{:S(2)}) %collective-permute-start.8) | collective-permute-done | bytes 65568 | tf_op jit(solution)/shard_map/ppermute | solution.py:145
  (38 shorter events, 9.1 us)
Async XLA Ops:
  0.0 12.1 %copy-start.4 = (s32[64]{0:T(128)S(1)}, s32[64]{0:T(128)}, u32[]{:S(2)}) copy-start(s32[64]{0:T(128)} %param.8) | copy-start | bytes 772
  0.0 12.1 %copy-start.9 = (bf16[64,8,576]{2,1,0:T(8,128)(2,1)S(1)}, bf16[64,8,576]{2,1,0:T(8,128)(2,1)}, u32[]{:S(2)}) copy-start(bf16[64,8,576]{2,1,0:T(8,128)(2,1)} %param.6) | copy-start | bytes 1769476
  2.0 12.4 %copy-start.3 = (bf16[1024,64]{0,1:T(8,128)(2,1)S(1)}, bf16[1024,64]{0,1:T(8,128)(2,1)}, u32[]{:S(2)}) copy-start(bf16[1024,64]{0,1:T(8,128)(2,1)} %param.11) | copy-start | bytes 393220
  2.0 26.6 %all-to-all-start = ((bf16[8,64,640]{2,1,0:T(8,128)(2,1)}), bf16[8,64,640]{2,1,0:T(8,128)(2,1)}, u32[]{:S(2)}, u32[]{:S(2)}) async-start(bf16[8,64,640]{2,1,0:T(8,128)(2,1)} %shard_map.65), calls=%async_computation | async-start | bytes 1310720 | tf_op jit(solution)/shard_map/all_to_all | solution.py:383
  12.5 5.7 %collective-permute-start = (bf16[8,64,640]{2,1,0:T(8,128)(2,1)S(1)}, bf16[8,64,640]{2,1,0:T(8,128)(2,1)S(1)}, u32[]{:S(2)}, u32[]{:S(2)}) collective-permute-start(bf16[8,64,640]{2,1,0:T(8,128)(2,1)S(1)} %shard_map.64), channel_id=1, source_target_pairs={{0,8},{8,0},{1,9},{9,1},{2,10},{10,2},{3,11},{11,3},{4,12},{12,4},... | collective-permute-start | bytes 1966088 | tf_op jit(solution)/shard_map/ppermute | solution.py:145
  14.4 11.5 %collective-permute-start.7 = (bf16[64,1024]{1,0:T(8,128)(2,1)S(1)}, bf16[64,1024]{1,0:T(8,128)(2,1)S(1)}, u32[]{:S(2)}, u32[]{:S(2)}) collective-permute-start(bf16[64,1024]{1,0:T(8,128)(2,1)S(1)} %bitcast.21), channel_id=1, source_target_pairs={{0,32},{32,0},{1,33},{33,1},{2,34},{34,2},{3,35},{35,3},{4,36},{36... | collective-permute-start | bytes 393224 | tf_op jit(solution)/shard_map/ppermute | solution.py:145
  18.3 10.4 %copy-start = (bf16[8,128,640]{2,1,0:T(8,128)(2,1)}, bf16[8,128,640]{2,1,0:T(8,128)(2,1)S(1)}, u32[]{:S(2)}) copy-start(bf16[8,128,640]{2,1,0:T(8,128)(2,1)S(1)} %pad_maximum_fusion.q_ref) | copy-start | bytes 3932164
  27.3 12.5 %copy-start.10 = (s32[8]{0:T(128)S(1)}, s32[8]{0:T(128)}, u32[]{:S(2)}) copy-start(s32[8]{0:T(128)} %param.9) | copy-start | bytes 100
  28.7 57.8 %all-to-all-start.1 = ((bf16[8,2,64,1024]{3,2,1,0:T(8,128)(2,1)}), bf16[8,2,64,1024]{3,2,1,0:T(8,128)(2,1)S(1)}, u32[]{:S(2)}, u32[]{:S(2)}) async-start(bf16[8,2,64,1024]{3,2,1,0:T(8,128)(2,1)} %shard_map.71), calls=%async_computation.1 | async-start | bytes 4194304 | tf_op jit(solution)/shard_map/all_to_all | solution.py:390
  34.6 5.9 %collective-permute-start.3 = (bf16[512,640]{1,0:T(8,128)(2,1)}, bf16[512,640]{1,0:T(8,128)(2,1)S(1)}, u32[]{:S(2)}, u32[]{:S(2)}) collective-permute-start(bf16[512,640]{1,0:T(8,128)(2,1)} %bitcast.7.key_ref), channel_id=1, source_target_pairs={{0,8},{8,0},{1,9},{9,1},{2,10},{10,2},{3,11},{11,3},{4,12},{12,4},... | collective-permute-start | bytes 1966088 | tf_op jit(solution)/shard_map/ppermute | solution.py:145
  36.5 18.8 %collective-permute-start.1 = (bf16[512,640]{1,0:T(8,128)(2,1)}, bf16[512,640]{1,0:T(8,128)(2,1)S(1)}, u32[]{:S(2)}, u32[]{:S(2)}) collective-permute-start(bf16[512,640]{1,0:T(8,128)(2,1)} %bitcast.7.key_ref), channel_id=1, source_target_pairs={{0,16},{8,60},{16,32},{24,8},{32,48},{40,24},{48,4},{56,40},{4,20}... | collective-permute-start | bytes 1966088 | tf_op jit(solution)/shard_map/ppermute | solution.py:141
  40.5 22.5 %collective-permute-start.4 = (bf16[512,640]{1,0:T(8,128)(2,1)S(1)}, bf16[512,640]{1,0:T(8,128)(2,1)S(1)}, u32[]{:S(2)}, u32[]{:S(2)}) collective-permute-start(bf16[512,640]{1,0:T(8,128)(2,1)S(1)} %collective-permute-done.3), channel_id=1, source_target_pairs={{0,16},{8,60},{16,32},{24,8},{32,48},{40,24},{48,4},{56,40},{4,20}... | collective-permute-start | bytes 1966088 | tf_op jit(solution)/shard_map/ppermute | solution.py:141
  44.8 12.4 %copy-start.1 = (bf16[8,128,640]{2,1,0:T(8,128)(2,1)S(1)}, bf16[8,128,640]{2,1,0:T(8,128)(2,1)}, u32[]{:S(2)}) copy-start(bf16[8,128,640]{2,1,0:T(8,128)(2,1)} %copy-done) | copy-start | bytes 3932164
  44.8 12.4 %copy-start.2 = (bf16[8,512,128]{2,1,0:T(8,128)(2,1)S(1)}, bf16[8,512,128]{2,1,0:T(8,128)(2,1)}, u32[]{:S(2)}) copy-start(bf16[8,512,128]{2,1,0:T(8,128)(2,1)} %up_ref.7) | copy-start | bytes 3145732
  44.8 12.4 %copy-start.5 = (s32[8,1]{0,1:T(1,128)S(1)}, s32[8,1]{0,1:T(1,128)}, u32[]{:S(2)}) copy-start(s32[8,1]{0,1:T(1,128)} %reduce-window.9) | copy-start | bytes 100
  55.3 14.0 %collective-permute-start.2 = (bf16[512,640]{1,0:T(8,128)(2,1)S(1)}, bf16[512,640]{1,0:T(8,128)(2,1)S(1)}, u32[]{:S(2)}, u32[]{:S(2)}) collective-permute-start(bf16[512,640]{1,0:T(8,128)(2,1)S(1)} %collective-permute-done.1.key_ref), channel_id=1, source_target_pairs={{0,16},{8,60},{16,32},{24,8},{32,48},{40,24},{48,4},{56,40},{4,20}... | collective-permute-start | bytes 1966088 | tf_op jit(solution)/shard_map/ppermute | solution.py:141
  57.2 1.0 copy-start.6
  58.3 1.0 copy-start.7
  59.3 1.0 copy-start.8
  72.2 3.5 %collective-permute-start.5 = (bf16[2,64,1152]{2,1,0:T(8,128)(2,1)S(1)}, bf16[2,64,1152]{2,1,0:T(8,128)(2,1)S(1)}, u32[]{:S(2)}, u32[]{:S(2)}) collective-permute-start(bf16[2,64,1152]{2,1,0:T(8,128)(2,1)S(1)} %shard_map.69.own_ref), channel_id=1, source_target_pairs={{0,8},{8,0},{1,9},{9,1},{2,10},{10,2},{3,11},{11,3},{4,12},{12,4},... | collective-permute-start | bytes 884744 | tf_op jit(solution)/shard_map/ppermute | solution.py:145
  76.2 10.2 %collective-permute-start.6 = (bf16[128,1024]{1,0:T(8,128)(2,1)S(1)}, bf16[128,1024]{1,0:T(8,128)(2,1)S(1)}, u32[]{:S(2)}, u32[]{:S(2)}) collective-permute-start(bf16[128,1024]{1,0:T(8,128)(2,1)S(1)} %shard_map.70), channel_id=1, source_target_pairs={{0,16},{16,0},{1,17},{17,1},{2,18},{18,2},{3,19},{19,3},{4,20},{20... | collective-permute-start | bytes 786440 | tf_op jit(solution)/shard_map/ppermute | solution.py:145
  104.0 11.7 %collective-permute-start.8 = (bf16[64,512]{1,0:T(8,128)(2,1)S(1)}, bf16[64,512]{1,0:T(8,128)(2,1)S(1)}, u32[]{:S(2)}, u32[]{:S(2)}) collective-permute-start(bf16[64,512]{1,0:T(8,128)(2,1)S(1)} %get-tuple-element.26), channel_id=1, source_target_pairs={{0,4},{4,0},{1,5},{5,1},{2,6},{6,2},{3,7},{7,3},{8,12},{12,8},{9,1... | collective-permute-start | bytes 196616 | tf_op jit(solution)/shard_map/ppermute | solution.py:145

commit v10 on v9

--- a/solution.py
+++ b/solution.py
@@ -350,6 +350,21 @@
     )(slots, parts)
 
 
+def add_z_kernel(keep_ref, arrived_ref, out_ref):
+    total = keep_ref[...] + arrived_ref[...].astype(jnp.float32)
+    out_ref[...] = total.astype(out_ref.dtype)
+
+
+def add_z(keep, arrived):
+    return pl.pallas_call(
+        add_z_kernel,
+        in_specs=[WHOLE] * 2,
+        out_specs=WHOLE,
+        out_shape=jax.ShapeDtypeStruct(arrived.shape, arrived.dtype),
+        compiler_params=pltpu.CompilerParams(vmem_limit_bytes=VMEM),
+    )(keep, arrived)
+
+
 def pair_kernel(far_ref, own_ref, other_ref, _, out_hbm, both_ref, sems):
     far = far_ref[0]
     both_ref[far] = own_ref[...]
@@ -409,7 +424,7 @@
         partial.reshape((16,) + partial.shape[3:]), ("x", "zl_lat", "core"), 0, 0
     )
     keep, give = add_x(slots, parts.reshape(partial.shape))
-    return (keep + swap(give, "z_hi").astype(jnp.float32)).astype(jnp.bfloat16)
+    return add_z(keep, swap(give, "z_hi"))
 
 
 def solution(mesh):

time: 117 us -> 117 us (level)
  no operation moved by 1% of the time
where the time goes in v10:
time: 117 us; the launch traced here: 116 us
  starting transfers between devices  46.1 us (39%)
  waiting for transfers between devices  29.4 us (25%)
  Pallas kernels  21.4 us (18%)
  blocking collectives  15.1 us (13%)
  local copies, waits for them, and re-layouts  3.23 us (3%)
    ppermute x6, starting transfers between devices, swap(): return lax.ppermute(x, axis, [(0, 1), (1, 0)])  20.6 us
    ppermute x6, waiting for transfers between devices, swap(): return lax.ppermute(x, axis, [(0, 1), (1, 0)])  19.8 us
    all_to_all x1, blocking collectives, on_device(): lax.all_to_all(partial.reshape((16,) + partial.shape[3:]), ('x', 'zl_lat'...  15.1 us
    pallas_call x4, Pallas kernels, attend(): pl.pallas_call(functools.partial(attend_kernel, group, first, last), in_s...  14 us
    all_to_all x1, starting transfers between devices, on_device(): along_y = lax.all_to_all(key_rows, 'y', 0, 0).reshape(8 * toks, WIDTH)  10 us
    ppermute x3, starting transfers between devices, shift_z(): return lax.ppermute(x, ('zh_lat', 'zl_lat', 'core', 'z_hi'), perm)  9.5 us
    ppermute x3, waiting for transfers between devices, shift_z(): return lax.ppermute(x, ('zh_lat', 'zl_lat', 'core', 'z_hi'), perm)  8.21 us
    all_to_all x1, starting transfers between devices, on_device(): w = lax.all_to_all(w, 'y', 0, 0)  5.93 us
  transfers between devices with their start and end apart: 11, of which 7 were waited for; matrix products, arithmetic and copies ran while one was open for 1% of the time, Pallas kernels for 14%

profile of v10, /device:TPU:8, one launch (start us, length us, event | category | flops | bytes accessed | tf_op | source)
XLA Modules:
  0.0 116.4 jit_solution(11443338975914058296)
XLA Ops:
  0.0 2.0 %shard_map.65 = bf16[8,64,640]{2,1,0:T(8,128)(2,1)} custom-call(s32[1,64]{1,0:T(1,128)} %bitcast.23, bf16[64,576]{1,0:T(8,128)(2,1)} %latents_hbm.1), custom_call_target="tpu_custom_call" | custom-call | tf_op jit(solution)/shard_map/pallas_call | solution.py:94
  2.0 10.0 %all-to-all-start = ((bf16[8,64,640]{2,1,0:T(8,128)(2,1)}), bf16[8,64,640]{2,1,0:T(8,128)(2,1)}, u32[]{:S(2)}, u32[]{:S(2)}) async-start(bf16[8,64,640]{2,1,0:T(8,128)(2,1)} %shard_map.65), calls=%async_computation | async-start | bytes 1310720 | tf_op jit(solution)/shard_map/all_to_all | solution.py:398
  12.5 1.9 %collective-permute-start = (bf16[8,64,640]{2,1,0:T(8,128)(2,1)S(1)}, bf16[8,64,640]{2,1,0:T(8,128)(2,1)S(1)}, u32[]{:S(2)}, u32[]{:S(2)}) collective-permute-start(bf16[8,64,640]{2,1,0:T(8,128)(2,1)S(1)} %shard_map.64), channel_id=1, source_target_pairs={{0,8},{8,0},{1,9},{9,1},{2,10},{10,2},{3,11},{11,3},{4,12},{12,4},... | collective-permute-start | bytes 1966088 | tf_op jit(solution)/shard_map/ppermute | solution.py:145
  14.4 3.7 %collective-permute-start.7 = (bf16[64,1024]{1,0:T(8,128)(2,1)S(1)}, bf16[64,1024]{1,0:T(8,128)(2,1)S(1)}, u32[]{:S(2)}, u32[]{:S(2)}) collective-permute-start(bf16[64,1024]{1,0:T(8,128)(2,1)S(1)} %bitcast.21), channel_id=1, source_target_pairs={{0,32},{32,0},{1,33},{33,1},{2,34},{34,2},{3,35},{35,3},{4,36},{36... | collective-permute-start | bytes 393224 | tf_op jit(solution)/shard_map/ppermute | solution.py:145
  18.3 7.6 %collective-permute-done.7.other_ref = bf16[64,1024]{1,0:T(8,128)(2,1)S(1)} collective-permute-done((bf16[64,1024]{1,0:T(8,128)(2,1)S(1)}, bf16[64,1024]{1,0:T(8,128)(2,1)S(1)}, u32[]{:S(2)}, u32[]{:S(2)}) %collective-permute-start.7) | collective-permute-done | bytes 131104 | tf_op jit(solution)/shard_map/ppermute | solution.py:145
  28.7 5.9 %all-to-all-start.1 = ((bf16[8,2,64,1024]{3,2,1,0:T(8,128)(2,1)}), bf16[8,2,64,1024]{3,2,1,0:T(8,128)(2,1)S(1)}, u32[]{:S(2)}, u32[]{:S(2)}) async-start(bf16[8,2,64,1024]{3,2,1,0:T(8,128)(2,1)} %shard_map.71), calls=%async_computation.1 | async-start | bytes 4194304 | tf_op jit(solution)/shard_map/all_to_all | solution.py:405
  34.6 1.9 %collective-permute-start.3 = (bf16[512,640]{1,0:T(8,128)(2,1)}, bf16[512,640]{1,0:T(8,128)(2,1)S(1)}, u32[]{:S(2)}, u32[]{:S(2)}) collective-permute-start(bf16[512,640]{1,0:T(8,128)(2,1)} %bitcast.7.key_ref), channel_id=1, source_target_pairs={{0,8},{8,0},{1,9},{9,1},{2,10},{10,2},{3,11},{11,3},{4,12},{12,4},... | collective-permute-start | bytes 1966088 | tf_op jit(solution)/shard_map/ppermute | solution.py:145
  36.5 3.3 %collective-permute-start.1 = (bf16[512,640]{1,0:T(8,128)(2,1)}, bf16[512,640]{1,0:T(8,128)(2,1)S(1)}, u32[]{:S(2)}, u32[]{:S(2)}) collective-permute-start(bf16[512,640]{1,0:T(8,128)(2,1)} %bitcast.7.key_ref), channel_id=1, source_target_pairs={{0,16},{8,60},{16,32},{24,8},{32,48},{40,24},{48,4},{56,40},{4,20}... | collective-permute-start | bytes 1966088 | tf_op jit(solution)/shard_map/ppermute | solution.py:141
  40.5 4.3 %collective-permute-start.4 = (bf16[512,640]{1,0:T(8,128)(2,1)S(1)}, bf16[512,640]{1,0:T(8,128)(2,1)S(1)}, u32[]{:S(2)}, u32[]{:S(2)}) collective-permute-start(bf16[512,640]{1,0:T(8,128)(2,1)S(1)} %collective-permute-done.3), channel_id=1, source_target_pairs={{0,16},{8,60},{16,32},{24,8},{32,48},{40,24},{48,4},{56,40},{4,20}... | collective-permute-start | bytes 1966088 | tf_op jit(solution)/shard_map/ppermute | solution.py:141
  44.8 5.8 %shard_map.66 = (f32[8,128,128]{2,1,0:T(8,128)}, f32[8,128,128]{2,1,0:T(8,128)}, f32[8,128,128]{2,1,0:T(8,128)}) custom-call(s32[8]{0:T(128)} %bitcast.25, bf16[8,128,640]{2,1,0:T(8,128)(2,1)} %copy-done, bf16[512,640]{1,0:T(8,128)(2,1)} %bitcast.7.key_ref, bf16[8,512,128]{2,1,0:T(8,128)(2,1)} %up_ref.7), custom_call_target="tpu_custom_call" | custom-call | flops 3623878656 | bytes 14548992 | tf_op jit(solution)/shard_map/pallas_call | solution.py:238
  50.6 4.6 %collective-permute-done.1.key_ref = bf16[512,640]{1,0:T(8,128)(2,1)S(1)} collective-permute-done((bf16[512,640]{1,0:T(8,128)(2,1)}, bf16[512,640]{1,0:T(8,128)(2,1)S(1)}, u32[]{:S(2)}, u32[]{:S(2)}) %collective-permute-start.1) | collective-permute-done | bytes 655392 | tf_op jit(solution)/shard_map/ppermute | solution.py:141
  55.3 1.9 %collective-permute-start.2 = (bf16[512,640]{1,0:T(8,128)(2,1)S(1)}, bf16[512,640]{1,0:T(8,128)(2,1)S(1)}, u32[]{:S(2)}, u32[]{:S(2)}) collective-permute-start(bf16[512,640]{1,0:T(8,128)(2,1)S(1)} %collective-permute-done.1.key_ref), channel_id=1, source_target_pairs={{0,16},{8,60},{16,32},{24,8},{32,48},{40,24},{48,4},{56,40},{4,20}... | collective-permute-start | bytes 1966088 | tf_op jit(solution)/shard_map/ppermute | solution.py:141
  60.3 2.7 %shard_map.67 = (f32[8,128,128]{2,1,0:T(8,128)S(1)}, f32[8,128,128]{2,1,0:T(8,128)S(1)}, f32[8,128,128]{2,1,0:T(8,128)S(1)}) custom-call(s32[8]{0:T(128)S(1)} %bitcast.26, bf16[8,128,640]{2,1,0:T(8,128)(2,1)S(1)} %copy-done.1, bf16[512,640]{1,0:T(8,128)(2,1)S(1)} %collective-permute-done.1.key_ref, bf16[8,512,128]{2,1,0:T(8,128)(2,1)S(1)} %copy-done.2, ...), custom_call_target="tpu_custom_call" | custom-call | flops 3623878656 | bytes 14548992 | tf_op jit(solution)/shard_map/pallas_call | solution.py:238
  63.0 2.7 %shard_map.68 = (f32[8,128,128]{2,1,0:T(8,128)S(1)}, f32[8,128,128]{2,1,0:T(8,128)S(1)}, f32[8,128,128]{2,1,0:T(8,128)S(1)}) custom-call(s32[8]{0:T(128)S(1)} %bitcast.27, bf16[8,128,640]{2,1,0:T(8,128)(2,1)S(1)} %copy-done.1, bf16[512,640]{1,0:T(8,128)(2,1)S(1)} %collective-permute-done.4.key_ref, bf16[8,512,128]{2,1,0:T(8,128)(2,1)S(1)} %copy-done.2, ...), custom_call_target="tpu_custom_call" | custom-call | flops 3623878656 | bytes 14548992 | tf_op jit(solution)/shard_map/pallas_call | solution.py:238
  65.7 3.6 %collective-permute-done.2.key_ref = bf16[512,640]{1,0:T(8,128)(2,1)S(1)} collective-permute-done((bf16[512,640]{1,0:T(8,128)(2,1)S(1)}, bf16[512,640]{1,0:T(8,128)(2,1)S(1)}, u32[]{:S(2)}, u32[]{:S(2)}) %collective-permute-start.2) | collective-permute-done | bytes 655392 | tf_op jit(solution)/shard_map/ppermute | solution.py:141
  69.3 2.8 %shard_map.69.own_ref = bf16[2,64,1152]{2,1,0:T(8,128)(2,1)S(1)} custom-call(s32[8]{0:T(128)S(1)} %bitcast.28, bf16[8,128,640]{2,1,0:T(8,128)(2,1)S(1)} %copy-done.1, bf16[512,640]{1,0:T(8,128)(2,1)S(1)} %collective-permute-done.2.key_ref, bf16[8,512,128]{2,1,0:T(8,128)(2,1)S(1)} %copy-done.2, f32[8,128,128]{2,1,0:T(8,128)S(1)} %get-tuple-element.22.refs_0_, ...), custom_call_target="tpu_custom_call" | custom-call | flops 1207959552 | bytes 4849664 | tf_op jit(solution)/shard_map/pallas_call | solution.py:238
  72.2 1.9 %collective-permute-start.5 = (bf16[2,64,1152]{2,1,0:T(8,128)(2,1)S(1)}, bf16[2,64,1152]{2,1,0:T(8,128)(2,1)S(1)}, u32[]{:S(2)}, u32[]{:S(2)}) collective-permute-start(bf16[2,64,1152]{2,1,0:T(8,128)(2,1)S(1)} %shard_map.69.own_ref), channel_id=1, source_target_pairs={{0,8},{8,0},{1,9},{9,1},{2,10},{10,2},{3,11},{11,3},{4,12},{12,4},... | collective-permute-start | bytes 884744 | tf_op jit(solution)/shard_map/ppermute | solution.py:145
  74.1 1.5 %collective-permute-done.5.other_ref = bf16[2,64,1152]{2,1,0:T(8,128)(2,1)S(1)} collective-permute-done((bf16[2,64,1152]{2,1,0:T(8,128)(2,1)S(1)}, bf16[2,64,1152]{2,1,0:T(8,128)(2,1)S(1)}, u32[]{:S(2)}, u32[]{:S(2)}) %collective-permute-start.5) | collective-permute-done | bytes 294944 | tf_op jit(solution)/shard_map/ppermute | solution.py:145
  76.2 1.9 %collective-permute-start.6 = (bf16[128,1024]{1,0:T(8,128)(2,1)S(1)}, bf16[128,1024]{1,0:T(8,128)(2,1)S(1)}, u32[]{:S(2)}, u32[]{:S(2)}) collective-permute-start(bf16[128,1024]{1,0:T(8,128)(2,1)S(1)} %shard_map.70), channel_id=1, source_target_pairs={{0,16},{16,0},{1,17},{17,1},{2,18},{18,2},{3,19},{19,3},{4,20},{20... | collective-permute-start | bytes 786440 | tf_op jit(solution)/shard_map/ppermute | solution.py:145
  78.2 8.2 %collective-permute-done.6 = bf16[128,1024]{1,0:T(8,128)(2,1)S(1)} collective-permute-done((bf16[128,1024]{1,0:T(8,128)(2,1)S(1)}, bf16[128,1024]{1,0:T(8,128)(2,1)S(1)}, u32[]{:S(2)}, u32[]{:S(2)}) %collective-permute-start.6) | collective-permute-done | bytes 262176 | tf_op jit(solution)/shard_map/ppermute | solution.py:145
  86.5 1.8 %shard_map.72 = bf16[4,2,2,2,64,128]{5,4,3,2,1,0:T(8,128)(2,1)S(1)} custom-call(s32[3]{0:T(128)S(1)} %pad_add_fusion.slots_ref, bf16[256,1024]{1,0:T(8,128)(2,1)S(1)} %pad_maximum_fusion.1.v_ref, bf16[8,128,1024]{2,1,0:T(8,128)(2,1)S(1)} %bitcast.16), custom_call_target="tpu_custom_call" | custom-call | flops 536870912 | bytes 2097152 | tf_op jit(solution)/shard_map/pallas_call | solution.py:307
  88.3 15.1 %all_to_all.15 = bf16[16,2,64,128]{3,2,1,0:T(8,128)(2,1)S(1)} all-to-all(bf16[16,2,64,128]{3,2,1,0:T(8,128)(2,1)S(1)} %bitcast.20), channel_id=1, replica_groups=mesh['y'=8,'zh_lat'=2,'zl_lat'=2,'core'=2,'z_hi'=2,'x'=4] {'x','zl_lat',..., dimensions={0} | all-to-all | bytes 1048576 | tf_op jit(solution)/shard_map/all_to_all | solution.py:423
  104.0 9.2 %collective-permute-start.8 = (bf16[64,512]{1,0:T(8,128)(2,1)S(1)}, bf16[64,512]{1,0:T(8,128)(2,1)S(1)}, u32[]{:S(2)}, u32[]{:S(2)}) collective-permute-start(bf16[64,512]{1,0:T(8,128)(2,1)S(1)} %get-tuple-element.26), channel_id=1, source_target_pairs={{0,4},{4,0},{1,5},{5,1},{2,6},{6,2},{3,7},{7,3},{8,12},{12,8},{9,1... | collective-permute-start | bytes 196616 | tf_op jit(solution)/shard_map/ppermute | solution.py:145
  113.3 2.5 %collective-permute-done.8.arrived_ref = bf16[64,512]{1,0:T(8,128)(2,1)S(1)} collective-permute-done((bf16[64,512]{1,0:T(8,128)(2,1)S(1)}, bf16[64,512]{1,0:T(8,128)(2,1)S(1)}, u32[]{:S(2)}, u32[]{:S(2)}) %collective-permute-start.8) | collective-permute-done | bytes 65568 | tf_op jit(solution)/shard_map/ppermute | solution.py:145
  (38 shorter events, 9.1 us)
Async XLA Ops:
  0.0 12.1 %copy-start.4 = (s32[64]{0:T(128)S(1)}, s32[64]{0:T(128)}, u32[]{:S(2)}) copy-start(s32[64]{0:T(128)} %param.8) | copy-start | bytes 772
  0.0 12.1 %copy-start.9 = (bf16[64,8,576]{2,1,0:T(8,128)(2,1)S(1)}, bf16[64,8,576]{2,1,0:T(8,128)(2,1)}, u32[]{:S(2)}) copy-start(bf16[64,8,576]{2,1,0:T(8,128)(2,1)} %param.6) | copy-start | bytes 1769476
  2.0 12.4 %copy-start.3 = (bf16[1024,64]{0,1:T(8,128)(2,1)S(1)}, bf16[1024,64]{0,1:T(8,128)(2,1)}, u32[]{:S(2)}) copy-start(bf16[1024,64]{0,1:T(8,128)(2,1)} %param.11) | copy-start | bytes 393220
  2.0 26.6 %all-to-all-start = ((bf16[8,64,640]{2,1,0:T(8,128)(2,1)}), bf16[8,64,640]{2,1,0:T(8,128)(2,1)}, u32[]{:S(2)}, u32[]{:S(2)}) async-start(bf16[8,64,640]{2,1,0:T(8,128)(2,1)} %shard_map.65), calls=%async_computation | async-start | bytes 1310720 | tf_op jit(solution)/shard_map/all_to_all | solution.py:398
  12.5 5.7 %collective-permute-start = (bf16[8,64,640]{2,1,0:T(8,128)(2,1)S(1)}, bf16[8,64,640]{2,1,0:T(8,128)(2,1)S(1)}, u32[]{:S(2)}, u32[]{:S(2)}) collective-permute-start(bf16[8,64,640]{2,1,0:T(8,128)(2,1)S(1)} %shard_map.64), channel_id=1, source_target_pairs={{0,8},{8,0},{1,9},{9,1},{2,10},{10,2},{3,11},{11,3},{4,12},{12,4},... | collective-permute-start | bytes 1966088 | tf_op jit(solution)/shard_map/ppermute | solution.py:145
  14.4 11.5 %collective-permute-start.7 = (bf16[64,1024]{1,0:T(8,128)(2,1)S(1)}, bf16[64,1024]{1,0:T(8,128)(2,1)S(1)}, u32[]{:S(2)}, u32[]{:S(2)}) collective-permute-start(bf16[64,1024]{1,0:T(8,128)(2,1)S(1)} %bitcast.21), channel_id=1, source_target_pairs={{0,32},{32,0},{1,33},{33,1},{2,34},{34,2},{3,35},{35,3},{4,36},{36... | collective-permute-start | bytes 393224 | tf_op jit(solution)/shard_map/ppermute | solution.py:145
  18.3 10.4 %copy-start = (bf16[8,128,640]{2,1,0:T(8,128)(2,1)}, bf16[8,128,640]{2,1,0:T(8,128)(2,1)S(1)}, u32[]{:S(2)}) copy-start(bf16[8,128,640]{2,1,0:T(8,128)(2,1)S(1)} %pad_maximum_fusion.q_ref) | copy-start | bytes 3932164
  27.3 12.5 %copy-start.10 = (s32[8]{0:T(128)S(1)}, s32[8]{0:T(128)}, u32[]{:S(2)}) copy-start(s32[8]{0:T(128)} %param.9) | copy-start | bytes 100
  28.7 57.8 %all-to-all-start.1 = ((bf16[8,2,64,1024]{3,2,1,0:T(8,128)(2,1)}), bf16[8,2,64,1024]{3,2,1,0:T(8,128)(2,1)S(1)}, u32[]{:S(2)}, u32[]{:S(2)}) async-start(bf16[8,2,64,1024]{3,2,1,0:T(8,128)(2,1)} %shard_map.71), calls=%async_computation.1 | async-start | bytes 4194304 | tf_op jit(solution)/shard_map/all_to_all | solution.py:405
  34.6 5.9 %collective-permute-start.3 = (bf16[512,640]{1,0:T(8,128)(2,1)}, bf16[512,640]{1,0:T(8,128)(2,1)S(1)}, u32[]{:S(2)}, u32[]{:S(2)}) collective-permute-start(bf16[512,640]{1,0:T(8,128)(2,1)} %bitcast.7.key_ref), channel_id=1, source_target_pairs={{0,8},{8,0},{1,9},{9,1},{2,10},{10,2},{3,11},{11,3},{4,12},{12,4},... | collective-permute-start | bytes 1966088 | tf_op jit(solution)/shard_map/ppermute | solution.py:145
  36.5 18.8 %collective-permute-start.1 = (bf16[512,640]{1,0:T(8,128)(2,1)}, bf16[512,640]{1,0:T(8,128)(2,1)S(1)}, u32[]{:S(2)}, u32[]{:S(2)}) collective-permute-start(bf16[512,640]{1,0:T(8,128)(2,1)} %bitcast.7.key_ref), channel_id=1, source_target_pairs={{0,16},{8,60},{16,32},{24,8},{32,48},{40,24},{48,4},{56,40},{4,20}... | collective-permute-start | bytes 1966088 | tf_op jit(solution)/shard_map/ppermute | solution.py:141
  40.5 22.5 %collective-permute-start.4 = (bf16[512,640]{1,0:T(8,128)(2,1)S(1)}, bf16[512,640]{1,0:T(8,128)(2,1)S(1)}, u32[]{:S(2)}, u32[]{:S(2)}) collective-permute-start(bf16[512,640]{1,0:T(8,128)(2,1)S(1)} %collective-permute-done.3), channel_id=1, source_target_pairs={{0,16},{8,60},{16,32},{24,8},{32,48},{40,24},{48,4},{56,40},{4,20}... | collective-permute-start | bytes 1966088 | tf_op jit(solution)/shard_map/ppermute | solution.py:141
  44.8 12.4 %copy-start.1 = (bf16[8,128,640]{2,1,0:T(8,128)(2,1)S(1)}, bf16[8,128,640]{2,1,0:T(8,128)(2,1)}, u32[]{:S(2)}) copy-start(bf16[8,128,640]{2,1,0:T(8,128)(2,1)} %copy-done) | copy-start | bytes 3932164
  44.8 12.4 %copy-start.2 = (bf16[8,512,128]{2,1,0:T(8,128)(2,1)S(1)}, bf16[8,512,128]{2,1,0:T(8,128)(2,1)}, u32[]{:S(2)}) copy-start(bf16[8,512,128]{2,1,0:T(8,128)(2,1)} %up_ref.7) | copy-start | bytes 3145732
  44.8 12.4 %copy-start.5 = (s32[8,1]{0,1:T(1,128)S(1)}, s32[8,1]{0,1:T(1,128)}, u32[]{:S(2)}) copy-start(s32[8,1]{0,1:T(1,128)} %reduce-window.9) | copy-start | bytes 100
  55.3 14.0 %collective-permute-start.2 = (bf16[512,640]{1,0:T(8,128)(2,1)S(1)}, bf16[512,640]{1,0:T(8,128)(2,1)S(1)}, u32[]{:S(2)}, u32[]{:S(2)}) collective-permute-start(bf16[512,640]{1,0:T(8,128)(2,1)S(1)} %collective-permute-done.1.key_ref), channel_id=1, source_target_pairs={{0,16},{8,60},{16,32},{24,8},{32,48},{40,24},{48,4},{56,40},{4,20}... | collective-permute-start | bytes 1966088 | tf_op jit(solution)/shard_map/ppermute | solution.py:141
  57.2 1.0 copy-start.6
  58.3 1.0 copy-start.7
  59.3 1.0 copy-start.8
  72.2 3.5 %collective-permute-start.5 = (bf16[2,64,1152]{2,1,0:T(8,128)(2,1)S(1)}, bf16[2,64,1152]{2,1,0:T(8,128)(2,1)S(1)}, u32[]{:S(2)}, u32[]{:S(2)}) collective-permute-start(bf16[2,64,1152]{2,1,0:T(8,128)(2,1)S(1)} %shard_map.69.own_ref), channel_id=1, source_target_pairs={{0,8},{8,0},{1,9},{9,1},{2,10},{10,2},{3,11},{11,3},{4,12},{12,4},... | collective-permute-start | bytes 884744 | tf_op jit(solution)/shard_map/ppermute | solution.py:145
  76.2 10.2 %collective-permute-start.6 = (bf16[128,1024]{1,0:T(8,128)(2,1)S(1)}, bf16[128,1024]{1,0:T(8,128)(2,1)S(1)}, u32[]{:S(2)}, u32[]{:S(2)}) collective-permute-start(bf16[128,1024]{1,0:T(8,128)(2,1)S(1)} %shard_map.70), channel_id=1, source_target_pairs={{0,16},{16,0},{1,17},{17,1},{2,18},{18,2},{3,19},{19,3},{4,20},{20... | collective-permute-start | bytes 786440 | tf_op jit(solution)/shard_map/ppermute | solution.py:145
  104.0 11.7 %collective-permute-start.8 = (bf16[64,512]{1,0:T(8,128)(2,1)S(1)}, bf16[64,512]{1,0:T(8,128)(2,1)S(1)}, u32[]{:S(2)}, u32[]{:S(2)}) collective-permute-start(bf16[64,512]{1,0:T(8,128)(2,1)S(1)} %get-tuple-element.26), channel_id=1, source_target_pairs={{0,4},{4,0},{1,5},{5,1},{2,6},{6,2},{3,7},{7,3},{8,12},{12,8},{9,1... | collective-permute-start | bytes 196616 | tf_op jit(solution)/shard_map/ppermute | solution.py:145
